TPU v7x, 128 devices: a whole 4x4x4 slice. The times are simulated.
128 devices in a mesh: gx: 16 (over y, z_lo, core), gy: 8 (over x, z_hi).
Axes of the slice: x: 4, y: 4, z: 4 (z_hi: 2, z_lo: 2; z = z_hi * 2 + z_lo), core: 2. Of those that a mesh axis runs over, the one named last changes fastest.
Arguments:
- fields: float32 [5, 24, 1024, 1024], P(None, None, 'gx', 'gy'), may hold values from -60 to 60
- embed_weight: bfloat16 [2560, 768], replicated, may hold values from -0.125 to 0.125
- qkv_weight: bfloat16 [768, 2304], replicated, may hold values from -0.21875 to 0.21875
- out_weight: bfloat16 [768, 768], replicated, may hold values from -0.21875 to 0.21875
- up_weight: bfloat16 [768, 3072], replicated, may hold values from -0.21875 to 0.21875
- down_weight: bfloat16 [3072, 768], replicated, may hold values from -0.109375 to 0.109375
Outputs:
- tokens_out: bfloat16 [2, 128, 128, 768], P(None, 'gy', 'gx')
All inputs are finite; a program needn't handle non-finite values.
Results may differ from a plain program's by a relative error of at most 0.029.
Values may be sent and summed in bfloat16 or wider, within the bound.
No kernel may reach another device: no remote copies, remote signals or barrier semaphores. Data moves between devices by JAX's collectives and lax.ppermute only.
A program may use at most 128 MiB of HBM per device.

v0:
```python
import jax
import jax.numpy as jnp
from jax import lax
from jax.sharding import PartitionSpec as P

R = 4
P_SIZE = 8
HEADS = 12


def padded(cells, sides, width):
    for axis, dim in sides:
        count = lax.axis_size(axis)
        head = lax.slice_in_dim(cells, 0, width, axis=dim)
        tail = lax.slice_in_dim(cells, cells.shape[dim] - width, cells.shape[dim], axis=dim)
        cells = jnp.concatenate(
            [
                lax.ppermute(tail, axis, [(i, (i + 1) % count) for i in range(count)]),
                cells,
                lax.ppermute(head, axis, [((i + 1) % count, i) for i in range(count)]),
            ],
            axis=dim,
        )
    return cells


def filter_taps():
    offsets = jnp.arange(-R, R + 1).astype(jnp.float32)
    values = jnp.exp(-offsets * offsets / 4.5)
    return values / jnp.sum(values)


def smooth_along(values, taps, axis, length):
    total = jnp.zeros(values.shape[:axis] + (length,) + values.shape[axis + 1 :], jnp.float32)
    for index in range(2 * R + 1):
        total = total + taps[index] * lax.slice_in_dim(values, index, index + length, axis=axis)
    return total


def layer_norm(hidden):
    center = hidden - jnp.mean(hidden, axis=-1, keepdims=True)
    spread = jnp.mean(center * center, axis=-1, keepdims=True)
    return (center * lax.rsqrt(spread + 1e-05)).astype(jnp.bfloat16)


def project_three(normed, qkv_weight):
    width = normed.shape[-1]
    both = jnp.dot(normed.reshape(-1, width), qkv_weight, preferred_element_type=jnp.float32)
    both = both.astype(jnp.bfloat16).reshape(normed.shape[:-1] + (3 * width,))
    return (both[..., :width], both[..., width : 2 * width], both[..., 2 * width :])


def attend_lines(query, keys, values, seq_dim):
    if seq_dim == 1:
        query = jnp.swapaxes(query, 1, 2)
        keys = jnp.swapaxes(keys, 1, 2)
        values = jnp.swapaxes(values, 1, 2)
    zdim, lines, length, width = query.shape
    shape_heads = (zdim, lines, length, HEADS, width // HEADS)
    query = query.reshape(shape_heads)
    keys = keys.reshape(shape_heads)
    values = values.reshape(shape_heads)
    scores = jnp.einsum("zlshe,zlthe->zlhst", query, keys, preferred_element_type=jnp.float32)
    scores = scores * (1.0 / (width // HEADS) ** 0.5)
    weights = jnp.exp(scores)
    weights = (weights / jnp.sum(weights, axis=-1, keepdims=True)).astype(jnp.bfloat16)
    mixed = jnp.einsum("zlhst,zlthe->zlshe", weights, values, preferred_element_type=jnp.float32)
    mixed = mixed.astype(jnp.bfloat16).reshape(zdim, lines, length, width)
    if seq_dim == 1:
        mixed = jnp.swapaxes(mixed, 1, 2)
    return mixed


def out_project(mixed, out_weight):
    width = mixed.shape[-1]
    branch = jnp.dot(mixed.reshape(-1, width), out_weight, preferred_element_type=jnp.float32)
    return branch.astype(jnp.bfloat16).reshape(mixed.shape)


def shards(fields, embed_weight, qkv_weight, out_weight, up_weight, down_weight):
    taps = filter_taps()
    span = fields.shape[1] - 2 * R
    cells_x = fields.shape[2]
    cells_y = fields.shape[3]
    wide = padded(fields, (("gx", 2), ("gy", 3)), R)
    along_x = smooth_along(wide, taps, 2, cells_x)
    along_y = smooth_along(along_x, taps, 3, cells_y)
    smooth = smooth_along(along_y, taps, 1, span)
    filtered = smooth.astype(jnp.bfloat16)
    nfield = fields.shape[0]
    zpatch = span // P_SIZE
    xpatch = cells_x // P_SIZE
    ypatch = cells_y // P_SIZE
    width = embed_weight.shape[1]
    split = filtered.reshape(nfield, zpatch, P_SIZE, xpatch, P_SIZE, ypatch, P_SIZE)
    patches = jnp.transpose(split, (1, 5, 3, 0, 2, 4, 6)).reshape(
        -1, nfield * P_SIZE * P_SIZE * P_SIZE
    )
    hidden = jnp.dot(patches, embed_weight, preferred_element_type=jnp.float32)
    hidden = hidden.reshape(zpatch, ypatch, xpatch, width)
    normed = layer_norm(hidden)
    query, keys, values = project_three(normed, qkv_weight)
    triple = (
        lax.all_to_all(query, "gx", split_axis=1, concat_axis=2, tiled=True),
        lax.all_to_all(keys, "gx", split_axis=1, concat_axis=2, tiled=True),
        lax.all_to_all(values, "gx", split_axis=1, concat_axis=2, tiled=True),
    )
    result = attend_lines(triple[0], triple[1], triple[2], 2)
    returned = lax.all_to_all(result, "gx", split_axis=2, concat_axis=1, tiled=True)
    branch = out_project(returned, out_weight)
    hidden = hidden + branch.astype(jnp.float32)
    normed = layer_norm(hidden)
    query, keys, values = project_three(normed, qkv_weight)
    triple = (
        lax.all_to_all(query, "gy", split_axis=2, concat_axis=1, tiled=True),
        lax.all_to_all(keys, "gy", split_axis=2, concat_axis=1, tiled=True),
        lax.all_to_all(values, "gy", split_axis=2, concat_axis=1, tiled=True),
    )
    result = attend_lines(triple[0], triple[1], triple[2], 1)
    returned = lax.all_to_all(result, "gy", split_axis=1, concat_axis=2, tiled=True)
    branch = out_project(returned, out_weight)
    hidden = hidden + branch.astype(jnp.float32)
    normed = layer_norm(hidden).reshape(-1, width)
    upper = jnp.dot(normed, up_weight, preferred_element_type=jnp.float32)
    upper = jax.nn.gelu(upper, approximate=True).astype(jnp.bfloat16)
    lower = jnp.dot(upper, down_weight, preferred_element_type=jnp.float32).reshape(hidden.shape)
    return (hidden + lower).astype(jnp.bfloat16)


def solution(mesh):
    return jax.shard_map(
        shards,
        mesh=mesh,
        in_specs=(P(None, None, "gx", "gy"), P(), P(), P(), P(), P()),
        out_specs=P(None, "gy", "gx", None),
        check_vma=False,
    )
```

profile of v0, /device:TPU:0, one launch (start us, length us, event | category | flops | bytes accessed | tf_op | source)
XLA Modules:
  0.0 377.6 jit_solution(335268985814991210)
XLA Ops:
  6.7 7.2 %copy.105 = f32[5,24,64,128]{2,1,3,0:T(8,128)} copy(f32[5,24,64,128]{3,2,1,0:T(8,128)} %param.6) | data formatting | bytes 7864320 | tf_op args[0]
  14.6 5.7 %copy.104 = f32[5,24,4,128]{2,1,3,0:T(8,128)} copy(f32[5,24,4,128]{3,1,2,0:T(8,128)} %collective-permute-done) | data formatting | bytes 491520 | tf_op jit(solution)/shard_map/ppermute | solution.py:18
  20.3 5.7 %copy.106 = f32[5,24,4,128]{2,1,3,0:T(8,128)} copy(f32[5,24,4,128]{3,1,2,0:T(8,128)} %collective-permute-done.1) | data formatting | bytes 491520 | tf_op jit(solution)/shard_map/ppermute | solution.py:20
  35.7 4.7 %collective-permute-done.2 = f32[5,24,72,4]{2,1,3,0:T(8,128)S(1)} collective-permute-done((f32[5,24,72,4]{2,1,3,0:T(8,128)S(1)}, f32[5,24,72,4]{2,1,3,0:T(8,128)S(1)}, u32[]{:S(2)}, u32[]{:S(2)}) %collective-permute-start.2) | collective-permute-done | bytes 138272 | tf_op jit(solution)/shard_map/ppermute | solution.py:18
  43.4 10.0 %pad_maximum_fusion = f32[5,24,72,136]{2,1,3,0:T(8,128)} fusion(f32[5,24,72,4]{2,1,3,0:T(8,128)S(1)} %collective-permute-done.3, f32[5,24,4,128]{2,1,3,0:T(8,128)S(1)} %copy-done.1, f32[5,24,64,128]{2,1,3,0:T(8,128)} %copy.105, f32[5,24,4,128]{2,1,3,0:T(8,128)} %copy.104, f32[5,24,72,4]{2,1,3,0:T(8,128)S(1)} %collective-permute-done.2), kind=kLoop, calls=%fused_computation.17 | loop fusion | flops 4700160 | bytes 9400320 | tf_op jit(solution)/shard_map/concatenate | solution.py:16
  53.4 39.8 %fusion = f32[5,24,64,136]{2,1,3,0:T(8,128)} fusion(f32[5,24,72,136]{2,1,3,0:T(8,128)} %pad_maximum_fusion, f32[]{:T(128)} %bitcast.8, f32[]{:T(128)} %bitcast.7, f32[]{:T(128)} %bitcast.6, f32[]{:T(128)} %bitcast.5, f32[]{:T(128)} %bitcast.4, f32[]{:T(128)} %bitcast.3, f32[]{:T(128)} %bitcast.2, f32[]{:T(128)} %bitcast.1, f32[]{:T(128)} %bitcast), kind=kLoop, calls=%fused_computation.1 | loop fusion | flops 17756160 | bytes 41779236 | tf_op jit(solution)/shard_map/add | solution.py:36
  93.2 32.9 %fusion.8 = f32[5,24,64,128]{2,1,3,0:T(8,128)} fusion(f32[5,24,64,136]{2,1,3,0:T(8,128)} %fusion, f32[]{:T(128)} %bitcast.8, f32[]{:T(128)} %bitcast.7, f32[]{:T(128)} %bitcast.6, f32[]{:T(128)} %bitcast.5, f32[]{:T(128)} %bitcast.4, f32[]{:T(128)} %bitcast.3, f32[]{:T(128)} %bitcast.2, f32[]{:T(128)} %bitcast.1, f32[]{:T(128)} %bitcast), kind=kLoop, calls=%fused_computation.19 | loop fusion | flops 16711680 | bytes 39321636 | tf_op jit(solution)/shard_map/add | solution.py:36
  126.1 29.7 %fusion.17 = bf16[5,16,64,128]{2,1,3,0:T(8,128)(2,1)} fusion(f32[5,24,64,128]{2,1,3,0:T(8,128)} %fusion.8, f32[]{:T(128)} %bitcast.8, f32[]{:T(128)} %bitcast.7, f32[]{:T(128)} %bitcast.6, f32[]{:T(128)} %bitcast.5, f32[]{:T(128)} %bitcast.4, f32[]{:T(128)} %bitcast.3, f32[]{:T(128)} %bitcast.2, f32[]{:T(128)} %bitcast.1, f32[]{:T(128)} %bitcast), kind=kLoop, calls=%fused_computation.37 | loop fusion | flops 11796480 | bytes 24903716 | tf_op jit(solution)/shard_map/convert_element_type | solution.py:89
  155.8 4.7 %copy.107 = bf16[5,16,64,128]{3,2,1,0:T(8,128)(2,1)} copy(bf16[5,16,64,128]{2,1,3,0:T(8,128)(2,1)} %fusion.17) | data formatting | bytes 2621440 | tf_op jit(solution)/shard_map/convert_element_type | solution.py:89
  160.5 27.4 %reshape.151 = bf16[5,2,8,8,8,16,8]{6,5,4,3,2,1,0:T(8,128)(2,1)} reshape(bf16[5,16,64,128]{3,2,1,0:T(8,128)(2,1)} %copy.107) | data formatting | bytes 2621440 | tf_op jit(solution)/shard_map/reshape | solution.py:95
  187.9 19.7 %copy.108 = bf16[2,16,8,5,8,8,8]{1,6,5,4,3,2,0:T(8,128)(2,1)} copy(bf16[2,16,8,5,8,8,8]{6,1,5,2,4,0,3:T(8,128)(2,1)} %bitcast.96) | data formatting | bytes 2621440 | tf_op jit(solution)/shard_map/transpose | solution.py:96
  207.5 7.0 %fusion.65 = (f32[2,16,8]{1,2,0:T(8,128)S(1)}, f32[2,16,8,768]{3,1,2,0:T(8,128)S(1)}) fusion(bf16[2,16,8,2560]{1,3,2,0:T(8,128)(2,1)} %bitcast.97, bf16[2560,768]{1,0:T(8,128)(2,1)} %param.7), kind=kOutput, calls=%fused_computation.123 | convolution fusion | flops 1006829312 | bytes 6030336 | tf_op jit(solution)/shard_map/dot_general | solution.py:99
  218.0 4.6 %all-to-all-start.1 = ((bf16[2,16,8,768]{3,2,0,1:T(8,128)(2,1)}), bf16[2,16,8,768]{3,2,0,1:T(8,128)(2,1)}, u32[]{:S(2)}, u32[]{:S(2)}) async-start(bf16[2,16,8,768]{3,2,0,1:T(8,128)(2,1)} %copy.149), calls=%async_computation.1 | async-start | bytes 786432 | tf_op jit(solution)/shard_map/all_to_all | solution.py:104
  224.4 7.5 %all-to-all-done.1 = bf16[2,16,8,768]{3,2,0,1:T(8,128)(2,1)} async-done(((bf16[2,16,8,768]{3,2,0,1:T(8,128)(2,1)}), bf16[2,16,8,768]{3,2,0,1:T(8,128)(2,1)}, u32[]{:S(2)}, u32[]{:S(2)}) %all-to-all-start.1) | async-done | bytes 393248 | tf_op jit(solution)/shard_map/all_to_all | solution.py:104
  231.9 4.2 %all-to-all-start.2 = ((bf16[2,16,8,768]{3,2,0,1:T(8,128)(2,1)}), bf16[2,16,8,768]{3,2,0,1:T(8,128)(2,1)}, u32[]{:S(2)}, u32[]{:S(2)}) async-start(bf16[2,16,8,768]{3,2,0,1:T(8,128)(2,1)} %copy.150), calls=%async_computation.2 | async-start | bytes 786432 | tf_op jit(solution)/shard_map/all_to_all | solution.py:105
  237.8 7.5 %all-to-all-done.2 = bf16[2,16,8,768]{3,2,0,1:T(8,128)(2,1)} async-done(((bf16[2,16,8,768]{3,2,0,1:T(8,128)(2,1)}), bf16[2,16,8,768]{3,2,0,1:T(8,128)(2,1)}, u32[]{:S(2)}, u32[]{:S(2)}) %all-to-all-start.2) | async-done | bytes 393248 | tf_op jit(solution)/shard_map/all_to_all | solution.py:105
  245.3 4.2 %all-to-all-start = ((bf16[2,16,8,768]{3,2,0,1:T(8,128)(2,1)}), bf16[2,16,8,768]{3,2,0,1:T(8,128)(2,1)}, u32[]{:S(2)}, u32[]{:S(2)}) async-start(bf16[2,16,8,768]{3,2,0,1:T(8,128)(2,1)} %copy.148), calls=%async_computation | async-start | bytes 786432 | tf_op jit(solution)/shard_map/all_to_all | solution.py:106
  271.7 13.9 %all_to_all.96 = bf16[2,1,128,768]{3,0,1,2:T(2,128)(2,1)S(1)} all-to-all(bf16[2,1,128,768]{3,0,1,2:T(2,128)(2,1)} %copy.121), channel_id=1, replica_groups=mesh['gx'=16,'gy'=8] {'gx'}, dimensions={2} | all-to-all | bytes 786432 | tf_op jit(solution)/shard_map/all_to_all | solution.py:109
  293.0 5.4 %all-to-all-start.5 = ((bf16[2,16,8,768]{3,1,0,2:T(8,128)(2,1)}), bf16[2,16,8,768]{3,1,0,2:T(8,128)(2,1)}, u32[]{:S(2)}, u32[]{:S(2)}) async-start(bf16[2,16,8,768]{3,1,0,2:T(8,128)(2,1)} %copy.152), calls=%async_computation.5 | async-start | bytes 786432 | tf_op jit(solution)/shard_map/all_to_all | solution.py:115
  300.2 7.9 %all-to-all-done.5 = bf16[2,16,8,768]{3,1,0,2:T(8,128)(2,1)} async-done(((bf16[2,16,8,768]{3,1,0,2:T(8,128)(2,1)}), bf16[2,16,8,768]{3,1,0,2:T(8,128)(2,1)}, u32[]{:S(2)}, u32[]{:S(2)}) %all-to-all-start.5) | async-done | bytes 393248 | tf_op jit(solution)/shard_map/all_to_all | solution.py:115
  314.0 7.2 %all-to-all-done.6 = bf16[2,16,8,768]{3,1,0,2:T(8,128)(2,1)} async-done(((bf16[2,16,8,768]{3,1,0,2:T(8,128)(2,1)}), bf16[2,16,8,768]{3,1,0,2:T(8,128)(2,1)}, u32[]{:S(2)}, u32[]{:S(2)}) %all-to-all-start.6) | async-done | bytes 393248 | tf_op jit(solution)/shard_map/all_to_all | solution.py:116
  321.2 4.1 %all-to-all-start.4 = ((bf16[2,16,8,768]{3,1,0,2:T(8,128)(2,1)}), bf16[2,16,8,768]{3,1,0,2:T(8,128)(2,1)}, u32[]{:S(2)}, u32[]{:S(2)}) async-start(bf16[2,16,8,768]{3,1,0,2:T(8,128)(2,1)} %copy.151), calls=%async_computation.4 | async-start | bytes 786432 | tf_op jit(solution)/shard_map/all_to_all | solution.py:117
  347.2 16.0 %all_to_all.97 = bf16[2,128,1,768]{3,0,2,1:T(2,128)(2,1)S(1)} all-to-all(bf16[2,128,1,768]{3,0,2,1:T(2,128)(2,1)} %copy.135), channel_id=1, replica_groups=mesh['gx'=16,'gy'=8] {'gy'}, dimensions={1} | all-to-all | bytes 786432 | tf_op jit(solution)/shard_map/all_to_all | solution.py:120
  367.4 7.8 %fusion.35 = f32[256,768]{1,0:T(8,128)} fusion(bf16[3072,768]{1,0:T(8,128)(2,1)} %param.11, bf16[256,768]{1,0:T(8,128)(2,1)} %bitcast.108, bf16[768,3072]{1,0:T(8,128)(2,1)} %param.10), kind=kOutput, calls=%fused_computation.66 | convolution fusion | flops 2422996992 | bytes 10616832 | tf_op jit(solution)/shard_map/dot_general | solution.py:126
  (81 shorter events, 92.8 us)
Async XLA Ops:
  0.0 215.1 %copy-start = (bf16[768,2304]{1,0:T(8,128)(2,1)S(1)}, bf16[768,2304]{1,0:T(8,128)(2,1)}, u32[]{:S(2)}) copy-start(bf16[768,2304]{1,0:T(8,128)(2,1)} %param.8) | copy-start | bytes 10616836
  2.1 12.5 %collective-permute-start = (f32[5,24,4,128]{3,1,2,0:T(8,128)}, f32[5,24,4,128]{3,1,2,0:T(8,128)}, u32[]{:S(2)}, u32[]{:S(2)}) collective-permute-start(f32[5,24,4,128]{3,1,2,0:T(8,128)} %copy.146), channel_id=1, source_target_pairs={{0,8},{8,16},{16,24},{24,32},{32,40},{40,48},{48,56},{56,64},{64,7... | collective-permute-start | bytes 737288 | tf_op jit(solution)/shard_map/ppermute | solution.py:18
  2.8 17.5 %collective-permute-start.1 = (f32[5,24,4,128]{3,1,2,0:T(8,128)}, f32[5,24,4,128]{3,1,2,0:T(8,128)}, u32[]{:S(2)}, u32[]{:S(2)}) collective-permute-start(f32[5,24,4,128]{3,1,2,0:T(8,128)} %copy.147), channel_id=1, source_target_pairs={{8,0},{16,8},{24,16},{32,24},{40,32},{48,40},{56,48},{64,56},{72,6... | collective-permute-start | bytes 737288 | tf_op jit(solution)/shard_map/ppermute | solution.py:20
  26.0 17.4 %copy-start.1 = (f32[5,24,4,128]{2,1,3,0:T(8,128)S(1)}, f32[5,24,4,128]{2,1,3,0:T(8,128)}, u32[]{:S(2)}) copy-start(f32[5,24,4,128]{2,1,3,0:T(8,128)} %copy.106) | copy-start | bytes 737284
  27.9 12.5 %collective-permute-start.2 = (f32[5,24,72,4]{2,1,3,0:T(8,128)S(1)}, f32[5,24,72,4]{2,1,3,0:T(8,128)S(1)}, u32[]{:S(2)}, u32[]{:S(2)}) collective-permute-start(f32[5,24,72,4]{2,1,3,0:T(8,128)S(1)} %get-tuple-element.9), channel_id=1, source_target_pairs={{0,1},{1,2},{2,3},{3,4},{4,5},{5,6},{6,7},{7,0},{8,9},{9,10},{10,1... | collective-permute-start | bytes 414728 | tf_op jit(solution)/shard_map/ppermute | solution.py:18
  31.9 11.5 %collective-permute-start.3 = (f32[5,24,72,4]{2,1,3,0:T(8,128)S(1)}, f32[5,24,72,4]{2,1,3,0:T(8,128)S(1)}, u32[]{:S(2)}, u32[]{:S(2)}) collective-permute-start(f32[5,24,72,4]{2,1,3,0:T(8,128)S(1)} %get-tuple-element.10), channel_id=1, source_target_pairs={{1,0},{2,1},{3,2},{4,3},{5,4},{6,5},{7,6},{0,7},{9,8},{10,9},{11,1... | collective-permute-start | bytes 414728 | tf_op jit(solution)/shard_map/ppermute | solution.py:20
  214.5 2.6 copy-start.2
  218.0 13.9 %all-to-all-start.1 = ((bf16[2,16,8,768]{3,2,0,1:T(8,128)(2,1)}), bf16[2,16,8,768]{3,2,0,1:T(8,128)(2,1)}, u32[]{:S(2)}, u32[]{:S(2)}) async-start(bf16[2,16,8,768]{3,2,0,1:T(8,128)(2,1)} %copy.149), calls=%async_computation.1 | async-start | bytes 786432 | tf_op jit(solution)/shard_map/all_to_all | solution.py:104
  231.9 13.5 %all-to-all-start.2 = ((bf16[2,16,8,768]{3,2,0,1:T(8,128)(2,1)}), bf16[2,16,8,768]{3,2,0,1:T(8,128)(2,1)}, u32[]{:S(2)}, u32[]{:S(2)}) async-start(bf16[2,16,8,768]{3,2,0,1:T(8,128)(2,1)} %copy.150), calls=%async_computation.2 | async-start | bytes 786432 | tf_op jit(solution)/shard_map/all_to_all | solution.py:105
  245.3 13.5 %all-to-all-start = ((bf16[2,16,8,768]{3,2,0,1:T(8,128)(2,1)}), bf16[2,16,8,768]{3,2,0,1:T(8,128)(2,1)}, u32[]{:S(2)}, u32[]{:S(2)}) async-start(bf16[2,16,8,768]{3,2,0,1:T(8,128)(2,1)} %copy.148), calls=%async_computation | async-start | bytes 786432 | tf_op jit(solution)/shard_map/all_to_all | solution.py:106
  289.0 0.9 copy-start.3
  293.0 15.1 %all-to-all-start.5 = ((bf16[2,16,8,768]{3,1,0,2:T(8,128)(2,1)}), bf16[2,16,8,768]{3,1,0,2:T(8,128)(2,1)}, u32[]{:S(2)}, u32[]{:S(2)}) async-start(bf16[2,16,8,768]{3,1,0,2:T(8,128)(2,1)} %copy.152), calls=%async_computation.5 | async-start | bytes 786432 | tf_op jit(solution)/shard_map/all_to_all | solution.py:115
  308.1 13.1 %all-to-all-start.6 = ((bf16[2,16,8,768]{3,1,0,2:T(8,128)(2,1)}), bf16[2,16,8,768]{3,1,0,2:T(8,128)(2,1)}, u32[]{:S(2)}, u32[]{:S(2)}) async-start(bf16[2,16,8,768]{3,1,0,2:T(8,128)(2,1)} %copy.153), calls=%async_computation.6 | async-start | bytes 786432 | tf_op jit(solution)/shard_map/all_to_all | solution.py:116
  321.2 13.1 %all-to-all-start.4 = ((bf16[2,16,8,768]{3,1,0,2:T(8,128)(2,1)}), bf16[2,16,8,768]{3,1,0,2:T(8,128)(2,1)}, u32[]{:S(2)}, u32[]{:S(2)}) async-start(bf16[2,16,8,768]{3,1,0,2:T(8,128)(2,1)} %copy.151), calls=%async_computation.4 | async-start | bytes 786432 | tf_op jit(solution)/shard_map/all_to_all | solution.py:117
  347.2 17.9 %copy-start.4 = (f32[2,16,8,768]{3,1,2,0:T(8,128)S(1)}, f32[2,16,8,768]{3,1,2,0:T(8,128)}, u32[]{:S(2)}) copy-start(f32[2,16,8,768]{3,1,2,0:T(8,128)} %copy-done.3) | copy-start | bytes 2359300
  365.5 0.9 copy-start.5
where the time goes:
time: 380 us; the launch traced here: 378 us
  other arithmetic  120 us (32%)
  local copies, waits for them, and re-layouts  117 us (31%)
  waiting for transfers between devices  39.1 us (10%)
  starting transfers between devices  36.9 us (10%)
  matrix products  34.1 us (9%)
  blocking collectives  29.9 us (8%)
    add x2, other arithmetic, smooth_along(): total + taps[index] * lax.slice_in_dim(values, index, index + length, axi...  72.7 us
    convert_element_type x1, other arithmetic, shards(): filtered = smooth.astype(jnp.bfloat16)  29.7 us
    reshape x1, local copies, waits for them, and re-layouts, shards(): filtered.reshape(nfield, zpatch, P_SIZE, xpatch, P_SIZE, ypatch, P_SIZE)  27.4 us
    transpose x1, local copies, waits for them, and re-layouts, shards(): jnp.transpose(split, (1, 5, 3, 0, 2, 4, 6))  19.7 us
    unnamed x21, local copies, waits for them, and re-layouts  18.7 us
    all_to_all x1, blocking collectives, shards(): lax.all_to_all(result, 'gy', split_axis=1, concat_axis=2, tiled=True)  16 us
    another operation x6, local copies, waits for them, and re-layouts  14.6 us
    all_to_all x1, blocking collectives, shards(): lax.all_to_all(result, 'gx', split_axis=2, concat_axis=1, tiled=True)  13.9 us
  transfers between devices with their start and end apart: 10, of which 8 were waited for; matrix products, arithmetic and copies ran while one was open for 10% of the time, Pallas kernels for 0%

commit v1 on v0

v1 whole, which is shorter than its diff:
```python
import functools

import jax
import jax.numpy as jnp
import ml_dtypes
import numpy as np
from jax import lax
from jax.experimental import pallas as pl
from jax.experimental.pallas import tpu as pltpu
from jax.sharding import PartitionSpec as P

R = 4
NF = 5
ZS = 16
CX = 64
CY = 128
D = 768
FF = 3072
KIN = 2560
PAIRS = 6
NXL = 16
TOK = 256
EXT = 10
SLOTS = 32
BOUND = (0, 1, 8, 9)
HI_ROWS = EXT * 32
ALL_ROWS = HI_ROWS + 128
PADX = 16
bf16 = jnp.bfloat16
f32 = jnp.float32


def np_taps():
    offsets = np.arange(-R, R + 1).astype(np.float32)
    values = np.exp(-offsets * offsets / np.float32(4.5)).astype(np.float32)
    return (values / values.sum(dtype=np.float32)).astype(np.float32)


TAPS = np_taps()


def as_bf16(values):
    return np.asarray(values, np.float32).astype(ml_dtypes.bfloat16)


def split_np(values):
    high = as_bf16(values)
    low = as_bf16(values - high.astype(np.float32))
    return high, low


def band_tables():
    wide = np.zeros((CY + 2 * R, CY), np.float32)
    for out in range(CY):
        column = (out % 8) * 16 + out // 8
        for k in range(2 * R + 1):
            wide[out + k, column] = TAPS[k]
    main_hi, main_lo = split_np(wide[R : R + CY])
    zero = np.zeros_like(main_hi)
    main = np.concatenate(
        [np.concatenate([main_hi, main_lo], 1), np.concatenate([main_hi, zero], 1)], 0
    )
    side_hi, side_lo = split_np(np.concatenate([wide[:R], wide[R + CY :]], 0))
    side = np.concatenate([side_hi, side_hi, side_lo, np.zeros_like(side_hi)], 0)
    return main, side


def permutation(rows, columns, source):
    table = np.zeros((rows, columns), np.float32)
    for row in range(rows):
        for column in source(row):
            table[row, column] = 1.0
    return as_bf16(table)


def weight_order():
    return permutation(256, 256, lambda r: [(r % 32) * 8 + r // 32])


def message_order():
    return permutation(
        16 * SLOTS,
        ALL_ROWS,
        lambda r: [(r % SLOTS) * 16 + r // SLOTS] if r % SLOTS < ALL_ROWS // 16 else [],
    )


def gather_sum():
    low = {ext: 2 * EXT + 2 * n for n, ext in enumerate(BOUND)}

    def source(row):
        a, i, c = row // 128, row // 8 % 16, row % 8
        found = [i * SLOTS + (c + 1) * 2 + a]
        if c == 0:
            left = (i - 1) % NXL * SLOTS
            found += [i * SLOTS + low[1] + a, left + 18 + a, left + low[9] + a]
        if c == 7:
            right = (i + 1) % NXL * SLOTS
            found += [i * SLOTS + low[8] + a, right + a, right + low[0] + a]
        return found

    return permutation(TOK, NXL * SLOTS, source)


def interleave():
    return permutation(TOK, TOK, lambda r: [(r % 2) * 128 + r // 2])


def separate():
    return permutation(TOK, TOK, lambda r: [(r % 128) * 2 + r // 128])


def to_owners():
    return permutation(TOK, TOK, lambda r: [(r // 16 % 2) * 128 + (r % 16) * 8 + r // 32])


def to_home():
    return permutation(TOK, TOK, lambda r: [(r % 8) * 32 + r // 8])


def dot(left, right):
    return lax.dot_general(left, right, (((1,), (0,)), ((), ())), preferred_element_type=f32)


def dot_t(left, right):
    return lax.dot_general(left, right, (((1,), (1,)), ((), ())), preferred_element_type=f32)


def halves(values):
    high = values.astype(bf16)
    return high, (values - high.astype(f32)).astype(bf16)


def prep_kernel(fields_ref, smooth_ref, upper_ref, lower_ref):
    for tile in range(CX // 8):
        rows = slice(tile * 8, tile * 8 + 8)
        plane = [fields_ref[0, z, rows, :] for z in range(ZS + 2 * R)]
        for z in range(ZS):
            total = float(TAPS[R]) * plane[z + R]
            for k in range(1, R + 1):
                total = total + float(TAPS[R + k]) * (plane[z + R - k] + plane[z + R + k])
            smooth_ref[0, z, rows, :] = total
    for pair in range(ZS // 2):
        turned = smooth_ref[0, 2 * pair : 2 * pair + 2].reshape(128, 128).T
        lower_ref[0, :, pair * 128 : pair * 128 + 128] = turned[:R]
        upper_ref[0, :, pair * 128 : pair * 128 + 128] = turned[CY - R :]


def band_kernel(smooth_ref, band_ref, along_ref):
    band = band_ref[...]

    def step(index, carry):
        f, part = index // 4, index % 4
        values = smooth_ref[f, pl.ds(part * 4, 4)].reshape(256, CY)
        high, low = halves(values)
        both = dot(jnp.concatenate([high, low], 1), band)
        along_ref[f, pl.ds(part * 4, 4)] = (both[:, :CY] + both[:, CY:]).reshape(4, CX, CY)
        return carry

    lax.fori_loop(0, NF * 4, step, 0)


def weight_kernel(weight_ref, order_ref, out_ref):
    order = order_ref[...]
    for tile in range(KIN // 256):
        turned = dot(order, weight_ref[tile * 256 : tile * 256 + 256, :]).astype(bf16)
        for y in range(8):
            if tile < 8:
                pair, inner = tile // 4, tile % 4
                start = pair * 1024 + y * 128 + inner * 32
            else:
                start = 2048 + y * 64 + (tile - 8) * 32
            out_ref[start : start + 32, :] = turned[y * 32 : y * 32 + 32]


def embed_kernel(
    along_ref, upper_ref, lower_ref, side_ref, weight_ref, order_ref, out_ref, wide, smooth, lhs, mid
):
    side = side_ref[...]
    zero = jnp.zeros((ZS, PADX, CY), f32)
    for f in range(NF):
        wide[f, :, 0:PADX] = zero
        wide[f, :, PADX + CX :] = zero
        cells = jnp.concatenate([upper_ref[f], lower_ref[f]], 0)
        high = cells.astype(bf16).astype(f32)
        stacked = jnp.concatenate([high, cells - high, high, jnp.zeros_like(high)], 0)
        added = dot(stacked.T.astype(bf16), side)
        wide[f, :, PADX : PADX + CX] = along_ref[f] + added.reshape(ZS, CX, CY)

    def step(index, carry):
        f, z = index // ZS, index % ZS
        total = float(TAPS[R]) * wide[f, z, pl.ds(PADX - 8, 80), :]
        for k in range(1, R + 1):
            total = total + float(TAPS[R + k]) * (
                wide[f, z, pl.ds(PADX - 8 - k, 80), :] + wide[f, z, pl.ds(PADX - 8 + k, 80), :]
            )
        smooth[f, z] = total
        return carry

    lax.fori_loop(0, NF * ZS, step, 0)

    lane = lax.broadcasted_iota(jnp.int32, (16, 128), 1)
    first = lane < 64

    def put(ext, a, start, values):
        high, low = halves(values)
        row = (ext * 2 + a) * 16
        lhs[row : row + 16, start : start + 128] = high
        if ext in BOUND:
            row = HI_ROWS + (BOUND.index(ext) * 2 + a) * 16
            lhs[row : row + 16, start : start + 128] = low

    for ext in range(EXT):
        rows = slice(ext * 8, ext * 8 + 8)
        for a in range(2):
            for pair in range(2):
                block = smooth[2 * pair : 2 * pair + 2, a * 8 : a * 8 + 8, rows, :]
                turned = block.reshape(128, 128).T
                for y in range(8):
                    put(ext, a, pair * 1024 + y * 128, turned[y * 16 : y * 16 + 16])
        turned = smooth[4, :, rows, :].reshape(128, 128).T
        for m in range(4):
            even = turned[m * 32 : m * 32 + 16]
            odd = turned[m * 32 + 16 : m * 32 + 32]
            start = 2048 + m * 128
            put(ext, 0, start, jnp.where(first, even, pltpu.roll(odd, 64, 1)))
            put(ext, 1, start, jnp.where(first, pltpu.roll(even, 64, 1), odd))

    for tile in range(3):
        columns = slice(tile * 256, tile * 256 + 256)
        both = dot(lhs[...], weight_ref[:, columns])
        lead = both[:64] + both[HI_ROWS : HI_ROWS + 64]
        tail = both[256:HI_ROWS] + both[HI_ROWS + 64 :]
        lead_hi, lead_lo = halves(lead)
        tail_hi, tail_lo = halves(tail)
        mid[0:64] = lead_hi
        mid[64:256] = both[64:256].astype(bf16)
        mid[256:HI_ROWS] = tail_hi
        mid[HI_ROWS : HI_ROWS + 64] = lead_lo
        mid[HI_ROWS + 64 :] = tail_lo
        out_ref[:, columns] = dot(order_ref[...], mid[...]).astype(bf16)


def layer_norm(hidden):
    center = hidden - jnp.mean(hidden, axis=-1, keepdims=True)
    spread = jnp.mean(center * center, axis=-1, keepdims=True)
    return (center * lax.rsqrt(spread + 1e-05)).astype(bf16)


def attend(hidden, qkv_ref, out_ref, three, mixed):
    normed = layer_norm(hidden[...])
    for tile in range(9):
        columns = slice(tile * 256, tile * 256 + 256)
        three[:, columns] = dot(normed, qkv_ref[:, columns]).astype(bf16)
    first = lax.broadcasted_iota(jnp.int32, (128, 128), 1) < 64
    none = jnp.zeros((128, 128), bf16)
    for a in range(2):
        rows = slice(a * 128, a * 128 + 128)
        for pair in range(PAIRS):
            start = pair * 128
            query = three[rows, start : start + 128]
            keys = three[rows, D + start : D + start + 128]
            values = three[rows, 2 * D + start : 2 * D + start + 128]
            keys = jnp.concatenate([jnp.where(first, keys, none), jnp.where(first, none, keys)], 0)
            values = jnp.concatenate(
                [jnp.where(first, values, none), jnp.where(first, none, values)], 0
            )
            weights = jnp.exp(dot_t(query, keys) * 0.125)
            left, right = weights[:, :128], weights[:, 128:]
            left = left * (1.0 / jnp.sum(left, axis=-1, keepdims=True))
            right = right * (1.0 / jnp.sum(right, axis=-1, keepdims=True))
            weights = jnp.concatenate([left.astype(bf16), right.astype(bf16)], 1)
            mixed[rows, start : start + 128] = dot(weights, values).astype(bf16)
    for tile in range(3):
        columns = slice(tile * 256, tile * 256 + 256)
        branch = dot(mixed[...], out_ref[:, columns]).astype(bf16)
        hidden[:, columns] = hidden[:, columns] + branch.astype(f32)


def x_kernel(slots_ref, sum_ref, qkv_ref, outw_ref, order_ref, out_ref, hidden, three, mixed):
    hidden[...] = dot(sum_ref[...], slots_ref[...])
    attend(hidden, qkv_ref, outw_ref, three, mixed)
    out_ref[...] = dot(order_ref[...], hidden[...].astype(bf16)).astype(bf16)


def y_kernel(
    tokens_ref,
    split_ref,
    qkv_ref,
    outw_ref,
    up_ref,
    down_ref,
    order_ref,
    out_ref,
    hidden,
    three,
    mixed,
    upper,
):
    hidden[...] = dot(split_ref[...], tokens_ref[...])
    attend(hidden, qkv_ref, outw_ref, three, mixed)
    normed = layer_norm(hidden[...])
    for tile in range(FF // 256):
        columns = slice(tile * 256, tile * 256 + 256)
        upper[:, columns] = jax.nn.gelu(dot(normed, up_ref[:, columns]), approximate=True).astype(bf16)
    for tile in range(3):
        columns = slice(tile * 256, tile * 256 + 256)
        total = hidden[:, columns] + dot(upper[...], down_ref[:, columns])
        out_ref[:, columns] = dot(order_ref[...], total.astype(bf16)).astype(bf16)


def home_kernel(tokens_ref, order_ref, out_ref):
    out_ref[...] = dot(order_ref[...], tokens_ref[...]).astype(bf16)


def whole(kernel, out_shape, scratch, flops, limit):
    space = pl.BlockSpec(memory_space=pltpu.VMEM)

    def call(*operands):
        size = sum(x.size * x.dtype.itemsize for x in operands)
        return pl.pallas_call(
            kernel,
            out_shape=out_shape,
            in_specs=[space] * len(operands),
            out_specs=space,
            scratch_shapes=scratch,
            compiler_params=pltpu.CompilerParams(vmem_limit_bytes=limit << 20),
            cost_estimate=pl.CostEstimate(flops=flops, bytes_accessed=size, transcendentals=0),
        )(*operands)

    return call


def like(shape, kind=bf16):
    return jax.ShapeDtypeStruct(shape, kind)


def prepare(fields):
    plane = (1, ZS + 2 * R, CX, CY)
    strip = pl.BlockSpec((1, R, ZS * CX), lambda f: (f, 0, 0))
    return pl.pallas_call(
        prep_kernel,
        grid=(NF,),
        in_specs=[pl.BlockSpec(plane, lambda f: (f, 0, 0, 0))],
        out_specs=[pl.BlockSpec((1, ZS, CX, CY), lambda f: (f, 0, 0, 0)), strip, strip],
        out_shape=[
            like((NF, ZS, CX, CY), f32),
            like((NF, R, ZS * CX), f32),
            like((NF, R, ZS * CX), f32),
        ],
        compiler_params=pltpu.CompilerParams(vmem_limit_bytes=16 << 20),
    )(fields)


def shards(fields, embed_weight, qkv_weight, out_weight, up_weight, down_weight):
    band, side = band_tables()
    count = lax.axis_size("gy")
    smooth, upper, lower = prepare(fields)
    upper = lax.ppermute(upper, "gy", [(i, (i + 1) % count) for i in range(count)])
    lower = lax.ppermute(lower, "gy", [((i + 1) % count, i) for i in range(count)])
    along = whole(band_kernel, like((NF, ZS, CX, CY), f32), [], 2 * 5120 * 256 * 256, 16)(
        smooth, band
    )
    weight = whole(weight_kernel, like((KIN, D)), [], 2 * KIN * 256 * D, 24)(
        embed_weight, weight_order()
    )
    slots = whole(
        embed_kernel,
        like((16 * SLOTS, D)),
        [
            pltpu.VMEM((NF, ZS, CX + 2 * PADX, CY), f32),
            pltpu.VMEM((NF, ZS, 80, CY), f32),
            pltpu.VMEM((ALL_ROWS, KIN), bf16),
            pltpu.VMEM((ALL_ROWS, 256), bf16),
        ],
        2 * ALL_ROWS * KIN * D,
        40,
    )(along, upper, lower, side, weight, message_order())
    slots = lax.all_to_all(
        slots.reshape(NXL, SLOTS, D), "gx", split_axis=0, concat_axis=0, tiled=True
    ).reshape(NXL * SLOTS, D)
    attention = [
        pltpu.VMEM((TOK, D), f32),
        pltpu.VMEM((TOK, 3 * D), bf16),
        pltpu.VMEM((TOK, D), bf16),
    ]
    tokens = whole(x_kernel, like((TOK, D)), attention, 2 * TOK * D * 4 * D, 24)(
        slots, gather_sum(), qkv_weight, out_weight, interleave()
    )
    tokens = lax.all_to_all(
        tokens.reshape(128, 2, D), ("gx", "gy"), split_axis=0, concat_axis=0, tiled=True
    ).reshape(TOK, D)
    tokens = whole(
        y_kernel,
        like((TOK, D)),
        attention + [pltpu.VMEM((TOK, FF), bf16)],
        2 * TOK * D * (4 * D + 2 * FF),
        40,
    )(tokens, separate(), qkv_weight, out_weight, up_weight, down_weight, to_owners())
    tokens = lax.all_to_all(
        tokens.reshape(8, 32, D), "gy", split_axis=0, concat_axis=0, tiled=True
    ).reshape(TOK, D)
    tokens = whole(home_kernel, like((TOK, D)), [], 2 * TOK * TOK * D, 8)(tokens, to_home())
    return tokens.reshape(2, 16, 8, D)


def solution(mesh):
    return jax.shard_map(
        shards,
        mesh=mesh,
        in_specs=(P(None, None, "gx", "gy"), P(), P(), P(), P(), P()),
        out_specs=P(None, "gy", "gx", None),
        check_vma=False,
    )
```

time: 380 us -> 100 us (0.26)
  other arithmetic: 120 us -> 0 us
  local copies, waits for them, and re-layouts: 117 us -> 14 us
  waiting for transfers between devices: 39.1 us -> 0.01 us
  matrix products: 34.1 us -> 0 us
  starting transfers between devices: 36.9 us -> 6.31 us
  Pallas kernels: 0 us -> 28.9 us
  blocking collectives: 29.9 us -> 50.6 us
    add x2 -> x0, other arithmetic: 72.7 us -> none  [smooth_along(): total + taps[index] * lax.slice_in_dim(values, index, index + length, axi...]
    dot_general x10 -> x0, matrix products: 34.1 us -> none  [the longest x1 7.75 us: shards(): jnp.dot(upper, down_weight, preferred_element_type=jnp.float32)]
    convert_element_type x5 -> x0, other arithmetic: 31.8 us -> none  [the longest x1 29.7 us: shards(): filtered = smooth.astype(jnp.bfloat16)]
    all_to_all x6 -> x0, waiting for transfers between devices: 31.5 us -> none  [the longest x1 7.89 us: shards(): lax.all_to_all(query, 'gy', split_axis=2, concat_axis=1, tiled=True)]
    pallas_call x0 -> x7, Pallas kernels: none -> 28.9 us  [the longest x6 27.3 us: call(): pl.pallas_call(kernel, out_shape=out_shape, in_specs=[space] * len(operan...]
    all_to_all x6 -> x0, starting transfers between devices: 26.6 us -> none  [the longest x1 5.36 us: shards(): lax.all_to_all(query, 'gy', split_axis=2, concat_axis=1, tiled=True)]
    reshape x2, local copies, waits for them, and re-layouts: 29.3 us -> 3.78 us  [the longest x1 1.89 us: shards(): tokens = lax.all_to_all(tokens.reshape(128, 2, D), ('gx', 'gy'), split_ax...]
    all_to_all x2 -> x3, blocking collectives: 29.9 us -> 50.6 us  [the longest x1 18.5 us: shards(): lax.all_to_all(slots.reshape(NXL, SLOTS, D), 'gx', split_axis=0, concat_a...]
  transfers between devices with their start and end apart: 10 -> 2, of which waited for: 8 -> 0; matrix products, arithmetic and copies ran while one was open for 10% -> 0% of each run, Pallas kernels for 0% -> 5%
where the time goes in v1:
time: 100 us; the launch traced here: 99.9 us
  blocking collectives  50.6 us (51%)
  Pallas kernels  28.9 us (29%)
  local copies, waits for them, and re-layouts  14 us (14%)
  starting transfers between devices  6.31 us (6%)
    pallas_call x6, Pallas kernels, call(): pl.pallas_call(kernel, out_shape=out_shape, in_specs=[space] * len(operan...  27.3 us
    all_to_all x1, blocking collectives, shards(): lax.all_to_all(slots.reshape(NXL, SLOTS, D), 'gx', split_axis=0, concat_a...  18.5 us
    all_to_all x1, blocking collectives, shards(): lax.all_to_all(tokens.reshape(128, 2, D), ('gx', 'gy'), split_axis=0, con...  18.5 us
    all_to_all x1, blocking collectives, shards(): lax.all_to_all(tokens.reshape(8, 32, D), 'gy', split_axis=0, concat_axis=...  13.6 us
    unnamed x34, local copies, waits for them, and re-layouts  10.2 us
    ppermute x1, starting transfers between devices, shards(): lax.ppermute(upper, 'gy', [(i, (i + 1) % count) for i in range(count)])  4.03 us
    ppermute x1, starting transfers between devices, shards(): lax.ppermute(lower, 'gy', [((i + 1) % count, i) for i in range(count)])  2.28 us
  transfers between devices with their start and end apart: 2, of which 0 were waited for; matrix products, arithmetic and copies ran while one was open for 0% of the time, Pallas kernels for 5%

profile of v1, /device:TPU:0, one launch (start us, length us, event | category | flops | bytes accessed | tf_op | source)
XLA Modules:
  0.0 99.9 jit_solution(15523461740105487505)
XLA Ops:
  0.0 2.1 %copy-done.4 = f32[5,24,64,128]{3,2,1,0:T(8,128)S(1)} copy-done((f32[5,24,64,128]{3,2,1,0:T(8,128)S(1)}, f32[5,24,64,128]{3,2,1,0:T(8,128)}, u32[]{:S(2)}) %copy-start.4) | copy-done | bytes 3932184
  2.1 1.5 %shard_map.145 = (f32[5,16,64,128]{3,2,1,0:T(8,128)S(1)}, f32[5,4,1024]{2,1,0:T(4,128)S(1)}, f32[5,4,1024]{2,1,0:T(4,128)S(1)}) custom-call(f32[5,24,64,128]{3,2,1,0:T(8,128)S(1)} %copy-done.4), custom_call_target="tpu_custom_call" | custom-call | tf_op jit(solution)/shard_map/pallas_call | solution.py:341
  3.6 4.0 %collective-permute-start = (f32[5,4,1024]{2,1,0:T(4,128)S(1)}, f32[5,4,1024]{2,1,0:T(4,128)S(1)}, u32[]{:S(2)}, u32[]{:S(2)}) collective-permute-start(f32[5,4,1024]{2,1,0:T(4,128)S(1)} %get-tuple-element.9), channel_id=1, source_target_pairs={{0,1},{1,2},{2,3},{3,4},{4,5},{5,6},{6,7},{7,0},{8,9},{9,10},{10,1... | collective-permute-start | bytes 245768 | tf_op jit(solution)/shard_map/ppermute | solution.py:359
  7.7 2.3 %collective-permute-start.1 = (f32[5,4,1024]{2,1,0:T(4,128)S(1)}, f32[5,4,1024]{2,1,0:T(4,128)S(1)}, u32[]{:S(2)}, u32[]{:S(2)}) collective-permute-start(f32[5,4,1024]{2,1,0:T(4,128)S(1)} %get-tuple-element.10), channel_id=1, source_target_pairs={{1,0},{2,1},{3,2},{4,3},{5,4},{6,5},{7,6},{0,7},{9,8},{10,9},{11,1... | collective-permute-start | bytes 245768 | tf_op jit(solution)/shard_map/ppermute | solution.py:360
  10.0 0.9 copy-done.14
  10.9 3.9 %shard_map.146.along_ref = f32[5,16,64,128]{3,2,1,0:T(8,128)S(1)} custom-call(f32[5,16,64,128]{3,2,1,0:T(8,128)S(1)} %get-tuple-element.8.smooth_ref, bf16[256,256]{1,0:T(8,128)(2,1)S(1)} %copy-done.14), custom_call_target="tpu_custom_call" | custom-call | flops 671088640 | bytes 2752512 | tf_op jit(solution)/shard_map/pallas_call | solution.py:321
  14.7 0.0 copy-start.8
  14.8 1.2 %shard_map.147.weight_ref = bf16[2560,768]{1,0:T(8,128)(2,1)S(1)} custom-call(bf16[2560,768]{1,0:T(8,128)(2,1)S(1)} %copy-done.5, bf16[256,256]{1,0:T(8,128)(2,1)S(1)} %copy-done.9), custom_call_target="tpu_custom_call" | custom-call | flops 1006632960 | bytes 4063232 | tf_op jit(solution)/shard_map/pallas_call | solution.py:321
  16.0 0.0 copy-start.11
  16.1 8.2 %shard_map.148 = bf16[512,768]{1,0:T(8,128)(2,1)S(1)} custom-call(f32[5,16,64,128]{3,2,1,0:T(8,128)S(1)} %shard_map.146.along_ref, f32[5,4,1024]{2,1,0:T(4,128)S(1)} %collective-permute-done.upper_ref, f32[5,4,1024]{2,1,0:T(4,128)S(1)} %collective-permute-done.1.lower_ref, bf16[32,128]{1,0:T(8,128)(2,1)S(1)} %copy-done.16, ...), custom_call_target="tpu_custom_call" | custom-call | flops 1761607680 | bytes 7184384 | tf_op jit(solution)/shard_map/pallas_call | solution.py:321
  24.3 18.5 %all_to_all.15 = bf16[16,32,768]{2,1,0:T(8,128)(2,1)S(1)} all-to-all(bf16[16,32,768]{2,1,0:T(8,128)(2,1)S(1)} %bitcast.5), channel_id=1, replica_groups=mesh['gx'=16,'gy'=8] {'gx'}, dimensions={0} | all-to-all | bytes 1572864 | tf_op jit(solution)/shard_map/all_to_all | solution.py:379
  42.8 3.0 %shard_map.149 = bf16[256,768]{1,0:T(8,128)(2,1)S(1)} custom-call(bf16[512,768]{1,0:T(8,128)(2,1)S(1)} %bitcast.6, bf16[256,512]{1,0:T(8,128)(2,1)S(1)} %copy-done.11, bf16[768,2304]{1,0:T(8,128)(2,1)S(1)} %copy-done, bf16[768,768]{1,0:T(8,128)(2,1)S(1)} %copy-done.2, bf16[256,256]{1,0:T(8,128)(2,1)S(1)} %copy-done.13), custom_call_target="tpu_custom_call" | custom-call | flops 1207959552 | bytes 5898240 | tf_op jit(solution)/shard_map/pallas_call | solution.py:321
  45.8 0.7 copy-done.6
  46.6 1.9 %reshape.23 = bf16[128,2,768]{2,1,0:T(2,128)(2,1)} reshape(bf16[256,768]{1,0:T(8,128)(2,1)} %copy-done.6) | data formatting | bytes 786432 | tf_op jit(solution)/shard_map/reshape | solution.py:391
  48.5 18.5 %all_to_all.16 = bf16[128,2,768]{2,1,0:T(2,128)(2,1)} all-to-all(bf16[128,2,768]{2,1,0:T(2,128)(2,1)} %reshape.23), channel_id=1, replica_groups=mesh['gx'=16,'gy'=8] {'gx','gy'}, dimensions={0} | all-to-all | bytes 786432 | tf_op jit(solution)/shard_map/all_to_all | solution.py:390
  66.9 1.9 %reshape.24.tokens_ref = bf16[256,768]{1,0:T(8,128)(2,1)} reshape(bf16[128,2,768]{2,1,0:T(2,128)(2,1)} %all_to_all.16) | data formatting | bytes 786432 | tf_op jit(solution)/shard_map/reshape | solution.py:392
  68.8 2.3 %copy-done.1 = bf16[768,3072]{1,0:T(8,128)(2,1)S(1)} copy-done((bf16[768,3072]{1,0:T(8,128)(2,1)S(1)}, bf16[768,3072]{1,0:T(8,128)(2,1)}, u32[]{:S(2)}) %copy-start.1) | copy-done | bytes 4718616
  71.2 1.3 %copy-done.3 = bf16[768,768]{1,0:T(8,128)(2,1)S(1)} copy-done((bf16[768,768]{1,0:T(8,128)(2,1)S(1)}, bf16[768,768]{1,0:T(8,128)(2,1)}, u32[]{:S(2)}) %copy-start.3) | copy-done | bytes 1179672
  72.4 1.0 copy-done.7
  73.4 0.9 copy-done.10
  74.3 0.9 copy-done.15
  75.2 10.1 %shard_map.150 = bf16[256,768]{1,0:T(8,128)(2,1)S(1)} custom-call(bf16[256,768]{1,0:T(8,128)(2,1)S(1)} %copy-done.7, bf16[256,256]{1,0:T(8,128)(2,1)S(1)} %copy-done.15, bf16[768,2304]{1,0:T(8,128)(2,1)S(1)} %copy-done, bf16[768,768]{1,0:T(8,128)(2,1)S(1)} %copy-done.3, bf16[768,3072]{1,0:T(8,128)(2,1)S(1)} %copy-done.1, bf16[3072,768]{1,0:T(8,128)(2,1)} %down_ref.1, ...), custom_call_target="tpu_custom_call" | custom-call | flops 3623878656 | bytes 14811136 | tf_op jit(solution)/shard_map/pallas_call | solution.py:321
  85.3 13.6 %all_to_all.17 = bf16[8,32,768]{2,1,0:T(8,128)(2,1)S(1)} all-to-all(bf16[8,32,768]{2,1,0:T(8,128)(2,1)S(1)} %bitcast.8), channel_id=1, replica_groups=mesh['gx'=16,'gy'=8] {'gy'}, dimensions={0} | all-to-all | bytes 786432 | tf_op jit(solution)/shard_map/all_to_all | solution.py:400
  98.9 1.0 %shard_map.151 = bf16[256,768]{1,0:T(8,128)(2,1)} custom-call(bf16[256,768]{1,0:T(8,128)(2,1)S(1)} %bitcast.7, bf16[256,256]{1,0:T(8,128)(2,1)S(1)} %copy-done.12), custom_call_target="tpu_custom_call" | custom-call | flops 100663296 | bytes 524288 | tf_op jit(solution)/shard_map/pallas_call | solution.py:321
  (26 shorter events, 0.1 us)
Async XLA Ops:
  0.0 2.1 %copy-start.4 = (f32[5,24,64,128]{3,2,1,0:T(8,128)S(1)}, f32[5,24,64,128]{3,2,1,0:T(8,128)}, u32[]{:S(2)}) copy-start(f32[5,24,64,128]{3,2,1,0:T(8,128)} %fields_ref.1) | copy-start | bytes 11796484
  2.1 12.6 %copy-start.5 = (bf16[2560,768]{1,0:T(8,128)(2,1)S(1)}, bf16[2560,768]{1,0:T(8,128)(2,1)}, u32[]{:S(2)}) copy-start(bf16[2560,768]{1,0:T(8,128)(2,1)} %weight_ref.1) | copy-start | bytes 11796484
  2.1 12.6 %copy-start.9 = (bf16[256,256]{1,0:T(8,128)(2,1)S(1)}, bf16[256,256]{1,0:T(8,128)(2,1)}, u32[]{:S(2)}) copy-start(bf16[256,256]{1,0:T(8,128)(2,1)} %constant.17.clone.order_ref) | copy-start | bytes 393220
  3.6 12.4 %collective-permute-start = (f32[5,4,1024]{2,1,0:T(4,128)S(1)}, f32[5,4,1024]{2,1,0:T(4,128)S(1)}, u32[]{:S(2)}, u32[]{:S(2)}) collective-permute-start(f32[5,4,1024]{2,1,0:T(4,128)S(1)} %get-tuple-element.9), channel_id=1, source_target_pairs={{0,1},{1,2},{2,3},{3,4},{4,5},{5,6},{6,7},{7,0},{8,9},{9,10},{10,1... | collective-permute-start | bytes 245768 | tf_op jit(solution)/shard_map/ppermute | solution.py:359
  7.7 8.4 %collective-permute-start.1 = (f32[5,4,1024]{2,1,0:T(4,128)S(1)}, f32[5,4,1024]{2,1,0:T(4,128)S(1)}, u32[]{:S(2)}, u32[]{:S(2)}) collective-permute-start(f32[5,4,1024]{2,1,0:T(4,128)S(1)} %get-tuple-element.10), channel_id=1, source_target_pairs={{1,0},{2,1},{3,2},{4,3},{5,4},{6,5},{7,6},{0,7},{9,8},{10,9},{11,1... | collective-permute-start | bytes 245768 | tf_op jit(solution)/shard_map/ppermute | solution.py:360
  10.0 0.9 copy-start.14
  14.7 1.3 %copy-start.8 = (bf16[512,448]{1,0:T(8,128)(2,1)S(1)}, bf16[512,448]{1,0:T(8,128)(2,1)}, u32[]{:S(2)}) copy-start(bf16[512,448]{1,0:T(8,128)(2,1)} %constant.19.clone.order_ref) | copy-start | bytes 1376260
  14.8 1.3 %copy-start.16 = (bf16[32,128]{1,0:T(8,128)(2,1)S(1)}, bf16[32,128]{1,0:T(8,128)(2,1)}, u32[]{:S(2)}) copy-start(bf16[32,128]{1,0:T(8,128)(2,1)} %constant.18.clone.side_ref) | copy-start | bytes 24580
  16.0 26.9 %copy-start = (bf16[768,2304]{1,0:T(8,128)(2,1)S(1)}, bf16[768,2304]{1,0:T(8,128)(2,1)}, u32[]{:S(2)}) copy-start(bf16[768,2304]{1,0:T(8,128)(2,1)} %qkv_ref.3) | copy-start | bytes 10616836
  16.0 26.9 %copy-start.2 = (bf16[768,768]{1,0:T(8,128)(2,1)S(1)}, bf16[768,768]{1,0:T(8,128)(2,1)}, u32[]{:S(2)}) copy-start(bf16[768,768]{1,0:T(8,128)(2,1)} %outw_ref.3) | copy-start | bytes 3538948
  16.0 26.8 %copy-start.11 = (bf16[256,512]{1,0:T(8,128)(2,1)S(1)}, bf16[256,512]{1,0:T(8,128)(2,1)}, u32[]{:S(2)}) copy-start(bf16[256,512]{1,0:T(8,128)(2,1)} %constant.20.clone.sum_ref) | copy-start | bytes 786436
  16.0 26.8 %copy-start.13 = (bf16[256,256]{1,0:T(8,128)(2,1)S(1)}, bf16[256,256]{1,0:T(8,128)(2,1)}, u32[]{:S(2)}) copy-start(bf16[256,256]{1,0:T(8,128)(2,1)} %constant.21.clone.order_ref) | copy-start | bytes 393220
  45.8 0.7 copy-start.6
  68.8 2.3 %copy-start.1 = (bf16[768,3072]{1,0:T(8,128)(2,1)S(1)}, bf16[768,3072]{1,0:T(8,128)(2,1)}, u32[]{:S(2)}) copy-start(bf16[768,3072]{1,0:T(8,128)(2,1)} %up_ref.1) | copy-start | bytes 14155780
  71.2 1.3 %copy-start.3 = (bf16[768,768]{1,0:T(8,128)(2,1)S(1)}, bf16[768,768]{1,0:T(8,128)(2,1)}, u32[]{:S(2)}) copy-start(bf16[768,768]{1,0:T(8,128)(2,1)} %outw_ref.3) | copy-start | bytes 3538948
  72.4 1.0 copy-start.7
  73.4 0.9 copy-start.10
  74.3 0.9 copy-start.15
  75.2 23.6 %copy-start.12 = (bf16[256,256]{1,0:T(8,128)(2,1)S(1)}, bf16[256,256]{1,0:T(8,128)(2,1)}, u32[]{:S(2)}) copy-start(bf16[256,256]{1,0:T(8,128)(2,1)} %constant.23.clone.order_ref) | copy-start | bytes 393220

commit v2 on v1

--- a/solution.py
+++ b/solution.py
@@ -280,7 +280,8 @@
 def x_kernel(slots_ref, sum_ref, qkv_ref, outw_ref, order_ref, out_ref, hidden, three, mixed):
     hidden[...] = dot(sum_ref[...], slots_ref[...])
     attend(hidden, qkv_ref, outw_ref, three, mixed)
-    out_ref[...] = dot(order_ref[...], hidden[...].astype(bf16)).astype(bf16)
+    tokens = dot(order_ref[...], hidden[...].astype(bf16)).astype(bf16)
+    out_ref[...] = tokens.reshape(128, 2, D)
 
 
 def y_kernel(
@@ -297,7 +298,7 @@
     mixed,
     upper,
 ):
-    hidden[...] = dot(split_ref[...], tokens_ref[...])
+    hidden[...] = dot(split_ref[...], tokens_ref[...].reshape(TOK, D))
     attend(hidden, qkv_ref, outw_ref, three, mixed)
     normed = layer_norm(hidden[...])
     for tile in range(FF // 256):
@@ -348,7 +349,7 @@
             like((NF, R, ZS * CX), f32),
             like((NF, R, ZS * CX), f32),
         ],
-        compiler_params=pltpu.CompilerParams(vmem_limit_bytes=16 << 20),
+        compiler_params=pltpu.CompilerParams(vmem_limit_bytes=8 << 20),
     )(fields)
 
 
@@ -358,10 +359,10 @@
     smooth, upper, lower = prepare(fields)
     upper = lax.ppermute(upper, "gy", [(i, (i + 1) % count) for i in range(count)])
     lower = lax.ppermute(lower, "gy", [((i + 1) % count, i) for i in range(count)])
-    along = whole(band_kernel, like((NF, ZS, CX, CY), f32), [], 2 * 5120 * 256 * 256, 16)(
+    along = whole(band_kernel, like((NF, ZS, CX, CY), f32), [], 2 * 5120 * 256 * 256, 8)(
         smooth, band
     )
-    weight = whole(weight_kernel, like((KIN, D)), [], 2 * KIN * 256 * D, 24)(
+    weight = whole(weight_kernel, like((KIN, D)), [], 2 * KIN * 256 * D, 8)(
         embed_weight, weight_order()
     )
     slots = whole(
@@ -374,7 +375,7 @@
             pltpu.VMEM((ALL_ROWS, 256), bf16),
         ],
         2 * ALL_ROWS * KIN * D,
-        40,
+        14,
     )(along, upper, lower, side, weight, message_order())
     slots = lax.all_to_all(
         slots.reshape(NXL, SLOTS, D), "gx", split_axis=0, concat_axis=0, tiled=True
@@ -384,18 +385,18 @@
         pltpu.VMEM((TOK, 3 * D), bf16),
         pltpu.VMEM((TOK, D), bf16),
     ]
-    tokens = whole(x_kernel, like((TOK, D)), attention, 2 * TOK * D * 4 * D, 24)(
+    tokens = whole(x_kernel, like((128, 2, D)), attention, 2 * TOK * D * 4 * D, 10)(
         slots, gather_sum(), qkv_weight, out_weight, interleave()
     )
     tokens = lax.all_to_all(
-        tokens.reshape(128, 2, D), ("gx", "gy"), split_axis=0, concat_axis=0, tiled=True
-    ).reshape(TOK, D)
+        tokens, ("gx", "gy"), split_axis=0, concat_axis=0, tiled=True
+    )
     tokens = whole(
         y_kernel,
         like((TOK, D)),
         attention + [pltpu.VMEM((TOK, FF), bf16)],
         2 * TOK * D * (4 * D + 2 * FF),
-        40,
+        14,
     )(tokens, separate(), qkv_weight, out_weight, up_weight, down_weight, to_owners())
     tokens = lax.all_to_all(
         tokens.reshape(8, 32, D), "gy", split_axis=0, concat_axis=0, tiled=True

time: 100 us -> 86.9 us (0.87)
  local copies, waits for them, and re-layouts: 14 us -> 3.1 us
  Pallas kernels: 28.9 us -> 26.5 us
    unnamed x34 -> x32, local copies, waits for them, and re-layouts: 10.2 us -> 3.1 us
    reshape x2 -> x0, local copies, waits for them, and re-layouts: 3.78 us -> none  [the longest x1 1.89 us: shards(): tokens = lax.all_to_all(tokens.reshape(128, 2, D), ('gx', 'gy'), split_ax...]
    pallas_call x6, Pallas kernels: 27.3 us -> 25 us  [call(): pl.pallas_call(kernel, out_shape=out_shape, in_specs=[space] * len(operan...]
  transfers between devices with their start and end apart: 2 -> 2, of which waited for: 0 -> 0; matrix products, arithmetic and copies ran while one was open for 0% -> 0% of each run, Pallas kernels for 5% -> 6%
where the time goes in v2:
time: 86.9 us; the launch traced here: 86.7 us
  blocking collectives  50.6 us (58%)
  Pallas kernels  26.5 us (30%)
  starting transfers between devices  6.31 us (7%)
  local copies, waits for them, and re-layouts  3.1 us (4%)
    pallas_call x6, Pallas kernels, call(): pl.pallas_call(kernel, out_shape=out_shape, in_specs=[space] * len(operan...  25 us
    all_to_all x1, blocking collectives, shards(): lax.all_to_all(slots.reshape(NXL, SLOTS, D), 'gx', split_axis=0, concat_a...  18.8 us
    all_to_all x1, blocking collectives, shards(): lax.all_to_all(tokens, ('gx', 'gy'), split_axis=0, concat_axis=0, tiled=T...  18.2 us
    all_to_all x1, blocking collectives, shards(): lax.all_to_all(tokens.reshape(8, 32, D), 'gy', split_axis=0, concat_axis=...  13.6 us
    ppermute x1, starting transfers between devices, shards(): lax.ppermute(upper, 'gy', [(i, (i + 1) % count) for i in range(count)])  4.03 us
    unnamed x32, local copies, waits for them, and re-layouts  3.1 us
    ppermute x1, starting transfers between devices, shards(): lax.ppermute(lower, 'gy', [((i + 1) % count, i) for i in range(count)])  2.28 us
  transfers between devices with their start and end apart: 2, of which 0 were waited for; matrix products, arithmetic and copies ran while one was open for 0% of the time, Pallas kernels for 6%

profile of v2, /device:TPU:0, one launch (start us, length us, event | category | flops | bytes accessed | tf_op | source)
XLA Modules:
  0.0 86.7 jit_solution(9385832794146574)
XLA Ops:
  0.0 2.1 %copy-done.2 = f32[5,24,64,128]{3,2,1,0:T(8,128)S(1)} copy-done((f32[5,24,64,128]{3,2,1,0:T(8,128)S(1)}, f32[5,24,64,128]{3,2,1,0:T(8,128)}, u32[]{:S(2)}) %copy-start.2) | copy-done | bytes 3932184
  2.1 1.5 %shard_map.145 = (f32[5,16,64,128]{3,2,1,0:T(8,128)S(1)}, f32[5,4,1024]{2,1,0:T(4,128)S(1)}, f32[5,4,1024]{2,1,0:T(4,128)S(1)}) custom-call(f32[5,24,64,128]{3,2,1,0:T(8,128)S(1)} %copy-done.2), custom_call_target="tpu_custom_call" | custom-call | tf_op jit(solution)/shard_map/pallas_call | solution.py:342
  3.6 4.0 %collective-permute-start = (f32[5,4,1024]{2,1,0:T(4,128)S(1)}, f32[5,4,1024]{2,1,0:T(4,128)S(1)}, u32[]{:S(2)}, u32[]{:S(2)}) collective-permute-start(f32[5,4,1024]{2,1,0:T(4,128)S(1)} %get-tuple-element.9), channel_id=1, source_target_pairs={{0,1},{1,2},{2,3},{3,4},{4,5},{5,6},{6,7},{7,0},{8,9},{9,10},{10,1... | collective-permute-start | bytes 245768 | tf_op jit(solution)/shard_map/ppermute | solution.py:360
  7.7 2.3 %collective-permute-start.1 = (f32[5,4,1024]{2,1,0:T(4,128)S(1)}, f32[5,4,1024]{2,1,0:T(4,128)S(1)}, u32[]{:S(2)}, u32[]{:S(2)}) collective-permute-start(f32[5,4,1024]{2,1,0:T(4,128)S(1)} %get-tuple-element.10), channel_id=1, source_target_pairs={{1,0},{2,1},{3,2},{4,3},{5,4},{6,5},{7,6},{0,7},{9,8},{10,9},{11,1... | collective-permute-start | bytes 245768 | tf_op jit(solution)/shard_map/ppermute | solution.py:361
  10.0 0.9 %copy-done.9 = bf16[256,256]{1,0:T(8,128)(2,1)S(1)} copy-done((bf16[256,256]{1,0:T(8,128)(2,1)S(1)}, bf16[256,256]{1,0:T(8,128)(2,1)}, u32[]{:S(2)}) %copy-start.9) | copy-done | bytes 131096
  10.9 3.9 %shard_map.146.along_ref = f32[5,16,64,128]{3,2,1,0:T(8,128)S(1)} custom-call(f32[5,16,64,128]{3,2,1,0:T(8,128)S(1)} %get-tuple-element.8.smooth_ref, bf16[256,256]{1,0:T(8,128)(2,1)S(1)} %copy-done.9), custom_call_target="tpu_custom_call" | custom-call | flops 671088640 | bytes 2752512 | tf_op jit(solution)/shard_map/pallas_call | solution.py:322
  14.7 0.0 copy-start.4
  14.8 0.0 copy-start.11
  14.8 0.0 slice-start.2
  14.8 1.2 %shard_map.147.weight_ref = bf16[2560,768]{1,0:T(8,128)(2,1)S(1)} custom-call(bf16[2560,768]{1,0:T(8,128)(2,1)S(1)} %copy-done.3, bf16[256,256]{1,0:T(8,128)(2,1)S(1)} %copy-done.5), custom_call_target="tpu_custom_call" | custom-call | flops 1006632960 | bytes 4063232 | tf_op jit(solution)/shard_map/pallas_call | solution.py:322
  16.0 0.0 copy-start
  16.0 0.0 copy-start.6
  16.0 0.0 copy-start.8
  16.0 0.0 slice-start.3
  16.1 0.0 slice-start
  16.1 8.2 %shard_map.148 = bf16[512,768]{1,0:T(8,128)(2,1)S(1)} custom-call(f32[5,16,64,128]{3,2,1,0:T(8,128)S(1)} %shard_map.146.along_ref, f32[5,4,1024]{2,1,0:T(4,128)S(1)} %collective-permute-done.upper_ref, f32[5,4,1024]{2,1,0:T(4,128)S(1)} %collective-permute-done.1.lower_ref, bf16[32,128]{1,0:T(8,128)(2,1)S(1)} %copy-done.11, ...), custom_call_target="tpu_custom_call" | custom-call | flops 1761607680 | bytes 7184384 | tf_op jit(solution)/shard_map/pallas_call | solution.py:322
  24.3 0.0 slice-start.1
  24.3 18.8 %all_to_all.15 = bf16[16,32,768]{2,1,0:T(8,128)(2,1)S(1)} all-to-all(bf16[16,32,768]{2,1,0:T(8,128)(2,1)S(1)} %bitcast.9), channel_id=1, replica_groups=mesh['gx'=16,'gy'=8] {'gx'}, dimensions={0} | all-to-all | bytes 1572864 | tf_op jit(solution)/shard_map/all_to_all | solution.py:380
  43.2 3.0 %shard_map.149 = bf16[128,2,768]{2,1,0:T(2,128)(2,1)S(1)} custom-call(bf16[512,768]{1,0:T(8,128)(2,1)S(1)} %bitcast.10, bf16[256,512]{1,0:T(8,128)(2,1)S(1)} %copy-done.6, bf16[768,2304]{1,0:T(8,128)(2,1)S(1)} %copy-done, bf16[768,768]{1,0:T(8,128)(2,1)S(1)} %copy-done.1, bf16[256,256]{1,0:T(8,128)(2,1)S(1)} %copy-done.8), custom_call_target="tpu_custom_call" | custom-call | flops 1207959552 | bytes 5898240 | tf_op jit(solution)/shard_map/pallas_call | solution.py:322
  46.2 18.2 %all_to_all.16.tokens_ref = bf16[128,2,768]{2,1,0:T(2,128)(2,1)S(1)} all-to-all(bf16[128,2,768]{2,1,0:T(2,128)(2,1)S(1)} %shard_map.149), channel_id=1, replica_groups=mesh['gx'=16,'gy'=8] {'gx','gy'}, dimensions={0} | all-to-all | bytes 786432 | tf_op jit(solution)/shard_map/all_to_all | solution.py:391
  64.4 0.0 copy-start.7
  64.4 7.7 %shard_map.150 = bf16[256,768]{1,0:T(8,128)(2,1)S(1)} custom-call(bf16[128,2,768]{2,1,0:T(2,128)(2,1)S(1)} %all_to_all.16.tokens_ref, bf16[256,256]{1,0:T(8,128)(2,1)S(1)} %copy-done.10, bf16[768,2304]{1,0:T(8,128)(2,1)S(1)} %copy-done, bf16[768,768]{1,0:T(8,128)(2,1)S(1)} %copy-done.1, bf16[768,3072]{1,0:T(8,128)(2,1)S(1)} %bitcast.6, ...), custom_call_target="tpu_custom_call" | custom-call | flops 3623878656 | bytes 14811136 | tf_op jit(solution)/shard_map/pallas_call | solution.py:322
  72.1 13.6 %all_to_all.17 = bf16[8,32,768]{2,1,0:T(8,128)(2,1)S(1)} all-to-all(bf16[8,32,768]{2,1,0:T(8,128)(2,1)S(1)} %bitcast.12), channel_id=1, replica_groups=mesh['gx'=16,'gy'=8] {'gy'}, dimensions={0} | all-to-all | bytes 786432 | tf_op jit(solution)/shard_map/all_to_all | solution.py:401
  85.7 1.0 %shard_map.151 = bf16[256,768]{1,0:T(8,128)(2,1)} custom-call(bf16[256,768]{1,0:T(8,128)(2,1)S(1)} %bitcast.11, bf16[256,256]{1,0:T(8,128)(2,1)S(1)} %copy-done.7), custom_call_target="tpu_custom_call" | custom-call | flops 100663296 | bytes 524288 | tf_op jit(solution)/shard_map/pallas_call | solution.py:322
  (24 shorter events, 0.0 us)
Async XLA Ops:
  0.0 2.1 %copy-start.2 = (f32[5,24,64,128]{3,2,1,0:T(8,128)S(1)}, f32[5,24,64,128]{3,2,1,0:T(8,128)}, u32[]{:S(2)}) copy-start(f32[5,24,64,128]{3,2,1,0:T(8,128)} %fields_ref.1) | copy-start | bytes 11796484
  2.1 12.6 %copy-start.3 = (bf16[2560,768]{1,0:T(8,128)(2,1)S(1)}, bf16[2560,768]{1,0:T(8,128)(2,1)}, u32[]{:S(2)}) copy-start(bf16[2560,768]{1,0:T(8,128)(2,1)} %weight_ref.1) | copy-start | bytes 11796484
  2.1 12.6 %copy-start.5 = (bf16[256,256]{1,0:T(8,128)(2,1)S(1)}, bf16[256,256]{1,0:T(8,128)(2,1)}, u32[]{:S(2)}) copy-start(bf16[256,256]{1,0:T(8,128)(2,1)} %constant.17.clone.order_ref) | copy-start | bytes 393220
  3.6 12.4 %collective-permute-start = (f32[5,4,1024]{2,1,0:T(4,128)S(1)}, f32[5,4,1024]{2,1,0:T(4,128)S(1)}, u32[]{:S(2)}, u32[]{:S(2)}) collective-permute-start(f32[5,4,1024]{2,1,0:T(4,128)S(1)} %get-tuple-element.9), channel_id=1, source_target_pairs={{0,1},{1,2},{2,3},{3,4},{4,5},{5,6},{6,7},{7,0},{8,9},{9,10},{10,1... | collective-permute-start | bytes 245768 | tf_op jit(solution)/shard_map/ppermute | solution.py:360
  7.7 8.4 %collective-permute-start.1 = (f32[5,4,1024]{2,1,0:T(4,128)S(1)}, f32[5,4,1024]{2,1,0:T(4,128)S(1)}, u32[]{:S(2)}, u32[]{:S(2)}) collective-permute-start(f32[5,4,1024]{2,1,0:T(4,128)S(1)} %get-tuple-element.10), channel_id=1, source_target_pairs={{1,0},{2,1},{3,2},{4,3},{5,4},{6,5},{7,6},{0,7},{9,8},{10,9},{11,1... | collective-permute-start | bytes 245768 | tf_op jit(solution)/shard_map/ppermute | solution.py:361
  10.0 0.9 %copy-start.9 = (bf16[256,256]{1,0:T(8,128)(2,1)S(1)}, bf16[256,256]{1,0:T(8,128)(2,1)}, u32[]{:S(2)}) copy-start(bf16[256,256]{1,0:T(8,128)(2,1)} %constant.16.clone.band_ref) | copy-start | bytes 393220
  14.7 1.3 %copy-start.4 = (bf16[512,448]{1,0:T(8,128)(2,1)S(1)}, bf16[512,448]{1,0:T(8,128)(2,1)}, u32[]{:S(2)}) copy-start(bf16[512,448]{1,0:T(8,128)(2,1)} %constant.19.clone.order_ref) | copy-start | bytes 1376260
  14.8 1.3 %copy-start.11 = (bf16[32,128]{1,0:T(8,128)(2,1)S(1)}, bf16[32,128]{1,0:T(8,128)(2,1)}, u32[]{:S(2)}) copy-start(bf16[32,128]{1,0:T(8,128)(2,1)} %constant.18.clone.side_ref) | copy-start | bytes 24580
  14.8 49.6 %slice-start.2 = ((s8[4718592]{0:T(1024)(128)(4,1)}), s8[4194304]{0:T(1024)(128)(4,1)S(1)}, s32[]{:S(2)}) async-start(s8[4718592]{0:T(1024)(128)(4,1)} %bitcast.7), calls=%async_computation.5 | async-start | bytes 8388608
  16.0 27.2 %copy-start = (bf16[768,2304]{1,0:T(8,128)(2,1)S(1)}, bf16[768,2304]{1,0:T(8,128)(2,1)}, u32[]{:S(2)}) copy-start(bf16[768,2304]{1,0:T(8,128)(2,1)} %qkv_ref.3) | copy-start | bytes 10616836
  16.0 27.2 %copy-start.1 = (bf16[768,768]{1,0:T(8,128)(2,1)S(1)}, bf16[768,768]{1,0:T(8,128)(2,1)}, u32[]{:S(2)}) copy-start(bf16[768,768]{1,0:T(8,128)(2,1)} %outw_ref.3) | copy-start | bytes 3538948
  16.0 27.1 %copy-start.6 = (bf16[256,512]{1,0:T(8,128)(2,1)S(1)}, bf16[256,512]{1,0:T(8,128)(2,1)}, u32[]{:S(2)}) copy-start(bf16[256,512]{1,0:T(8,128)(2,1)} %constant.20.clone.sum_ref) | copy-start | bytes 786436
  16.0 27.1 %copy-start.8 = (bf16[256,256]{1,0:T(8,128)(2,1)S(1)}, bf16[256,256]{1,0:T(8,128)(2,1)}, u32[]{:S(2)}) copy-start(bf16[256,256]{1,0:T(8,128)(2,1)} %constant.21.clone.order_ref) | copy-start | bytes 393220
  16.0 48.3 %slice-start.3 = ((s8[4718592]{0:T(1024)(128)(4,1)}), s8[524288]{0:T(1024)(128)(4,1)S(1)}, s32[]{:S(2)}) async-start(s8[4718592]{0:T(1024)(128)(4,1)} %bitcast.7), calls=%async_computation.6 | async-start | bytes 1048576
  16.1 48.3 %slice-start = ((s8[4718592]{0:T(1024)(128)(4,1)}), s8[524288]{0:T(1024)(128)(4,1)S(1)}, s32[]{:S(2)}) async-start(s8[4718592]{0:T(1024)(128)(4,1)} %bitcast.5), calls=%async_computation.3 | async-start | bytes 1048576
  24.3 40.0 %slice-start.1 = ((s8[4718592]{0:T(1024)(128)(4,1)}), s8[4194304]{0:T(1024)(128)(4,1)S(1)}, s32[]{:S(2)}) async-start(s8[4718592]{0:T(1024)(128)(4,1)} %bitcast.5), calls=%async_computation.4 | async-start | bytes 8388608
  43.1 21.2 %copy-start.10 = (bf16[256,256]{1,0:T(8,128)(2,1)S(1)}, bf16[256,256]{1,0:T(8,128)(2,1)}, u32[]{:S(2)}) copy-start(bf16[256,256]{1,0:T(8,128)(2,1)} %constant.22.clone.split_ref) | copy-start | bytes 393220
  64.4 21.3 %copy-start.7 = (bf16[256,256]{1,0:T(8,128)(2,1)S(1)}, bf16[256,256]{1,0:T(8,128)(2,1)}, u32[]{:S(2)}) copy-start(bf16[256,256]{1,0:T(8,128)(2,1)} %constant.23.clone.order_ref) | copy-start | bytes 393220

commit v3 on v2

--- a/solution.py
+++ b/solution.py
@@ -21,7 +21,7 @@
 NXL = 16
 TOK = 256
 EXT = 10
-SLOTS = 32
+SLOTS = 28
 BOUND = (0, 1, 8, 9)
 HI_ROWS = EXT * 32
 ALL_ROWS = HI_ROWS + 128
@@ -49,20 +49,35 @@
     return high, low
 
 
-def band_tables():
+def side_table():
     wide = np.zeros((CY + 2 * R, CY), np.float32)
     for out in range(CY):
         column = (out % 8) * 16 + out // 8
         for k in range(2 * R + 1):
             wide[out + k, column] = TAPS[k]
-    main_hi, main_lo = split_np(wide[R : R + CY])
-    zero = np.zeros_like(main_hi)
-    main = np.concatenate(
-        [np.concatenate([main_hi, main_lo], 1), np.concatenate([main_hi, zero], 1)], 0
-    )
-    side_hi, side_lo = split_np(np.concatenate([wide[:R], wide[R + CY :]], 0))
-    side = np.concatenate([side_hi, side_hi, side_lo, np.zeros_like(side_hi)], 0)
-    return main, side
+    high, low = split_np(np.concatenate([wide[:R], wide[R + CY :]], 0))
+    return np.concatenate([high, high, low, np.zeros_like(high)], 0)
+
+
+def band_table():
+    row = lax.broadcasted_iota(jnp.int32, (CY, CY), 0)
+    column = lax.broadcasted_iota(jnp.int32, (CY, CY), 1)
+    apart = jnp.abs(row - ((column & 15) * 8 + (column >> 4)))
+    high = jnp.zeros((CY, CY), f32)
+    low = jnp.zeros((CY, CY), f32)
+    for k in range(R + 1):
+        tap_hi, tap_lo = split_np(TAPS[R + k])
+        high = jnp.where(apart == k, float(tap_hi), high)
+        low = jnp.where(apart == k, float(tap_lo), low)
+    left = jnp.concatenate([high, high], 0)
+    right = jnp.concatenate([low, jnp.zeros_like(low)], 0)
+    return jnp.concatenate([left, right], 1).astype(bf16)
+
+
+def weight_order():
+    row = lax.broadcasted_iota(jnp.int32, (256, 256), 0)
+    column = lax.broadcasted_iota(jnp.int32, (256, 256), 1)
+    return jnp.where(column == (row & 31) * 8 + (row >> 5), 1.0, 0.0).astype(bf16)
 
 
 def permutation(rows, columns, source):
@@ -73,16 +88,8 @@
     return as_bf16(table)
 
 
-def weight_order():
-    return permutation(256, 256, lambda r: [(r % 32) * 8 + r // 32])
-
-
 def message_order():
-    return permutation(
-        16 * SLOTS,
-        ALL_ROWS,
-        lambda r: [(r % SLOTS) * 16 + r // SLOTS] if r % SLOTS < ALL_ROWS // 16 else [],
-    )
+    return permutation(16 * SLOTS, ALL_ROWS, lambda r: [(r % SLOTS) * 16 + r // SLOTS])
 
 
 def gather_sum():
@@ -131,74 +138,52 @@
     return high, (values - high.astype(f32)).astype(bf16)
 
 
-def prep_kernel(fields_ref, smooth_ref, upper_ref, lower_ref):
-    for tile in range(CX // 8):
-        rows = slice(tile * 8, tile * 8 + 8)
-        plane = [fields_ref[0, z, rows, :] for z in range(ZS + 2 * R)]
-        for z in range(ZS):
-            total = float(TAPS[R]) * plane[z + R]
-            for k in range(1, R + 1):
-                total = total + float(TAPS[R + k]) * (plane[z + R - k] + plane[z + R + k])
-            smooth_ref[0, z, rows, :] = total
-    for pair in range(ZS // 2):
-        turned = smooth_ref[0, 2 * pair : 2 * pair + 2].reshape(128, 128).T
-        lower_ref[0, :, pair * 128 : pair * 128 + 128] = turned[:R]
-        upper_ref[0, :, pair * 128 : pair * 128 + 128] = turned[CY - R :]
-
-
-def band_kernel(smooth_ref, band_ref, along_ref):
-    band = band_ref[...]
-
-    def step(index, carry):
-        f, part = index // 4, index % 4
-        values = smooth_ref[f, pl.ds(part * 4, 4)].reshape(256, CY)
-        high, low = halves(values)
-        both = dot(jnp.concatenate([high, low], 1), band)
-        along_ref[f, pl.ds(part * 4, 4)] = (both[:, :CY] + both[:, CY:]).reshape(4, CX, CY)
-        return carry
-
-    lax.fori_loop(0, NF * 4, step, 0)
-
-
-def weight_kernel(weight_ref, order_ref, out_ref):
-    order = order_ref[...]
-    for tile in range(KIN // 256):
-        turned = dot(order, weight_ref[tile * 256 : tile * 256 + 256, :]).astype(bf16)
-        for y in range(8):
-            if tile < 8:
-                pair, inner = tile // 4, tile % 4
-                start = pair * 1024 + y * 128 + inner * 32
-            else:
-                start = 2048 + y * 64 + (tile - 8) * 32
-            out_ref[start : start + 32, :] = turned[y * 32 : y * 32 + 32]
+def prep_kernel(fields_ref, smooth_ref, upper_ref, lower_ref, cells, arrived):
+    copies = [
+        pltpu.make_async_copy(fields_ref.at[f], cells.at[f], arrived.at[f]) for f in range(NF)
+    ]
+    for copy in copies:
+        copy.start()
+    for f in range(NF):
+        copies[f].wait()
+        for tile in range(CX // 8):
+            rows = slice(tile * 8, tile * 8 + 8)
+            plane = [cells[f, z, rows, :] for z in range(ZS + 2 * R)]
+            for z in range(ZS):
+                total = float(TAPS[R]) * plane[z + R]
+                for k in range(1, R + 1):
+                    total = total + float(TAPS[R + k]) * (plane[z + R - k] + plane[z + R + k])
+                smooth_ref[f, z, rows, :] = total
+        for pair in range(ZS // 2):
+            turned = smooth_ref[f, 2 * pair : 2 * pair + 2].reshape(128, 128).T
+            lower_ref[f, :, pair * 128 : pair * 128 + 128] = turned[:R]
+            upper_ref[f, :, pair * 128 : pair * 128 + 128] = turned[CY - R :]
+
+
+def band_kernel(smooth_ref, weight_ref, along_ref, out_ref):
+    band = band_table()
+    order = weight_order()
+    for f in range(NF):
+        for part in range(4):
+            planes = slice(part * 4, part * 4 + 4)
+            high, low = halves(smooth_ref[f, planes].reshape(256, CY))
+            both = dot(jnp.concatenate([high, low], 1), band)
+            along_ref[f, planes] = (both[:, :CY] + both[:, CY:]).reshape(4, CX, CY)
+        for tile in (2 * f, 2 * f + 1):
+            turned = dot(order, weight_ref[tile * 256 : tile * 256 + 256, :]).astype(bf16)
+            for y in range(8):
+                if tile < 8:
+                    start = tile // 4 * 1024 + y * 128 + tile % 4 * 32
+                else:
+                    start = 2048 + y * 64 + (tile - 8) * 32
+                out_ref[start : start + 32, :] = turned[y * 32 : y * 32 + 32]
 
 
 def embed_kernel(
-    along_ref, upper_ref, lower_ref, side_ref, weight_ref, order_ref, out_ref, wide, smooth, lhs, mid
+    along_ref, upper_ref, lower_ref, side_ref, weight_ref, order_ref, out_ref, wide, smooth, lhs, both, mid
 ):
     side = side_ref[...]
     zero = jnp.zeros((ZS, PADX, CY), f32)
-    for f in range(NF):
-        wide[f, :, 0:PADX] = zero
-        wide[f, :, PADX + CX :] = zero
-        cells = jnp.concatenate([upper_ref[f], lower_ref[f]], 0)
-        high = cells.astype(bf16).astype(f32)
-        stacked = jnp.concatenate([high, cells - high, high, jnp.zeros_like(high)], 0)
-        added = dot(stacked.T.astype(bf16), side)
-        wide[f, :, PADX : PADX + CX] = along_ref[f] + added.reshape(ZS, CX, CY)
-
-    def step(index, carry):
-        f, z = index // ZS, index % ZS
-        total = float(TAPS[R]) * wide[f, z, pl.ds(PADX - 8, 80), :]
-        for k in range(1, R + 1):
-            total = total + float(TAPS[R + k]) * (
-                wide[f, z, pl.ds(PADX - 8 - k, 80), :] + wide[f, z, pl.ds(PADX - 8 + k, 80), :]
-            )
-        smooth[f, z] = total
-        return carry
-
-    lax.fori_loop(0, NF * ZS, step, 0)
-
     lane = lax.broadcasted_iota(jnp.int32, (16, 128), 1)
     first = lane < 64
 
@@ -210,35 +195,58 @@
             row = HI_ROWS + (BOUND.index(ext) * 2 + a) * 16
             lhs[row : row + 16, start : start + 128] = low
 
-    for ext in range(EXT):
-        rows = slice(ext * 8, ext * 8 + 8)
-        for a in range(2):
-            for pair in range(2):
-                block = smooth[2 * pair : 2 * pair + 2, a * 8 : a * 8 + 8, rows, :]
-                turned = block.reshape(128, 128).T
-                for y in range(8):
-                    put(ext, a, pair * 1024 + y * 128, turned[y * 16 : y * 16 + 16])
-        turned = smooth[4, :, rows, :].reshape(128, 128).T
-        for m in range(4):
-            even = turned[m * 32 : m * 32 + 16]
-            odd = turned[m * 32 + 16 : m * 32 + 32]
-            start = 2048 + m * 128
-            put(ext, 0, start, jnp.where(first, even, pltpu.roll(odd, 64, 1)))
-            put(ext, 1, start, jnp.where(first, pltpu.roll(even, 64, 1), odd))
+    for chunk, members in enumerate(((0, 1), (2, 3), (4,))):
+        for f in members:
+            wide[f, :, 0:PADX] = zero
+            wide[f, :, PADX + CX :] = zero
+            cells = jnp.concatenate([upper_ref[f], lower_ref[f]], 0)
+            high = cells.astype(bf16).astype(f32)
+            stacked = jnp.concatenate([high, cells - high, high, jnp.zeros_like(high)], 0)
+            added = dot(stacked.T.astype(bf16), side)
+            wide[f, :, PADX : PADX + CX] = along_ref[f] + added.reshape(ZS, CX, CY)
+            for z in range(ZS):
+                total = float(TAPS[R]) * wide[f, z, PADX - 8 : PADX + 72, :]
+                for k in range(1, R + 1):
+                    total = total + float(TAPS[R + k]) * (
+                        wide[f, z, PADX - 8 - k : PADX + 72 - k, :]
+                        + wide[f, z, PADX - 8 + k : PADX + 72 + k, :]
+                    )
+                smooth[f, z] = total
+        for ext in range(EXT):
+            rows = slice(ext * 8, ext * 8 + 8)
+            if len(members) == 2:
+                for a in range(2):
+                    block = smooth[members[0] : members[0] + 2, a * 8 : a * 8 + 8, rows, :]
+                    turned = block.reshape(128, 128).T
+                    for y in range(8):
+                        put(ext, a, chunk * 1024 + y * 128, turned[y * 16 : y * 16 + 16])
+            else:
+                turned = smooth[4, :, rows, :].reshape(128, 128).T
+                for m in range(4):
+                    even = turned[m * 32 : m * 32 + 16]
+                    odd = turned[m * 32 + 16 : m * 32 + 32]
+                    start = 2048 + m * 128
+                    put(ext, 0, start, jnp.where(first, even, pltpu.roll(odd, 64, 1)))
+                    put(ext, 1, start, jnp.where(first, pltpu.roll(even, 64, 1), odd))
+        deep = slice(chunk * 1024, min(chunk * 1024 + 1024, KIN))
+        for tile in range(3):
+            columns = slice(tile * 256, tile * 256 + 256)
+            part = dot(lhs[:, deep], weight_ref[deep, columns])
+            both[:, columns] = part if chunk == 0 else both[:, columns] + part
 
     for tile in range(3):
         columns = slice(tile * 256, tile * 256 + 256)
-        both = dot(lhs[...], weight_ref[:, columns])
-        lead = both[:64] + both[HI_ROWS : HI_ROWS + 64]
-        tail = both[256:HI_ROWS] + both[HI_ROWS + 64 :]
+        lead = both[:64, columns] + both[HI_ROWS : HI_ROWS + 64, columns]
+        tail = both[256:HI_ROWS, columns] + both[HI_ROWS + 64 :, columns]
         lead_hi, lead_lo = halves(lead)
         tail_hi, tail_lo = halves(tail)
-        mid[0:64] = lead_hi
-        mid[64:256] = both[64:256].astype(bf16)
-        mid[256:HI_ROWS] = tail_hi
-        mid[HI_ROWS : HI_ROWS + 64] = lead_lo
-        mid[HI_ROWS + 64 :] = tail_lo
-        out_ref[:, columns] = dot(order_ref[...], mid[...]).astype(bf16)
+        mid[0:64, columns] = lead_hi
+        mid[64:256, columns] = both[64:256, columns].astype(bf16)
+        mid[256:HI_ROWS, columns] = tail_hi
+        mid[HI_ROWS : HI_ROWS + 64, columns] = lead_lo
+        mid[HI_ROWS + 64 :, columns] = tail_lo
+    slots = dot(order_ref[...], mid[...]).astype(bf16)
+    out_ref[...] = slots.reshape(16 * SLOTS // 4, 4, D)
 
 
 def layer_norm(hidden):
@@ -278,7 +286,7 @@
 
 
 def x_kernel(slots_ref, sum_ref, qkv_ref, outw_ref, order_ref, out_ref, hidden, three, mixed):
-    hidden[...] = dot(sum_ref[...], slots_ref[...])
+    hidden[...] = dot(sum_ref[...], slots_ref[...].reshape(NXL * SLOTS, D))
     attend(hidden, qkv_ref, outw_ref, three, mixed)
     tokens = dot(order_ref[...], hidden[...].astype(bf16)).astype(bf16)
     out_ref[...] = tokens.reshape(128, 2, D)
@@ -323,7 +331,7 @@
             kernel,
             out_shape=out_shape,
             in_specs=[space] * len(operands),
-            out_specs=space,
+            out_specs=[space] * len(out_shape) if isinstance(out_shape, list) else space,
             scratch_shapes=scratch,
             compiler_params=pltpu.CompilerParams(vmem_limit_bytes=limit << 20),
             cost_estimate=pl.CostEstimate(flops=flops, bytes_accessed=size, transcendentals=0),
@@ -337,49 +345,52 @@
 
 
 def prepare(fields):
-    plane = (1, ZS + 2 * R, CX, CY)
-    strip = pl.BlockSpec((1, R, ZS * CX), lambda f: (f, 0, 0))
+    space = pl.BlockSpec(memory_space=pltpu.VMEM)
     return pl.pallas_call(
         prep_kernel,
-        grid=(NF,),
-        in_specs=[pl.BlockSpec(plane, lambda f: (f, 0, 0, 0))],
-        out_specs=[pl.BlockSpec((1, ZS, CX, CY), lambda f: (f, 0, 0, 0)), strip, strip],
+        in_specs=[pl.BlockSpec(memory_space=pltpu.HBM)],
+        out_specs=[space] * 3,
         out_shape=[
             like((NF, ZS, CX, CY), f32),
             like((NF, R, ZS * CX), f32),
             like((NF, R, ZS * CX), f32),
         ],
-        compiler_params=pltpu.CompilerParams(vmem_limit_bytes=8 << 20),
+        scratch_shapes=[
+            pltpu.VMEM((NF, ZS + 2 * R, CX, CY), f32),
+            pltpu.SemaphoreType.DMA((NF,)),
+        ],
+        compiler_params=pltpu.CompilerParams(vmem_limit_bytes=49 << 20),
     )(fields)
 
 
 def shards(fields, embed_weight, qkv_weight, out_weight, up_weight, down_weight):
-    band, side = band_tables()
     count = lax.axis_size("gy")
     smooth, upper, lower = prepare(fields)
     upper = lax.ppermute(upper, "gy", [(i, (i + 1) % count) for i in range(count)])
     lower = lax.ppermute(lower, "gy", [((i + 1) % count, i) for i in range(count)])
-    along = whole(band_kernel, like((NF, ZS, CX, CY), f32), [], 2 * 5120 * 256 * 256, 8)(
-        smooth, band
-    )
-    weight = whole(weight_kernel, like((KIN, D)), [], 2 * KIN * 256 * D, 8)(
-        embed_weight, weight_order()
-    )
+    along, weight = whole(
+        band_kernel,
+        [like((NF, ZS, CX, CY), f32), like((KIN, D))],
+        [],
+        2 * 5120 * 256 * 256 + 2 * KIN * 256 * D,
+        8,
+    )(smooth, embed_weight)
     slots = whole(
         embed_kernel,
-        like((16 * SLOTS, D)),
+        like((16 * SLOTS // 4, 4, D)),
         [
             pltpu.VMEM((NF, ZS, CX + 2 * PADX, CY), f32),
             pltpu.VMEM((NF, ZS, 80, CY), f32),
             pltpu.VMEM((ALL_ROWS, KIN), bf16),
-            pltpu.VMEM((ALL_ROWS, 256), bf16),
+            pltpu.VMEM((ALL_ROWS, D), f32),
+            pltpu.VMEM((ALL_ROWS, D), bf16),
         ],
         2 * ALL_ROWS * KIN * D,
-        14,
-    )(along, upper, lower, side, weight, message_order())
+        18,
+    )(along, upper, lower, side_table(), weight, message_order())
     slots = lax.all_to_all(
-        slots.reshape(NXL, SLOTS, D), "gx", split_axis=0, concat_axis=0, tiled=True
-    ).reshape(NXL * SLOTS, D)
+        slots.reshape(NXL, SLOTS // 4, 4, D), "gx", split_axis=0, concat_axis=0, tiled=True
+    ).reshape(NXL * SLOTS // 4, 4, D)
     attention = [
         pltpu.VMEM((TOK, D), f32),
         pltpu.VMEM((TOK, 3 * D), bf16),

time: 86.9 us -> 80.9 us (0.931)
  Pallas kernels: 26.5 us -> 21.9 us
  local copies, waits for them, and re-layouts: 3.1 us -> 0.08 us
  waiting for transfers between devices: 0.01 us -> 2.2 us
    pallas_call x6 -> x5, Pallas kernels: 25 us -> 19.1 us  [call(): pl.pallas_call(kernel, out_shape=out_shape, in_specs=[space] * len(operan...]
    unnamed x32 -> x28, local copies, waits for them, and re-layouts: 3.1 us -> 0.08 us
    ppermute x1, waiting for transfers between devices: 0.01 us -> 1.66 us  [shards(): lax.ppermute(lower, 'gy', [((i + 1) % count, i) for i in range(count)])]
    pallas_call x1, Pallas kernels: 1.52 us -> 2.83 us  [prepare(): pl.pallas_call(prep_kernel, in_specs=[pl.BlockSpec(memory_space=pltpu.HBM...]
    all_to_all x1, blocking collectives: 18.8 us -> 17.5 us  [shards(): lax.all_to_all(slots.reshape(NXL, SLOTS // 4, 4, D), 'gx', split_axis=0,...]
  transfers between devices with their start and end apart: 2 -> 2, of which waited for: 0 -> 2; matrix products, arithmetic and copies ran while one was open for 0% -> 0% of each run, Pallas kernels for 6% -> 2%
where the time goes in v3:
time: 80.9 us; the launch traced here: 80.7 us
  blocking collectives  50 us (62%)
  Pallas kernels  21.9 us (27%)
  starting transfers between devices  6.31 us (8%)
  waiting for transfers between devices  2.2 us (3%)
    pallas_call x5, Pallas kernels, call(): pl.pallas_call(kernel, out_shape=out_shape, in_specs=[space] * len(operan...  19.1 us
    all_to_all x1, blocking collectives, shards(): lax.all_to_all(tokens, ('gx', 'gy'), split_axis=0, concat_axis=0, tiled=T...  18.9 us
    all_to_all x1, blocking collectives, shards(): lax.all_to_all(slots.reshape(NXL, SLOTS // 4, 4, D), 'gx', split_axis=0,...  17.5 us
    all_to_all x1, blocking collectives, shards(): lax.all_to_all(tokens.reshape(8, 32, D), 'gy', split_axis=0, concat_axis=...  13.6 us
    ppermute x1, starting transfers between devices, shards(): lax.ppermute(upper, 'gy', [(i, (i + 1) % count) for i in range(count)])  4.03 us
    pallas_call x1, Pallas kernels, prepare(): pl.pallas_call(prep_kernel, in_specs=[pl.BlockSpec(memory_space=pltpu.HBM...  2.83 us
    ppermute x1, starting transfers between devices, shards(): lax.ppermute(lower, 'gy', [((i + 1) % count, i) for i in range(count)])  2.28 us
    ppermute x1, waiting for transfers between devices, shards(): lax.ppermute(lower, 'gy', [((i + 1) % count, i) for i in range(count)])  1.66 us
  transfers between devices with their start and end apart: 2, of which 2 were waited for; matrix products, arithmetic and copies ran while one was open for 0% of the time, Pallas kernels for 2%

profile of v3, /device:TPU:0, one launch (start us, length us, event | category | flops | bytes accessed | tf_op | source)
XLA Modules:
  0.0 80.7 jit_solution(8087525548910915250)
XLA Ops:
  0.0 2.8 %shard_map.127 = (f32[5,16,64,128]{3,2,1,0:T(8,128)S(1)}, f32[5,4,1024]{2,1,0:T(4,128)S(1)}, f32[5,4,1024]{2,1,0:T(4,128)S(1)}) custom-call(f32[5,24,64,128]{3,2,1,0:T(8,128)} %fields_ref.1), custom_call_target="tpu_custom_call" | custom-call | tf_op jit(solution)/shard_map/pallas_call | solution.py:349
  2.8 0.0 copy-start.3
  2.9 0.0 copy-start.9
  2.9 4.0 %collective-permute-start = (f32[5,4,1024]{2,1,0:T(4,128)S(1)}, f32[5,4,1024]{2,1,0:T(4,128)S(1)}, u32[]{:S(2)}, u32[]{:S(2)}) collective-permute-start(f32[5,4,1024]{2,1,0:T(4,128)S(1)} %get-tuple-element.12), channel_id=1, source_target_pairs={{0,1},{1,2},{2,3},{3,4},{4,5},{5,6},{6,7},{7,0},{8,9},{9,10},{10,1... | collective-permute-start | bytes 245768 | tf_op jit(solution)/shard_map/ppermute | solution.py:369
  6.9 2.3 %collective-permute-start.1 = (f32[5,4,1024]{2,1,0:T(4,128)S(1)}, f32[5,4,1024]{2,1,0:T(4,128)S(1)}, u32[]{:S(2)}, u32[]{:S(2)}) collective-permute-start(f32[5,4,1024]{2,1,0:T(4,128)S(1)} %get-tuple-element.13), channel_id=1, source_target_pairs={{1,0},{2,1},{3,2},{4,3},{5,4},{6,5},{7,6},{0,7},{9,8},{10,9},{11,1... | collective-permute-start | bytes 245768 | tf_op jit(solution)/shard_map/ppermute | solution.py:370
  9.2 1.9 %shard_map.128 = (f32[5,16,64,128]{3,2,1,0:T(8,128)S(1)}, bf16[2560,768]{1,0:T(8,128)(2,1)S(1)}) custom-call(f32[5,16,64,128]{3,2,1,0:T(8,128)S(1)} %get-tuple-element.10.smooth_ref, bf16[2560,768]{1,0:T(8,128)(2,1)S(1)} %copy-done.2), custom_call_target="tpu_custom_call" | custom-call | flops 1677721600 | bytes 6553600 | tf_op jit(solution)/shard_map/pallas_call | solution.py:330
  11.1 0.5 collective-permute-done.upper_ref
  11.6 1.7 %collective-permute-done.1.lower_ref = f32[5,4,1024]{2,1,0:T(4,128)S(1)} collective-permute-done((f32[5,4,1024]{2,1,0:T(4,128)S(1)}, f32[5,4,1024]{2,1,0:T(4,128)S(1)}, u32[]{:S(2)}, u32[]{:S(2)}) %collective-permute-start.1) | collective-permute-done | bytes 81952 | tf_op jit(solution)/shard_map/ppermute | solution.py:370
  13.3 0.0 copy-done.9
  13.3 0.0 copy-start.6
  13.3 0.0 slice-start
  13.3 0.0 slice-start.3
  13.3 5.5 %shard_map.129 = bf16[112,4,768]{2,1,0:T(4,128)(2,1)S(1)} custom-call(f32[5,16,64,128]{3,2,1,0:T(8,128)S(1)} %get-tuple-element.11.along_ref, f32[5,4,1024]{2,1,0:T(4,128)S(1)} %collective-permute-done.upper_ref, f32[5,4,1024]{2,1,0:T(4,128)S(1)} %collective-permute-done.1.lower_ref, bf16[32,128]{1,0:T(8,128)(2,1)S(1)} %copy-done.9, ...), custom_call_target="tpu_custom_call" | custom-call | flops 1761607680 | bytes 7127040 | tf_op jit(solution)/shard_map/pallas_call | solution.py:330
  18.8 0.0 slice-start.1
  18.8 0.0 copy-start.7
  18.8 0.0 copy-start.8
  18.9 17.5 %all_to_all.15 = bf16[16,7,4,768]{3,2,1,0:T(4,128)(2,1)S(1)} all-to-all(bf16[16,7,4,768]{3,2,1,0:T(4,128)(2,1)S(1)} %bitcast.10), channel_id=1, replica_groups=mesh['gx'=16,'gy'=8] {'gx'}, dimensions={0} | all-to-all | bytes 1376256 | tf_op jit(solution)/shard_map/all_to_all | solution.py:391
  36.4 0.0 copy-done.1
  36.4 3.0 %shard_map.130 = bf16[128,2,768]{2,1,0:T(2,128)(2,1)S(1)} custom-call(bf16[112,4,768]{2,1,0:T(4,128)(2,1)S(1)} %bitcast.9, bf16[256,448]{1,0:T(8,128)(2,1)S(1)} %copy-done.4, bf16[768,2304]{1,0:T(8,128)(2,1)S(1)} %copy-done, bf16[768,768]{1,0:T(8,128)(2,1)S(1)} %copy-done.1, bf16[256,256]{1,0:T(8,128)(2,1)S(1)} %copy-done.6), custom_call_target="tpu_custom_call" | custom-call | flops 1207959552 | bytes 5767168 | tf_op jit(solution)/shard_map/pallas_call | solution.py:330
  39.4 18.9 %all_to_all.16.tokens_ref = bf16[128,2,768]{2,1,0:T(2,128)(2,1)S(1)} all-to-all(bf16[128,2,768]{2,1,0:T(2,128)(2,1)S(1)} %shard_map.130), channel_id=1, replica_groups=mesh['gx'=16,'gy'=8] {'gx','gy'}, dimensions={0} | all-to-all | bytes 786432 | tf_op jit(solution)/shard_map/all_to_all | solution.py:402
  58.4 0.0 copy-start.5
  58.4 7.7 %shard_map.131 = bf16[256,768]{1,0:T(8,128)(2,1)S(1)} custom-call(bf16[128,2,768]{2,1,0:T(2,128)(2,1)S(1)} %all_to_all.16.tokens_ref, bf16[256,256]{1,0:T(8,128)(2,1)S(1)} %copy-done.8, bf16[768,2304]{1,0:T(8,128)(2,1)S(1)} %copy-done, bf16[768,768]{1,0:T(8,128)(2,1)S(1)} %copy-done.1, bf16[768,3072]{1,0:T(8,128)(2,1)S(1)} %bitcast.6, ...), custom_call_target="tpu_custom_call" | custom-call | flops 3623878656 | bytes 14811136 | tf_op jit(solution)/shard_map/pallas_call | solution.py:330
  66.1 13.6 %all_to_all.17 = bf16[8,32,768]{2,1,0:T(8,128)(2,1)S(1)} all-to-all(bf16[8,32,768]{2,1,0:T(8,128)(2,1)S(1)} %bitcast.12), channel_id=1, replica_groups=mesh['gx'=16,'gy'=8] {'gy'}, dimensions={0} | all-to-all | bytes 786432 | tf_op jit(solution)/shard_map/all_to_all | solution.py:412
  79.7 1.0 %shard_map.132 = bf16[256,768]{1,0:T(8,128)(2,1)} custom-call(bf16[256,768]{1,0:T(8,128)(2,1)S(1)} %bitcast.11, bf16[256,256]{1,0:T(8,128)(2,1)S(1)} %copy-done.5), custom_call_target="tpu_custom_call" | custom-call | flops 100663296 | bytes 524288 | tf_op jit(solution)/shard_map/pallas_call | solution.py:330
  (19 shorter events, 0.0 us)
Async XLA Ops:
  0.0 9.2 %copy-start.2 = (bf16[2560,768]{1,0:T(8,128)(2,1)S(1)}, bf16[2560,768]{1,0:T(8,128)(2,1)}, u32[]{:S(2)}) copy-start(bf16[2560,768]{1,0:T(8,128)(2,1)} %weight_ref.1) | copy-start | bytes 11796484
  2.8 10.5 %copy-start.3 = (bf16[448,448]{1,0:T(8,128)(2,1)S(1)}, bf16[448,448]{1,0:T(8,128)(2,1)}, u32[]{:S(2)}) copy-start(bf16[448,448]{1,0:T(8,128)(2,1)} %constant.15.clone.order_ref) | copy-start | bytes 1204228
  2.9 10.4 %copy-start.9 = (bf16[32,128]{1,0:T(8,128)(2,1)S(1)}, bf16[32,128]{1,0:T(8,128)(2,1)}, u32[]{:S(2)}) copy-start(bf16[32,128]{1,0:T(8,128)(2,1)} %constant.14.clone.side_ref) | copy-start | bytes 24580
  2.9 8.8 %collective-permute-start = (f32[5,4,1024]{2,1,0:T(4,128)S(1)}, f32[5,4,1024]{2,1,0:T(4,128)S(1)}, u32[]{:S(2)}, u32[]{:S(2)}) collective-permute-start(f32[5,4,1024]{2,1,0:T(4,128)S(1)} %get-tuple-element.12), channel_id=1, source_target_pairs={{0,1},{1,2},{2,3},{3,4},{4,5},{5,6},{6,7},{7,0},{8,9},{9,10},{10,1... | collective-permute-start | bytes 245768 | tf_op jit(solution)/shard_map/ppermute | solution.py:369
  6.9 6.4 %collective-permute-start.1 = (f32[5,4,1024]{2,1,0:T(4,128)S(1)}, f32[5,4,1024]{2,1,0:T(4,128)S(1)}, u32[]{:S(2)}, u32[]{:S(2)}) collective-permute-start(f32[5,4,1024]{2,1,0:T(4,128)S(1)} %get-tuple-element.13), channel_id=1, source_target_pairs={{1,0},{2,1},{3,2},{4,3},{5,4},{6,5},{7,6},{0,7},{9,8},{10,9},{11,1... | collective-permute-start | bytes 245768 | tf_op jit(solution)/shard_map/ppermute | solution.py:370
  9.2 27.2 %copy-start.1 = (bf16[768,768]{1,0:T(8,128)(2,1)S(1)}, bf16[768,768]{1,0:T(8,128)(2,1)}, u32[]{:S(2)}) copy-start(bf16[768,768]{1,0:T(8,128)(2,1)} %outw_ref.3) | copy-start | bytes 3538948
  9.2 49.1 %slice-start.2 = ((s8[4718592]{0:T(1024)(128)(4,1)}), s8[4194304]{0:T(1024)(128)(4,1)S(1)}, s32[]{:S(2)}) async-start(s8[4718592]{0:T(1024)(128)(4,1)} %bitcast.7), calls=%async_computation.5 | async-start | bytes 8388608
  13.3 23.1 %copy-start = (bf16[768,2304]{1,0:T(8,128)(2,1)S(1)}, bf16[768,2304]{1,0:T(8,128)(2,1)}, u32[]{:S(2)}) copy-start(bf16[768,2304]{1,0:T(8,128)(2,1)} %qkv_ref.3) | copy-start | bytes 10616836
  13.3 23.1 %copy-start.4 = (bf16[256,448]{1,0:T(8,128)(2,1)S(1)}, bf16[256,448]{1,0:T(8,128)(2,1)}, u32[]{:S(2)}) copy-start(bf16[256,448]{1,0:T(8,128)(2,1)} %constant.16.clone.sum_ref) | copy-start | bytes 688132
  13.3 23.1 %copy-start.6 = (bf16[256,256]{1,0:T(8,128)(2,1)S(1)}, bf16[256,256]{1,0:T(8,128)(2,1)}, u32[]{:S(2)}) copy-start(bf16[256,256]{1,0:T(8,128)(2,1)} %constant.17.clone.order_ref) | copy-start | bytes 393220
  13.3 45.0 %slice-start = ((s8[4718592]{0:T(1024)(128)(4,1)}), s8[4194304]{0:T(1024)(128)(4,1)S(1)}, s32[]{:S(2)}) async-start(s8[4718592]{0:T(1024)(128)(4,1)} %bitcast.5), calls=%async_computation.3 | async-start | bytes 8388608
  13.3 45.0 %slice-start.3 = ((s8[4718592]{0:T(1024)(128)(4,1)}), s8[524288]{0:T(1024)(128)(4,1)S(1)}, s32[]{:S(2)}) async-start(s8[4718592]{0:T(1024)(128)(4,1)} %bitcast.7), calls=%async_computation.6 | async-start | bytes 1048576
  18.8 39.5 %slice-start.1 = ((s8[4718592]{0:T(1024)(128)(4,1)}), s8[524288]{0:T(1024)(128)(4,1)S(1)}, s32[]{:S(2)}) async-start(s8[4718592]{0:T(1024)(128)(4,1)} %bitcast.5), calls=%async_computation.4 | async-start | bytes 1048576
  18.8 39.5 %copy-start.7 = (bf16[256,256]{1,0:T(8,128)(2,1)S(1)}, bf16[256,256]{1,0:T(8,128)(2,1)}, u32[]{:S(2)}) copy-start(bf16[256,256]{1,0:T(8,128)(2,1)} %constant.19.clone.order_ref) | copy-start | bytes 393220
  18.8 39.5 %copy-start.8 = (bf16[256,256]{1,0:T(8,128)(2,1)S(1)}, bf16[256,256]{1,0:T(8,128)(2,1)}, u32[]{:S(2)}) copy-start(bf16[256,256]{1,0:T(8,128)(2,1)} %constant.18.clone.split_ref) | copy-start | bytes 393220
  58.4 21.3 %copy-start.5 = (bf16[256,256]{1,0:T(8,128)(2,1)S(1)}, bf16[256,256]{1,0:T(8,128)(2,1)}, u32[]{:S(2)}) copy-start(bf16[256,256]{1,0:T(8,128)(2,1)} %constant.20.clone.order_ref) | copy-start | bytes 393220

commit v4 on v3

--- a/solution.py
+++ b/solution.py
@@ -74,6 +74,25 @@
     return jnp.concatenate([left, right], 1).astype(bf16)
 
 
+def strip_tables():
+    inside = np.zeros((128, 128), np.float32)
+    beyond = np.zeros((512, 128), np.float32)
+    for x in range(CX):
+        for k in range(-R, R + 1):
+            if 0 <= x + k < CX:
+                for z in range(2):
+                    inside[z * 64 + x, z * 64 + x + k] = TAPS[R + k]
+            else:
+                place = x + k + 8 if x + k < 0 else x + k - 56
+                for z in range(8):
+                    beyond[z * 64 + x, z * 16 + place] = TAPS[R + k]
+    tables = []
+    for table in (inside, beyond):
+        high, low = split_np(table)
+        tables.append(np.concatenate([high, high, low], 0))
+    return tables
+
+
 def weight_order():
     row = lax.broadcasted_iota(jnp.int32, (256, 256), 0)
     column = lax.broadcasted_iota(jnp.int32, (256, 256), 1)
@@ -129,6 +148,11 @@
     return lax.dot_general(left, right, (((1,), (0,)), ((), ())), preferred_element_type=f32)
 
 
+def dot_split(left, table):
+    high, low = halves(left)
+    return dot(jnp.concatenate([high, low, high], 1), table)
+
+
 def dot_t(left, right):
     return lax.dot_general(left, right, (((1,), (1,)), ((), ())), preferred_element_type=f32)
 
@@ -144,6 +168,9 @@
     ]
     for copy in copies:
         copy.start()
+    zero = jnp.zeros((NF, ZS, PADX, CY), f32)
+    smooth_ref[:, :, 0:PADX] = zero
+    smooth_ref[:, :, PADX + CX :] = zero
     for f in range(NF):
         copies[f].wait()
         for tile in range(CX // 8):
@@ -153,22 +180,31 @@
                 total = float(TAPS[R]) * plane[z + R]
                 for k in range(1, R + 1):
                     total = total + float(TAPS[R + k]) * (plane[z + R - k] + plane[z + R + k])
-                smooth_ref[f, z, rows, :] = total
+                smooth_ref[f, z, PADX + tile * 8 : PADX + tile * 8 + 8, :] = total
         for pair in range(ZS // 2):
-            turned = smooth_ref[f, 2 * pair : 2 * pair + 2].reshape(128, 128).T
+            block = smooth_ref[f, 2 * pair : 2 * pair + 2, PADX : PADX + CX]
+            turned = block.reshape(128, 128).T
             lower_ref[f, :, pair * 128 : pair * 128 + 128] = turned[:R]
             upper_ref[f, :, pair * 128 : pair * 128 + 128] = turned[CY - R :]
 
 
-def band_kernel(smooth_ref, weight_ref, along_ref, out_ref):
+def band_kernel(smooth_ref, weight_ref, along_ref, out_ref, across):
     band = band_table()
     order = weight_order()
     for f in range(NF):
+        for z in range(ZS):
+            total = float(TAPS[R]) * smooth_ref[f, z, PADX - 8 : PADX + 72, :]
+            for k in range(1, R + 1):
+                total = total + float(TAPS[R + k]) * (
+                    smooth_ref[f, z, PADX - 8 - k : PADX + 72 - k, :]
+                    + smooth_ref[f, z, PADX - 8 + k : PADX + 72 + k, :]
+                )
+            across[f, z] = total
         for part in range(4):
             planes = slice(part * 4, part * 4 + 4)
-            high, low = halves(smooth_ref[f, planes].reshape(256, CY))
+            high, low = halves(across[f, planes].reshape(320, CY))
             both = dot(jnp.concatenate([high, low], 1), band)
-            along_ref[f, planes] = (both[:, :CY] + both[:, CY:]).reshape(4, CX, CY)
+            along_ref[f, planes] = (both[:, :CY] + both[:, CY:]).reshape(4, 80, CY)
         for tile in (2 * f, 2 * f + 1):
             turned = dot(order, weight_ref[tile * 256 : tile * 256 + 256, :]).astype(bf16)
             for y in range(8):
@@ -180,10 +216,26 @@
 
 
 def embed_kernel(
-    along_ref, upper_ref, lower_ref, side_ref, weight_ref, order_ref, out_ref, wide, smooth, lhs, both, mid
+    along_ref,
+    upper_ref,
+    lower_ref,
+    inside_ref,
+    beyond_ref,
+    side_ref,
+    weight_ref,
+    order_ref,
+    out_ref,
+    smooth,
+    lhs,
+    both,
+    mid,
 ):
     side = side_ref[...]
-    zero = jnp.zeros((ZS, PADX, CY), f32)
+    strips = [jnp.concatenate([upper_ref[f], lower_ref[f]], 0) for f in range(NF)]
+    within = [strips[f][:, p * 128 : p * 128 + 128] for f in range(NF) for p in range(ZS // 2)]
+    within = dot_split(jnp.concatenate(within, 0), inside_ref[...])
+    ends = [strips[f][:, h * 512 : h * 512 + 512] for f in range(NF) for h in range(2)]
+    ends = dot_split(jnp.concatenate(ends, 0), beyond_ref[...])
     lane = lax.broadcasted_iota(jnp.int32, (16, 128), 1)
     first = lane < 64
 
@@ -197,21 +249,17 @@
 
     for chunk, members in enumerate(((0, 1), (2, 3), (4,))):
         for f in members:
-            wide[f, :, 0:PADX] = zero
-            wide[f, :, PADX + CX :] = zero
-            cells = jnp.concatenate([upper_ref[f], lower_ref[f]], 0)
+            parts = [within[(f * 8 + p) * 8 : (f * 8 + p) * 8 + 8] for p in range(ZS // 2)]
+            parts += [ends[(f * 2 + h) * 8 : (f * 2 + h) * 8 + 8] for h in range(2)]
+            cells = jnp.concatenate(parts, 1)
             high = cells.astype(bf16).astype(f32)
             stacked = jnp.concatenate([high, cells - high, high, jnp.zeros_like(high)], 0)
             added = dot(stacked.T.astype(bf16), side)
-            wide[f, :, PADX : PADX + CX] = along_ref[f] + added.reshape(ZS, CX, CY)
-            for z in range(ZS):
-                total = float(TAPS[R]) * wide[f, z, PADX - 8 : PADX + 72, :]
-                for k in range(1, R + 1):
-                    total = total + float(TAPS[R + k]) * (
-                        wide[f, z, PADX - 8 - k : PADX + 72 - k, :]
-                        + wide[f, z, PADX - 8 + k : PADX + 72 + k, :]
-                    )
-                smooth[f, z] = total
+            middle = added[: ZS * CX].reshape(ZS, CX, CY)
+            outer = added[ZS * CX :].reshape(ZS, 16, CY)
+            smooth[f, :, 0:8] = along_ref[f, :, 0:8] + outer[:, :8]
+            smooth[f, :, 8:72] = along_ref[f, :, 8:72] + middle
+            smooth[f, :, 72:80] = along_ref[f, :, 72:80] + outer[:, 8:]
         for ext in range(EXT):
             rows = slice(ext * 8, ext * 8 + 8)
             if len(members) == 2:
@@ -351,7 +399,7 @@
         in_specs=[pl.BlockSpec(memory_space=pltpu.HBM)],
         out_specs=[space] * 3,
         out_shape=[
-            like((NF, ZS, CX, CY), f32),
+            like((NF, ZS, CX + 2 * PADX, CY), f32),
             like((NF, R, ZS * CX), f32),
             like((NF, R, ZS * CX), f32),
         ],
@@ -370,24 +418,23 @@
     lower = lax.ppermute(lower, "gy", [((i + 1) % count, i) for i in range(count)])
     along, weight = whole(
         band_kernel,
-        [like((NF, ZS, CX, CY), f32), like((KIN, D))],
-        [],
-        2 * 5120 * 256 * 256 + 2 * KIN * 256 * D,
+        [like((NF, ZS, 80, CY), f32), like((KIN, D))],
+        [pltpu.VMEM((NF, ZS, 80, CY), f32)],
+        2 * 6400 * 256 * 256 + 2 * KIN * 256 * D,
         8,
     )(smooth, embed_weight)
     slots = whole(
         embed_kernel,
         like((16 * SLOTS // 4, 4, D)),
         [
-            pltpu.VMEM((NF, ZS, CX + 2 * PADX, CY), f32),
             pltpu.VMEM((NF, ZS, 80, CY), f32),
             pltpu.VMEM((ALL_ROWS, KIN), bf16),
             pltpu.VMEM((ALL_ROWS, D), f32),
             pltpu.VMEM((ALL_ROWS, D), bf16),
         ],
         2 * ALL_ROWS * KIN * D,
-        18,
-    )(along, upper, lower, side_table(), weight, message_order())
+        14,
+    )(along, upper, lower, *strip_tables(), side_table(), weight, message_order())
     slots = lax.all_to_all(
         slots.reshape(NXL, SLOTS // 4, 4, D), "gx", split_axis=0, concat_axis=0, tiled=True
     ).reshape(NXL * SLOTS // 4, 4, D)

time: 80.9 us -> 79.6 us (0.984)
  waiting for transfers between devices: 2.2 us -> 1.17 us
  transfers between devices with their start and end apart: 2 -> 2, of which waited for: 2 -> 1; matrix products, arithmetic and copies ran while one was open for 0% -> 0% of each run, Pallas kernels for 2% -> 4%
where the time goes in v4:
time: 79.6 us; the launch traced here: 79.4 us
  blocking collectives  50 us (63%)
  Pallas kernels  21.6 us (27%)
  starting transfers between devices  6.32 us (8%)
  waiting for transfers between devices  1.17 us (1%)
    all_to_all x1, blocking collectives, shards(): lax.all_to_all(tokens, ('gx', 'gy'), split_axis=0, concat_axis=0, tiled=T...  18.9 us
    pallas_call x5, Pallas kernels, call(): pl.pallas_call(kernel, out_shape=out_shape, in_specs=[space] * len(operan...  18.8 us
    all_to_all x1, blocking collectives, shards(): lax.all_to_all(slots.reshape(NXL, SLOTS // 4, 4, D), 'gx', split_axis=0,...  17.5 us
    all_to_all x1, blocking collectives, shards(): lax.all_to_all(tokens.reshape(8, 32, D), 'gy', split_axis=0, concat_axis=...  13.6 us
    ppermute x1, starting transfers between devices, shards(): lax.ppermute(upper, 'gy', [(i, (i + 1) % count) for i in range(count)])  4.05 us
    pallas_call x1, Pallas kernels, prepare(): pl.pallas_call(prep_kernel, in_specs=[pl.BlockSpec(memory_space=pltpu.HBM...  2.84 us
    ppermute x1, starting transfers between devices, shards(): lax.ppermute(lower, 'gy', [((i + 1) % count, i) for i in range(count)])  2.28 us
  transfers between devices with their start and end apart: 2, of which 1 were waited for; matrix products, arithmetic and copies ran while one was open for 0% of the time, Pallas kernels for 4%

profile of v4, /device:TPU:0, one launch (start us, length us, event | category | flops | bytes accessed | tf_op | source)
XLA Modules:
  0.0 79.4 jit_solution(10234451204126900469)
XLA Ops:
  0.0 2.8 %shard_map.145 = (f32[5,16,96,128]{3,2,1,0:T(8,128)S(1)}, f32[5,4,1024]{2,1,0:T(4,128)S(1)}, f32[5,4,1024]{2,1,0:T(4,128)S(1)}) custom-call(f32[5,24,64,128]{3,2,1,0:T(8,128)} %fields_ref.1), custom_call_target="tpu_custom_call" | custom-call | tf_op jit(solution)/shard_map/pallas_call | solution.py:397
  2.9 4.0 %collective-permute-start = (f32[5,4,1024]{2,1,0:T(4,128)S(1)}, f32[5,4,1024]{2,1,0:T(4,128)S(1)}, u32[]{:S(2)}, u32[]{:S(2)}) collective-permute-start(f32[5,4,1024]{2,1,0:T(4,128)S(1)} %get-tuple-element.12), channel_id=1, source_target_pairs={{0,1},{1,2},{2,3},{3,4},{4,5},{5,6},{6,7},{7,0},{8,9},{9,10},{10,1... | collective-permute-start | bytes 245768 | tf_op jit(solution)/shard_map/ppermute | solution.py:417
  6.9 2.3 %collective-permute-start.1 = (f32[5,4,1024]{2,1,0:T(4,128)S(1)}, f32[5,4,1024]{2,1,0:T(4,128)S(1)}, u32[]{:S(2)}, u32[]{:S(2)}) collective-permute-start(f32[5,4,1024]{2,1,0:T(4,128)S(1)} %get-tuple-element.13), channel_id=1, source_target_pairs={{1,0},{2,1},{3,2},{4,3},{5,4},{6,5},{7,6},{0,7},{9,8},{10,9},{11,1... | collective-permute-start | bytes 245768 | tf_op jit(solution)/shard_map/ppermute | solution.py:418
  9.2 2.9 %shard_map.146 = (f32[5,16,80,128]{3,2,1,0:T(8,128)S(1)}, bf16[2560,768]{1,0:T(8,128)(2,1)S(1)}) custom-call(f32[5,16,96,128]{3,2,1,0:T(8,128)S(1)} %get-tuple-element.10.smooth_ref, bf16[2560,768]{1,0:T(8,128)(2,1)S(1)} %copy-done.2), custom_call_target="tpu_custom_call" | custom-call | flops 1845493760 | bytes 7864320 | tf_op jit(solution)/shard_map/pallas_call | solution.py:378
  12.1 0.0 collective-permute-done.upper_ref
  12.1 1.2 %collective-permute-done.1.lower_ref = f32[5,4,1024]{2,1,0:T(4,128)S(1)} collective-permute-done((f32[5,4,1024]{2,1,0:T(4,128)S(1)}, f32[5,4,1024]{2,1,0:T(4,128)S(1)}, u32[]{:S(2)}, u32[]{:S(2)}) %collective-permute-start.1) | collective-permute-done | bytes 81952 | tf_op jit(solution)/shard_map/ppermute | solution.py:418
  13.3 0.0 copy-done.4
  13.3 0.0 copy-start
  13.3 0.0 copy-start.1
  13.3 0.0 copy-start.5
  13.4 0.0 copy-start.7
  13.4 0.0 slice-start.1
  13.4 0.0 slice-start.3
  13.4 4.2 %shard_map.147 = bf16[112,4,768]{2,1,0:T(4,128)(2,1)S(1)} custom-call(f32[5,16,80,128]{3,2,1,0:T(8,128)S(1)} %get-tuple-element.11.along_ref, f32[5,4,1024]{2,1,0:T(4,128)S(1)} %collective-permute-done.upper_ref, f32[5,4,1024]{2,1,0:T(4,128)S(1)} %collective-permute-done.1.lower_ref, bf16[384,128]{1,0:T(8,128)(2,1)S(1)} %copy-done.10, ...), custom_call_target="tpu_custom_call" | custom-call | flops 1761607680 | bytes 8273920 | tf_op jit(solution)/shard_map/pallas_call | solution.py:378
  17.6 0.0 copy-start.8
  17.6 0.0 copy-start.9
  17.6 17.5 %all_to_all.15 = bf16[16,7,4,768]{3,2,1,0:T(4,128)(2,1)S(1)} all-to-all(bf16[16,7,4,768]{3,2,1,0:T(4,128)(2,1)S(1)} %bitcast.10), channel_id=1, replica_groups=mesh['gx'=16,'gy'=8] {'gx'}, dimensions={0} | all-to-all | bytes 1376256 | tf_op jit(solution)/shard_map/all_to_all | solution.py:438
  35.1 0.0 copy-done.1
  35.2 3.0 %shard_map.148 = bf16[128,2,768]{2,1,0:T(2,128)(2,1)S(1)} custom-call(bf16[112,4,768]{2,1,0:T(4,128)(2,1)S(1)} %bitcast.9, bf16[256,448]{1,0:T(8,128)(2,1)S(1)} %copy-done.5, bf16[768,2304]{1,0:T(8,128)(2,1)S(1)} %copy-done, bf16[768,768]{1,0:T(8,128)(2,1)S(1)} %copy-done.1, bf16[256,256]{1,0:T(8,128)(2,1)S(1)} %copy-done.7), custom_call_target="tpu_custom_call" | custom-call | flops 1207959552 | bytes 5767168 | tf_op jit(solution)/shard_map/pallas_call | solution.py:378
  38.1 18.9 %all_to_all.16.tokens_ref = bf16[128,2,768]{2,1,0:T(2,128)(2,1)S(1)} all-to-all(bf16[128,2,768]{2,1,0:T(2,128)(2,1)S(1)} %shard_map.148), channel_id=1, replica_groups=mesh['gx'=16,'gy'=8] {'gx','gy'}, dimensions={0} | all-to-all | bytes 786432 | tf_op jit(solution)/shard_map/all_to_all | solution.py:449
  57.1 0.0 copy-start.6
  57.1 7.7 %shard_map.149 = bf16[256,768]{1,0:T(8,128)(2,1)S(1)} custom-call(bf16[128,2,768]{2,1,0:T(2,128)(2,1)S(1)} %all_to_all.16.tokens_ref, bf16[256,256]{1,0:T(8,128)(2,1)S(1)} %copy-done.9, bf16[768,2304]{1,0:T(8,128)(2,1)S(1)} %copy-done, bf16[768,768]{1,0:T(8,128)(2,1)S(1)} %copy-done.1, bf16[768,3072]{1,0:T(8,128)(2,1)S(1)} %bitcast.6, ...), custom_call_target="tpu_custom_call" | custom-call | flops 3623878656 | bytes 14811136 | tf_op jit(solution)/shard_map/pallas_call | solution.py:378
  64.8 13.6 %all_to_all.17 = bf16[8,32,768]{2,1,0:T(8,128)(2,1)S(1)} all-to-all(bf16[8,32,768]{2,1,0:T(8,128)(2,1)S(1)} %bitcast.12), channel_id=1, replica_groups=mesh['gx'=16,'gy'=8] {'gy'}, dimensions={0} | all-to-all | bytes 786432 | tf_op jit(solution)/shard_map/all_to_all | solution.py:459
  78.4 1.0 %shard_map.150 = bf16[256,768]{1,0:T(8,128)(2,1)} custom-call(bf16[256,768]{1,0:T(8,128)(2,1)S(1)} %bitcast.11, bf16[256,256]{1,0:T(8,128)(2,1)S(1)} %copy-done.6), custom_call_target="tpu_custom_call" | custom-call | flops 100663296 | bytes 524288 | tf_op jit(solution)/shard_map/pallas_call | solution.py:378
  (23 shorter events, 0.0 us)
Async XLA Ops:
  0.0 9.2 %copy-start.2 = (bf16[2560,768]{1,0:T(8,128)(2,1)S(1)}, bf16[2560,768]{1,0:T(8,128)(2,1)}, u32[]{:S(2)}) copy-start(bf16[2560,768]{1,0:T(8,128)(2,1)} %weight_ref.1) | copy-start | bytes 11796484
  0.0 13.3 %copy-start.3 = (bf16[448,448]{1,0:T(8,128)(2,1)S(1)}, bf16[448,448]{1,0:T(8,128)(2,1)}, u32[]{:S(2)}) copy-start(bf16[448,448]{1,0:T(8,128)(2,1)} %constant.21.clone.order_ref) | copy-start | bytes 1204228
  0.0 13.3 %copy-start.4 = (bf16[1536,128]{1,0:T(8,128)(2,1)S(1)}, bf16[1536,128]{1,0:T(8,128)(2,1)}, u32[]{:S(2)}) copy-start(bf16[1536,128]{1,0:T(8,128)(2,1)} %constant.19.clone.beyond_ref) | copy-start | bytes 1179652
  0.0 13.3 %copy-start.10 = (bf16[384,128]{1,0:T(8,128)(2,1)S(1)}, bf16[384,128]{1,0:T(8,128)(2,1)}, u32[]{:S(2)}) copy-start(bf16[384,128]{1,0:T(8,128)(2,1)} %constant.18.clone.inside_ref) | copy-start | bytes 294916
  0.0 13.3 %copy-start.11 = (bf16[32,128]{1,0:T(8,128)(2,1)S(1)}, bf16[32,128]{1,0:T(8,128)(2,1)}, u32[]{:S(2)}) copy-start(bf16[32,128]{1,0:T(8,128)(2,1)} %constant.20.clone.side_ref) | copy-start | bytes 24580
  2.9 9.3 %collective-permute-start = (f32[5,4,1024]{2,1,0:T(4,128)S(1)}, f32[5,4,1024]{2,1,0:T(4,128)S(1)}, u32[]{:S(2)}, u32[]{:S(2)}) collective-permute-start(f32[5,4,1024]{2,1,0:T(4,128)S(1)} %get-tuple-element.12), channel_id=1, source_target_pairs={{0,1},{1,2},{2,3},{3,4},{4,5},{5,6},{6,7},{7,0},{8,9},{9,10},{10,1... | collective-permute-start | bytes 245768 | tf_op jit(solution)/shard_map/ppermute | solution.py:417
  6.9 6.4 %collective-permute-start.1 = (f32[5,4,1024]{2,1,0:T(4,128)S(1)}, f32[5,4,1024]{2,1,0:T(4,128)S(1)}, u32[]{:S(2)}, u32[]{:S(2)}) collective-permute-start(f32[5,4,1024]{2,1,0:T(4,128)S(1)} %get-tuple-element.13), channel_id=1, source_target_pairs={{1,0},{2,1},{3,2},{4,3},{5,4},{6,5},{7,6},{0,7},{9,8},{10,9},{11,1... | collective-permute-start | bytes 245768 | tf_op jit(solution)/shard_map/ppermute | solution.py:418
  9.2 47.8 %slice-start = ((s8[4718592]{0:T(1024)(128)(4,1)}), s8[4194304]{0:T(1024)(128)(4,1)S(1)}, s32[]{:S(2)}) async-start(s8[4718592]{0:T(1024)(128)(4,1)} %bitcast.5), calls=%async_computation.3 | async-start | bytes 8388608
  9.2 47.8 %slice-start.2 = ((s8[4718592]{0:T(1024)(128)(4,1)}), s8[4194304]{0:T(1024)(128)(4,1)S(1)}, s32[]{:S(2)}) async-start(s8[4718592]{0:T(1024)(128)(4,1)} %bitcast.7), calls=%async_computation.5 | async-start | bytes 8388608
  13.3 21.8 %copy-start = (bf16[768,2304]{1,0:T(8,128)(2,1)S(1)}, bf16[768,2304]{1,0:T(8,128)(2,1)}, u32[]{:S(2)}) copy-start(bf16[768,2304]{1,0:T(8,128)(2,1)} %qkv_ref.3) | copy-start | bytes 10616836
  13.3 21.8 %copy-start.1 = (bf16[768,768]{1,0:T(8,128)(2,1)S(1)}, bf16[768,768]{1,0:T(8,128)(2,1)}, u32[]{:S(2)}) copy-start(bf16[768,768]{1,0:T(8,128)(2,1)} %outw_ref.3) | copy-start | bytes 3538948
  13.3 21.8 %copy-start.5 = (bf16[256,448]{1,0:T(8,128)(2,1)S(1)}, bf16[256,448]{1,0:T(8,128)(2,1)}, u32[]{:S(2)}) copy-start(bf16[256,448]{1,0:T(8,128)(2,1)} %constant.22.clone.sum_ref) | copy-start | bytes 688132
  13.4 21.8 %copy-start.7 = (bf16[256,256]{1,0:T(8,128)(2,1)S(1)}, bf16[256,256]{1,0:T(8,128)(2,1)}, u32[]{:S(2)}) copy-start(bf16[256,256]{1,0:T(8,128)(2,1)} %constant.23.clone.order_ref) | copy-start | bytes 393220
  13.4 43.6 %slice-start.1 = ((s8[4718592]{0:T(1024)(128)(4,1)}), s8[524288]{0:T(1024)(128)(4,1)S(1)}, s32[]{:S(2)}) async-start(s8[4718592]{0:T(1024)(128)(4,1)} %bitcast.5), calls=%async_computation.4 | async-start | bytes 1048576
  13.4 43.6 %slice-start.3 = ((s8[4718592]{0:T(1024)(128)(4,1)}), s8[524288]{0:T(1024)(128)(4,1)S(1)}, s32[]{:S(2)}) async-start(s8[4718592]{0:T(1024)(128)(4,1)} %bitcast.7), calls=%async_computation.6 | async-start | bytes 1048576
  17.6 39.5 %copy-start.8 = (bf16[256,256]{1,0:T(8,128)(2,1)S(1)}, bf16[256,256]{1,0:T(8,128)(2,1)}, u32[]{:S(2)}) copy-start(bf16[256,256]{1,0:T(8,128)(2,1)} %constant.25.clone.order_ref) | copy-start | bytes 393220
  17.6 39.5 %copy-start.9 = (bf16[256,256]{1,0:T(8,128)(2,1)S(1)}, bf16[256,256]{1,0:T(8,128)(2,1)}, u32[]{:S(2)}) copy-start(bf16[256,256]{1,0:T(8,128)(2,1)} %constant.24.clone.split_ref) | copy-start | bytes 393220
  57.1 21.3 %copy-start.6 = (bf16[256,256]{1,0:T(8,128)(2,1)S(1)}, bf16[256,256]{1,0:T(8,128)(2,1)}, u32[]{:S(2)}) copy-start(bf16[256,256]{1,0:T(8,128)(2,1)} %constant.26.clone.order_ref) | copy-start | bytes 393220

commit v5 on v3

--- a/solution.py
+++ b/solution.py
@@ -49,16 +49,6 @@
     return high, low
 
 
-def side_table():
-    wide = np.zeros((CY + 2 * R, CY), np.float32)
-    for out in range(CY):
-        column = (out % 8) * 16 + out // 8
-        for k in range(2 * R + 1):
-            wide[out + k, column] = TAPS[k]
-    high, low = split_np(np.concatenate([wide[:R], wide[R + CY :]], 0))
-    return np.concatenate([high, high, low, np.zeros_like(high)], 0)
-
-
 def band_table():
     row = lax.broadcasted_iota(jnp.int32, (CY, CY), 0)
     column = lax.broadcasted_iota(jnp.int32, (CY, CY), 1)
@@ -74,6 +64,17 @@
     return jnp.concatenate([left, right], 1).astype(bf16)
 
 
+def strip_table():
+    table = np.zeros((384, 128), np.float32)
+    for group in range(16):
+        for x in range(8):
+            for k in range(-R, R + 1):
+                source = x + k + 8
+                table[source // 8 * 128 + group * 8 + source % 8, group * 8 + x] = TAPS[R + k]
+    high, low = split_np(table)
+    return np.concatenate([high, high, low], 0)
+
+
 def weight_order():
     row = lax.broadcasted_iota(jnp.int32, (256, 256), 0)
     column = lax.broadcasted_iota(jnp.int32, (256, 256), 1)
@@ -96,7 +97,7 @@
     low = {ext: 2 * EXT + 2 * n for n, ext in enumerate(BOUND)}
 
     def source(row):
-        a, i, c = row // 128, row // 8 % 16, row % 8
+        a, i, c = row // 16 % 2, row // 32 * 2 + row // 8 % 2, row % 8
         found = [i * SLOTS + (c + 1) * 2 + a]
         if c == 0:
             left = (i - 1) % NXL * SLOTS
@@ -110,15 +111,11 @@
 
 
 def interleave():
-    return permutation(TOK, TOK, lambda r: [(r % 2) * 128 + r // 2])
+    return permutation(TOK, TOK, lambda r: [r // 32 * 32 + r % 2 * 16 + r // 2 % 16])
 
 
 def separate():
-    return permutation(TOK, TOK, lambda r: [(r % 128) * 2 + r // 128])
-
-
-def to_owners():
-    return permutation(TOK, TOK, lambda r: [(r // 16 % 2) * 128 + (r % 16) * 8 + r // 32])
+    return permutation(TOK, TOK, lambda r: [((r % 16) * 8 + r // 32) * 2 + r // 16 % 2])
 
 
 def to_home():
@@ -127,6 +124,11 @@
 
 def dot(left, right):
     return lax.dot_general(left, right, (((1,), (0,)), ((), ())), preferred_element_type=f32)
+
+
+def dot_split(left, table):
+    high, low = halves(left)
+    return dot(jnp.concatenate([high, low, high], 1), table)
 
 
 def dot_t(left, right):
@@ -144,6 +146,15 @@
     ]
     for copy in copies:
         copy.start()
+    zero = jnp.zeros((NF, ZS, PADX, CY), f32)
+    smooth_ref[:, :, 0:PADX] = zero
+    smooth_ref[:, :, PADX + CX :] = zero
+
+    def strip(index, block):
+        turned = block.reshape(128, 128).T
+        lower_ref[index] = turned[:R]
+        upper_ref[index] = turned[CY - R :]
+
     for f in range(NF):
         copies[f].wait()
         for tile in range(CX // 8):
@@ -153,22 +164,39 @@
                 total = float(TAPS[R]) * plane[z + R]
                 for k in range(1, R + 1):
                     total = total + float(TAPS[R + k]) * (plane[z + R - k] + plane[z + R + k])
-                smooth_ref[f, z, rows, :] = total
-        for pair in range(ZS // 2):
-            turned = smooth_ref[f, 2 * pair : 2 * pair + 2].reshape(128, 128).T
-            lower_ref[f, :, pair * 128 : pair * 128 + 128] = turned[:R]
-            upper_ref[f, :, pair * 128 : pair * 128 + 128] = turned[CY - R :]
-
-
-def band_kernel(smooth_ref, weight_ref, along_ref, out_ref):
+                smooth_ref[f, z, PADX + tile * 8 : PADX + tile * 8 + 8, :] = total
+        if f % 2 == 1:
+            for a in range(2):
+                for c in range(8):
+                    rows = slice(PADX + c * 8, PADX + c * 8 + 8)
+                    block = smooth_ref[f - 1 : f + 1, a * 8 : a * 8 + 8, rows, :]
+                    strip((f // 2 * 2 + a) * 8 + c, block)
+    for c in range(8):
+        strip(32 + c, smooth_ref[NF - 1, :, PADX + c * 8 : PADX + c * 8 + 8, :])
+
+
+def main_kernel(smooth_ref, weight_ref, total_ref, edge_ref, order_ref, across, along, lhs, both):
     band = band_table()
     order = weight_order()
-    for f in range(NF):
+    first = lax.broadcasted_iota(jnp.int32, (16, 128), 1) < 64
+    edge_ref[...] = jnp.zeros_like(edge_ref)
+
+    def filtered(f):
+        for z in range(ZS):
+            total = float(TAPS[R]) * smooth_ref[f, z, PADX - 8 : PADX + 72, :]
+            for k in range(1, R + 1):
+                total = total + float(TAPS[R + k]) * (
+                    smooth_ref[f, z, PADX - 8 - k : PADX + 72 - k, :]
+                    + smooth_ref[f, z, PADX - 8 + k : PADX + 72 + k, :]
+                )
+            across[f, z] = total
         for part in range(4):
             planes = slice(part * 4, part * 4 + 4)
-            high, low = halves(smooth_ref[f, planes].reshape(256, CY))
-            both = dot(jnp.concatenate([high, low], 1), band)
-            along_ref[f, planes] = (both[:, :CY] + both[:, CY:]).reshape(4, CX, CY)
+            high, low = halves(across[f, planes].reshape(320, CY))
+            pair = dot(jnp.concatenate([high, low], 1), band)
+            along[f, planes] = (pair[:, :CY] + pair[:, CY:]).reshape(4, 80, CY)
+
+    def reordered(f):
         for tile in (2 * f, 2 * f + 1):
             turned = dot(order, weight_ref[tile * 256 : tile * 256 + 256, :]).astype(bf16)
             for y in range(8):
@@ -176,75 +204,132 @@
                     start = tile // 4 * 1024 + y * 128 + tile % 4 * 32
                 else:
                     start = 2048 + y * 64 + (tile - 8) * 32
-                out_ref[start : start + 32, :] = turned[y * 32 : y * 32 + 32]
-
-
-def embed_kernel(
-    along_ref, upper_ref, lower_ref, side_ref, weight_ref, order_ref, out_ref, wide, smooth, lhs, both, mid
-):
-    side = side_ref[...]
-    zero = jnp.zeros((ZS, PADX, CY), f32)
-    lane = lax.broadcasted_iota(jnp.int32, (16, 128), 1)
-    first = lane < 64
-
-    def put(ext, a, start, values):
-        high, low = halves(values)
+                order_ref[start : start + 32, :] = turned[y * 32 : y * 32 + 32]
+
+    def put(ext, a, start, side, place, values):
+        high = values.astype(bf16)
+        rest = values - high.astype(f32)
         row = (ext * 2 + a) * 16
         lhs[row : row + 16, start : start + 128] = high
         if ext in BOUND:
             row = HI_ROWS + (BOUND.index(ext) * 2 + a) * 16
-            lhs[row : row + 16, start : start + 128] = low
+            lhs[row : row + 16, start : start + 128] = rest.astype(bf16)
+        else:
+            row = a * 16 + ext
+            edge_ref[side, row : row + 1, place : place + 128] = rest[side * 15 : side * 15 + 1]
 
     for chunk, members in enumerate(((0, 1), (2, 3), (4,))):
         for f in members:
-            wide[f, :, 0:PADX] = zero
-            wide[f, :, PADX + CX :] = zero
-            cells = jnp.concatenate([upper_ref[f], lower_ref[f]], 0)
-            high = cells.astype(bf16).astype(f32)
-            stacked = jnp.concatenate([high, cells - high, high, jnp.zeros_like(high)], 0)
-            added = dot(stacked.T.astype(bf16), side)
-            wide[f, :, PADX : PADX + CX] = along_ref[f] + added.reshape(ZS, CX, CY)
-            for z in range(ZS):
-                total = float(TAPS[R]) * wide[f, z, PADX - 8 : PADX + 72, :]
-                for k in range(1, R + 1):
-                    total = total + float(TAPS[R + k]) * (
-                        wide[f, z, PADX - 8 - k : PADX + 72 - k, :]
-                        + wide[f, z, PADX - 8 + k : PADX + 72 + k, :]
-                    )
-                smooth[f, z] = total
+            filtered(f)
+            reordered(f)
         for ext in range(EXT):
             rows = slice(ext * 8, ext * 8 + 8)
             if len(members) == 2:
                 for a in range(2):
-                    block = smooth[members[0] : members[0] + 2, a * 8 : a * 8 + 8, rows, :]
+                    block = along[members[0] : members[0] + 2, a * 8 : a * 8 + 8, rows, :]
                     turned = block.reshape(128, 128).T
                     for y in range(8):
-                        put(ext, a, chunk * 1024 + y * 128, turned[y * 16 : y * 16 + 16])
+                        values = turned[y * 16 : y * 16 + 16]
+                        start = chunk * 1024 + y * 128
+                        put(ext, a, start, y // 4, chunk * 512 + y % 4 * 128, values)
             else:
-                turned = smooth[4, :, rows, :].reshape(128, 128).T
+                turned = along[4, :, rows, :].reshape(128, 128).T
                 for m in range(4):
                     even = turned[m * 32 : m * 32 + 16]
                     odd = turned[m * 32 + 16 : m * 32 + 32]
-                    start = 2048 + m * 128
-                    put(ext, 0, start, jnp.where(first, even, pltpu.roll(odd, 64, 1)))
-                    put(ext, 1, start, jnp.where(first, pltpu.roll(even, 64, 1), odd))
+                    start, place = 2048 + m * 128, 1024 + m % 2 * 128
+                    put(ext, 0, start, m // 2, place, jnp.where(first, even, pltpu.roll(odd, 64, 1)))
+                    put(ext, 1, start, m // 2, place, jnp.where(first, pltpu.roll(even, 64, 1), odd))
         deep = slice(chunk * 1024, min(chunk * 1024 + 1024, KIN))
         for tile in range(3):
             columns = slice(tile * 256, tile * 256 + 256)
-            part = dot(lhs[:, deep], weight_ref[deep, columns])
-            both[:, columns] = part if chunk == 0 else both[:, columns] + part
-
-    for tile in range(3):
-        columns = slice(tile * 256, tile * 256 + 256)
-        lead = both[:64, columns] + both[HI_ROWS : HI_ROWS + 64, columns]
-        tail = both[256:HI_ROWS, columns] + both[HI_ROWS + 64 :, columns]
-        lead_hi, lead_lo = halves(lead)
-        tail_hi, tail_lo = halves(tail)
-        mid[0:64, columns] = lead_hi
-        mid[64:256, columns] = both[64:256, columns].astype(bf16)
-        mid[256:HI_ROWS, columns] = tail_hi
-        mid[HI_ROWS : HI_ROWS + 64, columns] = lead_lo
-        mid[HI_ROWS + 64 :, columns] = tail_lo
+            part = dot(lhs[:, deep], order_ref[deep, columns])
+            if chunk < 2:
+                both[:, columns] = part if chunk == 0 else both[:, columns] + part
+            else:
+                part = both[:, columns] + part
+                total_ref[0:64, columns] = part[:64] + part[HI_ROWS : HI_ROWS + 64]
+                total_ref[64:256, columns] = part[64:256]
+                total_ref[256:HI_ROWS, columns] = part[256:HI_ROWS] + part[HI_ROWS + 64 :]
+
+
+def edge_kernel(
+    upper_ref,
+    lower_ref,
+    table_ref,
+    edge_ref,
+    total_ref,
+    weight_ref,
+    order_ref,
+    out_ref,
+    parts,
+    mixed,
+    lhs,
+    mid,
+):
+    cells = jnp.concatenate([upper_ref[...], lower_ref[...]], 1).reshape(320, 128)
+    place = lax.broadcasted_iota(jnp.int32, (320, 128), 0) & 7
+    sums = jnp.zeros((320, 128), f32)
+    for m in range(R):
+        ahead = cells if m == 0 else pltpu.roll(cells, 320 - m, 0)
+        behind = cells if m == 0 else pltpu.roll(cells, m, 0)
+        used = jnp.where(place < R - m, ahead, jnp.where(place >= R + m, behind, 0.0))
+        sums = sums + float(TAPS[2 * R - m]) * used
+    none = jnp.zeros((16, 128), f32)
+    blocks = []
+    for group in range(5):
+        tiles = sums[group * 64 : group * 64 + 64]
+        blocks.append(
+            jnp.concatenate(
+                [
+                    jnp.concatenate([none, tiles], 0),
+                    jnp.concatenate([none[:8], tiles, none[:8]], 0),
+                    jnp.concatenate([tiles, none], 0),
+                ],
+                1,
+            )
+        )
+    high, low = halves(jnp.concatenate(blocks, 0))
+    parts[...] = dot(jnp.concatenate([high, low, high], 1), table_ref[...])
+    last = parts[320:]
+    first = lax.broadcasted_iota(jnp.int32, (80, 128), 1) < 64
+    rolled = pltpu.roll(last, 64, 1)
+    mixed[0:80] = jnp.where(first, last, pltpu.roll(rolled, 79, 0))
+    mixed[80:160] = jnp.where(first, rolled, pltpu.roll(last, 79, 0))
+    lhs[...] = edge_ref[...]
+    for side in range(2):
+        for a in range(2):
+            rows = slice(a * 16, a * 16 + EXT)
+            for pair in range(2):
+                for q in range(4):
+                    columns = slice(pair * 512 + q * 128, pair * 512 + q * 128 + 128)
+                    found = parts[pl.ds((pair * 2 + a) * 80 + side * 4 + q, EXT, stride=8), :]
+                    lhs[side, rows, columns] += found
+            for q in range(2):
+                columns = slice(1024 + q * 128, 1024 + q * 128 + 128)
+                found = mixed[pl.ds(a * 80 + side * 4 + q * 2, EXT, stride=8), :]
+                lhs[side, rows, columns] += found
+    added = []
+    for side in range(2):
+        high, low = halves(lhs[side])
+        values = jnp.concatenate([high, low], 0)
+        result = dot(values[:, :512], weight_ref[side * 512 : side * 512 + 512, :])
+        result = result + dot(values[:, 512:1024], weight_ref[1024 + side * 512 : 1536 + side * 512, :])
+        result = result + dot(values[:, 1024:], weight_ref[2048 + side * 256 : 2304 + side * 256, :])
+        added.append(result[:32] + result[32:])
+    patch = lax.broadcasted_iota(jnp.int32, (16, D), 0)
+    for ext in range(EXT):
+        for a in range(2):
+            row = (ext * 2 + a) * 16
+            near = a * 16 + ext
+            values = total_ref[row : row + 16]
+            values = values + jnp.where(patch == 0, added[0][near : near + 1], 0.0)
+            values = values + jnp.where(patch == 15, added[1][near : near + 1], 0.0)
+            high, low = halves(values)
+            mid[row : row + 16] = high
+            if ext in BOUND:
+                row = HI_ROWS + (BOUND.index(ext) * 2 + a) * 16
+                mid[row : row + 16] = low
     slots = dot(order_ref[...], mid[...]).astype(bf16)
     out_ref[...] = slots.reshape(16 * SLOTS // 4, 4, D)
 
@@ -263,12 +348,13 @@
     first = lax.broadcasted_iota(jnp.int32, (128, 128), 1) < 64
     none = jnp.zeros((128, 128), bf16)
     for a in range(2):
-        rows = slice(a * 128, a * 128 + 128)
+        groups = [slice(g * 32 + a * 16, g * 32 + a * 16 + 16) for g in range(8)]
         for pair in range(PAIRS):
             start = pair * 128
-            query = three[rows, start : start + 128]
-            keys = three[rows, D + start : D + start + 128]
-            values = three[rows, 2 * D + start : 2 * D + start + 128]
+            query, keys, values = [
+                jnp.concatenate([three[rows, D * n + start : D * n + start + 128] for rows in groups], 0)
+                for n in range(3)
+            ]
             keys = jnp.concatenate([jnp.where(first, keys, none), jnp.where(first, none, keys)], 0)
             values = jnp.concatenate(
                 [jnp.where(first, values, none), jnp.where(first, none, values)], 0
@@ -278,7 +364,9 @@
             left = left * (1.0 / jnp.sum(left, axis=-1, keepdims=True))
             right = right * (1.0 / jnp.sum(right, axis=-1, keepdims=True))
             weights = jnp.concatenate([left.astype(bf16), right.astype(bf16)], 1)
-            mixed[rows, start : start + 128] = dot(weights, values).astype(bf16)
+            result = dot(weights, values).astype(bf16)
+            for g, rows in enumerate(groups):
+                mixed[rows, start : start + 128] = result[g * 16 : g * 16 + 16]
     for tile in range(3):
         columns = slice(tile * 256, tile * 256 + 256)
         branch = dot(mixed[...], out_ref[:, columns]).astype(bf16)
@@ -299,7 +387,6 @@
     outw_ref,
     up_ref,
     down_ref,
-    order_ref,
     out_ref,
     hidden,
     three,
@@ -315,7 +402,7 @@
     for tile in range(3):
         columns = slice(tile * 256, tile * 256 + 256)
         total = hidden[:, columns] + dot(upper[...], down_ref[:, columns])
-        out_ref[:, columns] = dot(order_ref[...], total.astype(bf16)).astype(bf16)
+        out_ref[:, columns] = total.astype(bf16)
 
 
 def home_kernel(tokens_ref, order_ref, out_ref):
@@ -351,9 +438,9 @@
         in_specs=[pl.BlockSpec(memory_space=pltpu.HBM)],
         out_specs=[space] * 3,
         out_shape=[
-            like((NF, ZS, CX, CY), f32),
-            like((NF, R, ZS * CX), f32),
-            like((NF, R, ZS * CX), f32),
+            like((NF, ZS, CX + 2 * PADX, CY), f32),
+            like((40, R, 128), f32),
+            like((40, R, 128), f32),
         ],
         scratch_shapes=[
             pltpu.VMEM((NF, ZS + 2 * R, CX, CY), f32),
@@ -368,26 +455,30 @@
     smooth, upper, lower = prepare(fields)
     upper = lax.ppermute(upper, "gy", [(i, (i + 1) % count) for i in range(count)])
     lower = lax.ppermute(lower, "gy", [((i + 1) % count, i) for i in range(count)])
-    along, weight = whole(
-        band_kernel,
-        [like((NF, ZS, CX, CY), f32), like((KIN, D))],
-        [],
-        2 * 5120 * 256 * 256 + 2 * KIN * 256 * D,
-        8,
-    )(smooth, embed_weight)
-    slots = whole(
-        embed_kernel,
-        like((16 * SLOTS // 4, 4, D)),
+    total, edge, weight = whole(
+        main_kernel,
+        [like((HI_ROWS, D), f32), like((2, 32, KIN // 2), f32), like((KIN, D))],
         [
-            pltpu.VMEM((NF, ZS, CX + 2 * PADX, CY), f32),
+            pltpu.VMEM((NF, ZS, 80, CY), f32),
             pltpu.VMEM((NF, ZS, 80, CY), f32),
             pltpu.VMEM((ALL_ROWS, KIN), bf16),
             pltpu.VMEM((ALL_ROWS, D), f32),
+        ],
+        2 * 6400 * 256 * 256 + 2 * KIN * 256 * D + 2 * ALL_ROWS * KIN * D,
+        16,
+    )(smooth, embed_weight)
+    slots = whole(
+        edge_kernel,
+        like((16 * SLOTS // 4, 4, D)),
+        [
+            pltpu.VMEM((400, 128), f32),
+            pltpu.VMEM((160, 128), f32),
+            pltpu.VMEM((2, 32, KIN // 2), f32),
             pltpu.VMEM((ALL_ROWS, D), bf16),
         ],
-        2 * ALL_ROWS * KIN * D,
-        18,
-    )(along, upper, lower, side_table(), weight, message_order())
+        2 * 64 * KIN * D,
+        8,
+    )(upper, lower, strip_table(), edge, total, weight, message_order())
     slots = lax.all_to_all(
         slots.reshape(NXL, SLOTS // 4, 4, D), "gx", split_axis=0, concat_axis=0, tiled=True
     ).reshape(NXL * SLOTS // 4, 4, D)
@@ -408,7 +499,7 @@
         attention + [pltpu.VMEM((TOK, FF), bf16)],
         2 * TOK * D * (4 * D + 2 * FF),
         14,
-    )(tokens, separate(), qkv_weight, out_weight, up_weight, down_weight, to_owners())
+    )(tokens, separate(), qkv_weight, out_weight, up_weight, down_weight)
     tokens = lax.all_to_all(
         tokens.reshape(8, 32, D), "gy", split_axis=0, concat_axis=0, tiled=True
     ).reshape(TOK, D)

time: 80.9 us -> 77 us (0.952)
  waiting for transfers between devices: 2.2 us -> 0.01 us
  Pallas kernels: 21.9 us -> 20.8 us
    ppermute x1, waiting for transfers between devices: 1.66 us -> 0.01 us  [shards(): lax.ppermute(lower, 'gy', [((i + 1) % count, i) for i in range(count)])]
    pallas_call x5, Pallas kernels: 19.1 us -> 18.1 us  [call(): pl.pallas_call(kernel, out_shape=out_shape, in_specs=[space] * len(operan...]
    all_to_all x1, blocking collectives: 18.9 us -> 18.1 us  [shards(): lax.all_to_all(tokens, ('gx', 'gy'), split_axis=0, concat_axis=0, tiled=T...]
  transfers between devices with their start and end apart: 2 -> 2, of which waited for: 2 -> 0; matrix products, arithmetic and copies ran while one was open for 0% -> 0% of each run, Pallas kernels for 2% -> 7%
where the time goes in v5:
time: 77 us; the launch traced here: 76.8 us
  blocking collectives  49.4 us (64%)
  Pallas kernels  20.8 us (27%)
  starting transfers between devices  6.31 us (8%)
    pallas_call x5, Pallas kernels, call(): pl.pallas_call(kernel, out_shape=out_shape, in_specs=[space] * len(operan...  18.1 us
    all_to_all x1, blocking collectives, shards(): lax.all_to_all(tokens, ('gx', 'gy'), split_axis=0, concat_axis=0, tiled=T...  18.1 us
    all_to_all x1, blocking collectives, shards(): lax.all_to_all(slots.reshape(NXL, SLOTS // 4, 4, D), 'gx', split_axis=0,...  17.7 us
    all_to_all x1, blocking collectives, shards(): lax.all_to_all(tokens.reshape(8, 32, D), 'gy', split_axis=0, concat_axis=...  13.6 us
    ppermute x1, starting transfers between devices, shards(): lax.ppermute(upper, 'gy', [(i, (i + 1) % count) for i in range(count)])  4.03 us
    pallas_call x1, Pallas kernels, prepare(): pl.pallas_call(prep_kernel, in_specs=[pl.BlockSpec(memory_space=pltpu.HBM...  2.76 us
    ppermute x1, starting transfers between devices, shards(): lax.ppermute(lower, 'gy', [((i + 1) % count, i) for i in range(count)])  2.28 us
  transfers between devices with their start and end apart: 2, of which 0 were waited for; matrix products, arithmetic and copies ran while one was open for 0% of the time, Pallas kernels for 7%

profile of v5, /device:TPU:0, one launch (start us, length us, event | category | flops | bytes accessed | tf_op | source)
XLA Modules:
  0.0 76.8 jit_solution(8265856235822250915)
XLA Ops:
  0.0 2.8 %shard_map.118 = (f32[5,16,96,128]{3,2,1,0:T(8,128)S(1)}, f32[40,4,128]{2,1,0:T(4,128)S(1)}, f32[40,4,128]{2,1,0:T(4,128)S(1)}) custom-call(f32[5,24,64,128]{3,2,1,0:T(8,128)} %fields_ref.1), custom_call_target="tpu_custom_call" | custom-call | tf_op jit(solution)/shard_map/pallas_call | solution.py:436
  2.8 4.0 %collective-permute-start = (f32[40,4,128]{2,1,0:T(4,128)S(1)}, f32[40,4,128]{2,1,0:T(4,128)S(1)}, u32[]{:S(2)}, u32[]{:S(2)}) collective-permute-start(f32[40,4,128]{2,1,0:T(4,128)S(1)} %get-tuple-element.11), channel_id=1, source_target_pairs={{0,1},{1,2},{2,3},{3,4},{4,5},{5,6},{6,7},{7,0},{8,9},{9,10},{10,1... | collective-permute-start | bytes 245768 | tf_op jit(solution)/shard_map/ppermute | solution.py:456
  6.8 2.3 %collective-permute-start.1 = (f32[40,4,128]{2,1,0:T(4,128)S(1)}, f32[40,4,128]{2,1,0:T(4,128)S(1)}, u32[]{:S(2)}, u32[]{:S(2)}) collective-permute-start(f32[40,4,128]{2,1,0:T(4,128)S(1)} %get-tuple-element.12), channel_id=1, source_target_pairs={{1,0},{2,1},{3,2},{4,3},{5,4},{6,5},{7,6},{0,7},{9,8},{10,9},{11,1... | collective-permute-start | bytes 245768 | tf_op jit(solution)/shard_map/ppermute | solution.py:457
  9.1 0.0 copy-done.8
  9.1 0.0 slice-start.3
  9.1 5.2 %shard_map.119 = (f32[320,768]{1,0:T(8,128)S(1)}, f32[2,32,1280]{2,1,0:T(8,128)S(1)}, bf16[2560,768]{1,0:T(8,128)(2,1)S(1)}) custom-call(f32[5,16,96,128]{3,2,1,0:T(8,128)S(1)} %get-tuple-element.13.smooth_ref, bf16[2560,768]{1,0:T(8,128)(2,1)S(1)} %copy-done.8), custom_call_target="tpu_custom_call" | custom-call | flops 3607101440 | bytes 7864320 | tf_op jit(solution)/shard_map/pallas_call | solution.py:417
  14.3 0.0 collective-permute-done.upper_ref
  14.3 0.0 collective-permute-done.1.lower_ref
  14.3 0.0 copy-start
  14.4 0.0 copy-start.4
  14.4 0.0 copy-start.7
  14.4 0.0 slice-start
  14.4 2.4 %shard_map.120 = bf16[112,4,768]{2,1,0:T(4,128)(2,1)S(1)} custom-call(f32[40,4,128]{2,1,0:T(4,128)S(1)} %collective-permute-done.upper_ref, f32[40,4,128]{2,1,0:T(4,128)S(1)} %collective-permute-done.1.lower_ref, bf16[1152,128]{1,0:T(8,128)(2,1)S(1)} %copy-done.3, f32[2,32,1280]{2,1,0:T(8,128)S(1)} %get-tuple-element.14.edge_ref, ...), custom_call_target="tpu_custom_call" | custom-call | flops 251658240 | bytes 6103040 | tf_op jit(solution)/shard_map/pallas_call | solution.py:417
  16.8 0.0 slice-start.1
  16.8 0.0 copy-start.5
  16.8 17.7 %all_to_all.15 = bf16[16,7,4,768]{3,2,1,0:T(4,128)(2,1)S(1)} all-to-all(bf16[16,7,4,768]{3,2,1,0:T(4,128)(2,1)S(1)} %bitcast.10), channel_id=1, replica_groups=mesh['gx'=16,'gy'=8] {'gx'}, dimensions={0} | all-to-all | bytes 1376256 | tf_op jit(solution)/shard_map/all_to_all | solution.py:482
  34.6 0.0 copy-done.1
  34.6 3.0 %shard_map.121 = bf16[128,2,768]{2,1,0:T(2,128)(2,1)S(1)} custom-call(bf16[112,4,768]{2,1,0:T(4,128)(2,1)S(1)} %bitcast.9, bf16[256,448]{1,0:T(8,128)(2,1)S(1)} %copy-done.4, bf16[768,2304]{1,0:T(8,128)(2,1)S(1)} %copy-done, bf16[768,768]{1,0:T(8,128)(2,1)S(1)} %copy-done.1, bf16[256,256]{1,0:T(8,128)(2,1)S(1)} %copy-done.7), custom_call_target="tpu_custom_call" | custom-call | flops 1207959552 | bytes 5767168 | tf_op jit(solution)/shard_map/pallas_call | solution.py:417
  37.6 18.1 %all_to_all.16.tokens_ref = bf16[128,2,768]{2,1,0:T(2,128)(2,1)S(1)} all-to-all(bf16[128,2,768]{2,1,0:T(2,128)(2,1)S(1)} %shard_map.121), channel_id=1, replica_groups=mesh['gx'=16,'gy'=8] {'gx','gy'}, dimensions={0} | all-to-all | bytes 786432 | tf_op jit(solution)/shard_map/all_to_all | solution.py:493
  55.7 0.0 slice-done
  55.7 0.0 copy-start.6
  55.7 6.5 %shard_map.122 = bf16[256,768]{1,0:T(8,128)(2,1)S(1)} custom-call(bf16[128,2,768]{2,1,0:T(2,128)(2,1)S(1)} %all_to_all.16.tokens_ref, bf16[256,256]{1,0:T(8,128)(2,1)S(1)} %copy-done.5, bf16[768,2304]{1,0:T(8,128)(2,1)S(1)} %copy-done, bf16[768,768]{1,0:T(8,128)(2,1)S(1)} %copy-done.1, bf16[768,3072]{1,0:T(8,128)(2,1)S(1)} %bitcast.6, ...), custom_call_target="tpu_custom_call" | custom-call | flops 3623878656 | bytes 14680064 | tf_op jit(solution)/shard_map/pallas_call | solution.py:417
  62.2 13.6 %all_to_all.17 = bf16[8,32,768]{2,1,0:T(8,128)(2,1)S(1)} all-to-all(bf16[8,32,768]{2,1,0:T(8,128)(2,1)S(1)} %bitcast.12), channel_id=1, replica_groups=mesh['gx'=16,'gy'=8] {'gy'}, dimensions={0} | all-to-all | bytes 786432 | tf_op jit(solution)/shard_map/all_to_all | solution.py:503
  75.8 1.0 %shard_map.123 = bf16[256,768]{1,0:T(8,128)(2,1)} custom-call(bf16[256,768]{1,0:T(8,128)(2,1)S(1)} %bitcast.11, bf16[256,256]{1,0:T(8,128)(2,1)S(1)} %copy-done.6), custom_call_target="tpu_custom_call" | custom-call | flops 100663296 | bytes 524288 | tf_op jit(solution)/shard_map/pallas_call | solution.py:417
  (17 shorter events, 0.0 us)
Async XLA Ops:
  0.0 9.1 %copy-start.8 = (bf16[2560,768]{1,0:T(8,128)(2,1)S(1)}, bf16[2560,768]{1,0:T(8,128)(2,1)}, u32[]{:S(2)}) copy-start(bf16[2560,768]{1,0:T(8,128)(2,1)} %weight_ref.1) | copy-start | bytes 11796484
  0.0 55.7 %slice-start.2 = ((s8[4718592]{0:T(1024)(128)(4,1)}), s8[524288]{0:T(1024)(128)(4,1)S(1)}, s32[]{:S(2)}) async-start(s8[4718592]{0:T(1024)(128)(4,1)} %bitcast.7), calls=%async_computation.5 | async-start | bytes 1048576
  2.8 11.5 %collective-permute-start = (f32[40,4,128]{2,1,0:T(4,128)S(1)}, f32[40,4,128]{2,1,0:T(4,128)S(1)}, u32[]{:S(2)}, u32[]{:S(2)}) collective-permute-start(f32[40,4,128]{2,1,0:T(4,128)S(1)} %get-tuple-element.11), channel_id=1, source_target_pairs={{0,1},{1,2},{2,3},{3,4},{4,5},{5,6},{6,7},{7,0},{8,9},{9,10},{10,1... | collective-permute-start | bytes 245768 | tf_op jit(solution)/shard_map/ppermute | solution.py:456
  6.8 7.5 %collective-permute-start.1 = (f32[40,4,128]{2,1,0:T(4,128)S(1)}, f32[40,4,128]{2,1,0:T(4,128)S(1)}, u32[]{:S(2)}, u32[]{:S(2)}) collective-permute-start(f32[40,4,128]{2,1,0:T(4,128)S(1)} %get-tuple-element.12), channel_id=1, source_target_pairs={{1,0},{2,1},{3,2},{4,3},{5,4},{6,5},{7,6},{0,7},{9,8},{10,9},{11,1... | collective-permute-start | bytes 245768 | tf_op jit(solution)/shard_map/ppermute | solution.py:457
  9.1 5.2 %copy-start.2 = (bf16[448,448]{1,0:T(8,128)(2,1)S(1)}, bf16[448,448]{1,0:T(8,128)(2,1)}, u32[]{:S(2)}) copy-start(bf16[448,448]{1,0:T(8,128)(2,1)} %constant.13.clone.order_ref) | copy-start | bytes 1204228
  9.1 5.2 %copy-start.3 = (bf16[1152,128]{1,0:T(8,128)(2,1)S(1)}, bf16[1152,128]{1,0:T(8,128)(2,1)}, u32[]{:S(2)}) copy-start(bf16[1152,128]{1,0:T(8,128)(2,1)} %constant.12.clone.table_ref) | copy-start | bytes 884740
  9.1 25.5 %copy-start.1 = (bf16[768,768]{1,0:T(8,128)(2,1)S(1)}, bf16[768,768]{1,0:T(8,128)(2,1)}, u32[]{:S(2)}) copy-start(bf16[768,768]{1,0:T(8,128)(2,1)} %outw_ref.3) | copy-start | bytes 3538948
  9.1 46.6 %slice-start.3 = ((s8[4718592]{0:T(1024)(128)(4,1)}), s8[4194304]{0:T(1024)(128)(4,1)S(1)}, s32[]{:S(2)}) async-start(s8[4718592]{0:T(1024)(128)(4,1)} %bitcast.7), calls=%async_computation.6 | async-start | bytes 8388608
  14.3 20.2 %copy-start = (bf16[768,2304]{1,0:T(8,128)(2,1)S(1)}, bf16[768,2304]{1,0:T(8,128)(2,1)}, u32[]{:S(2)}) copy-start(bf16[768,2304]{1,0:T(8,128)(2,1)} %qkv_ref.3) | copy-start | bytes 10616836
  14.4 20.2 %copy-start.4 = (bf16[256,448]{1,0:T(8,128)(2,1)S(1)}, bf16[256,448]{1,0:T(8,128)(2,1)}, u32[]{:S(2)}) copy-start(bf16[256,448]{1,0:T(8,128)(2,1)} %constant.14.clone.sum_ref) | copy-start | bytes 688132
  14.4 20.2 %copy-start.7 = (bf16[256,256]{1,0:T(8,128)(2,1)S(1)}, bf16[256,256]{1,0:T(8,128)(2,1)}, u32[]{:S(2)}) copy-start(bf16[256,256]{1,0:T(8,128)(2,1)} %constant.15.clone.order_ref) | copy-start | bytes 393220
  14.4 41.3 %slice-start = ((s8[4718592]{0:T(1024)(128)(4,1)}), s8[4194304]{0:T(1024)(128)(4,1)S(1)}, s32[]{:S(2)}) async-start(s8[4718592]{0:T(1024)(128)(4,1)} %bitcast.5), calls=%async_computation.3 | async-start | bytes 8388608
  16.8 38.9 %slice-start.1 = ((s8[4718592]{0:T(1024)(128)(4,1)}), s8[524288]{0:T(1024)(128)(4,1)S(1)}, s32[]{:S(2)}) async-start(s8[4718592]{0:T(1024)(128)(4,1)} %bitcast.5), calls=%async_computation.4 | async-start | bytes 1048576
  16.8 38.9 %copy-start.5 = (bf16[256,256]{1,0:T(8,128)(2,1)S(1)}, bf16[256,256]{1,0:T(8,128)(2,1)}, u32[]{:S(2)}) copy-start(bf16[256,256]{1,0:T(8,128)(2,1)} %constant.16.clone.split_ref) | copy-start | bytes 393220
  55.7 20.1 %copy-start.6 = (bf16[256,256]{1,0:T(8,128)(2,1)S(1)}, bf16[256,256]{1,0:T(8,128)(2,1)}, u32[]{:S(2)}) copy-start(bf16[256,256]{1,0:T(8,128)(2,1)} %constant.17.clone.order_ref) | copy-start | bytes 393220

commit v6 on v5

--- a/solution.py
+++ b/solution.py
@@ -26,6 +26,7 @@
 HI_ROWS = EXT * 32
 ALL_ROWS = HI_ROWS + 128
 PADX = 16
+SHRINK = 2.0**15
 bf16 = jnp.bfloat16
 f32 = jnp.float32
 
@@ -90,7 +91,10 @@
 
 
 def message_order():
-    return permutation(16 * SLOTS, ALL_ROWS, lambda r: [(r % SLOTS) * 16 + r // SLOTS])
+    row = lax.broadcasted_iota(jnp.int32, (ALL_ROWS, ALL_ROWS), 0)
+    column = lax.broadcasted_iota(jnp.int32, (ALL_ROWS, ALL_ROWS), 1)
+    slot, line = column >> 4, column & 15
+    return jnp.where(row == line * SLOTS + slot, 1.0, 0.0).astype(bf16)
 
 
 def gather_sum():
@@ -175,7 +179,20 @@
         strip(32 + c, smooth_ref[NF - 1, :, PADX + c * 8 : PADX + c * 8 + 8, :])
 
 
-def main_kernel(smooth_ref, weight_ref, total_ref, edge_ref, order_ref, across, along, lhs, both):
+def main_kernel(
+    smooth_ref,
+    weight_ref,
+    out_ref,
+    base_ref,
+    edge_ref,
+    order_ref,
+    across,
+    along,
+    lhs,
+    both,
+    sums,
+    mid,
+):
     band = band_table()
     order = weight_order()
     first = lax.broadcasted_iota(jnp.int32, (16, 128), 1) < 64
@@ -215,8 +232,8 @@
             row = HI_ROWS + (BOUND.index(ext) * 2 + a) * 16
             lhs[row : row + 16, start : start + 128] = rest.astype(bf16)
         else:
-            row = a * 16 + ext
-            edge_ref[side, row : row + 1, place : place + 128] = rest[side * 15 : side * 15 + 1]
+            row = ext * 2 + a
+            edge_ref[side * 10 + place, row : row + 1, :] = rest[side * 15 : side * 15 + 1]
 
     for chunk, members in enumerate(((0, 1), (2, 3), (4,))):
         for f in members:
@@ -231,26 +248,35 @@
                     for y in range(8):
                         values = turned[y * 16 : y * 16 + 16]
                         start = chunk * 1024 + y * 128
-                        put(ext, a, start, y // 4, chunk * 512 + y % 4 * 128, values)
+                        put(ext, a, start, y // 4, chunk * 4 + y % 4, values)
             else:
                 turned = along[4, :, rows, :].reshape(128, 128).T
                 for m in range(4):
                     even = turned[m * 32 : m * 32 + 16]
                     odd = turned[m * 32 + 16 : m * 32 + 32]
-                    start, place = 2048 + m * 128, 1024 + m % 2 * 128
+                    start, place = 2048 + m * 128, 8 + m % 2
                     put(ext, 0, start, m // 2, place, jnp.where(first, even, pltpu.roll(odd, 64, 1)))
                     put(ext, 1, start, m // 2, place, jnp.where(first, pltpu.roll(even, 64, 1), odd))
         deep = slice(chunk * 1024, min(chunk * 1024 + 1024, KIN))
         for tile in range(3):
             columns = slice(tile * 256, tile * 256 + 256)
             part = dot(lhs[:, deep], order_ref[deep, columns])
-            if chunk < 2:
-                both[:, columns] = part if chunk == 0 else both[:, columns] + part
-            else:
-                part = both[:, columns] + part
-                total_ref[0:64, columns] = part[:64] + part[HI_ROWS : HI_ROWS + 64]
-                total_ref[64:256, columns] = part[64:256]
-                total_ref[256:HI_ROWS, columns] = part[256:HI_ROWS] + part[HI_ROWS + 64 :]
+            both[:, columns] = part if chunk == 0 else both[:, columns] + part
+    for tile in range(6):
+        columns = slice(tile * 128, tile * 128 + 128)
+        for start, low in ((0, HI_ROWS), (256, HI_ROWS + 64)):
+            rows, rest = slice(start, start + 64), slice(low, low + 64)
+            total = both[rows, columns] + both[rest, columns]
+            sums[tile, rows] = total
+            mid[rows, columns], mid[rest, columns] = halves(total)
+        total = both[64:256, columns]
+        sums[tile, 64:256] = total
+        mid[64:256, columns] = total.astype(bf16)
+        for side in range(2):
+            base_ref[side, 0 : 2 * EXT, columns] = sums[tile, pl.ds(side * 15, 2 * EXT, stride=16), :]
+            base_ref[side, 2 * EXT :, columns] = jnp.zeros((4, 128), f32)
+    slots = dot(message_order(), mid[...]).astype(bf16)
+    out_ref[...] = slots.reshape(16 * SLOTS // 4, 4, D)
 
 
 def edge_kernel(
@@ -258,15 +284,18 @@
     lower_ref,
     table_ref,
     edge_ref,
-    total_ref,
+    base_ref,
     weight_ref,
-    order_ref,
+    slots_ref,
     out_ref,
     parts,
     mixed,
     lhs,
-    mid,
+    copied,
 ):
+    inner = pl.ds(SLOTS // 4, 14 * SLOTS // 4)
+    copy = pltpu.make_async_copy(slots_ref.at[inner], out_ref.at[inner], copied)
+    copy.start()
     cells = jnp.concatenate([upper_ref[...], lower_ref[...]], 1).reshape(320, 128)
     place = lax.broadcasted_iota(jnp.int32, (320, 128), 0) & 7
     sums = jnp.zeros((320, 128), f32)
@@ -299,39 +328,33 @@
     lhs[...] = edge_ref[...]
     for side in range(2):
         for a in range(2):
-            rows = slice(a * 16, a * 16 + EXT)
+            rows = pl.ds(a, EXT, stride=2)
             for pair in range(2):
                 for q in range(4):
                     columns = slice(pair * 512 + q * 128, pair * 512 + q * 128 + 128)
                     found = parts[pl.ds((pair * 2 + a) * 80 + side * 4 + q, EXT, stride=8), :]
-                    lhs[side, rows, columns] += found
+                    lhs[side * 10 + pair * 4 + q, rows] += found
             for q in range(2):
-                columns = slice(1024 + q * 128, 1024 + q * 128 + 128)
                 found = mixed[pl.ds(a * 80 + side * 4 + q * 2, EXT, stride=8), :]
-                lhs[side, rows, columns] += found
-    added = []
+                lhs[side * 10 + 8 + q, rows] += found
     for side in range(2):
-        high, low = halves(lhs[side])
-        values = jnp.concatenate([high, low], 0)
-        result = dot(values[:, :512], weight_ref[side * 512 : side * 512 + 512, :])
-        result = result + dot(values[:, 512:1024], weight_ref[1024 + side * 512 : 1536 + side * 512, :])
-        result = result + dot(values[:, 1024:], weight_ref[2048 + side * 256 : 2304 + side * 256, :])
-        added.append(result[:32] + result[32:])
-    patch = lax.broadcasted_iota(jnp.int32, (16, D), 0)
-    for ext in range(EXT):
-        for a in range(2):
-            row = (ext * 2 + a) * 16
-            near = a * 16 + ext
-            values = total_ref[row : row + 16]
-            values = values + jnp.where(patch == 0, added[0][near : near + 1], 0.0)
-            values = values + jnp.where(patch == 15, added[1][near : near + 1], 0.0)
-            high, low = halves(values)
-            mid[row : row + 16] = high
-            if ext in BOUND:
-                row = HI_ROWS + (BOUND.index(ext) * 2 + a) * 16
-                mid[row : row + 16] = low
-    slots = dot(order_ref[...], mid[...]).astype(bf16)
-    out_ref[...] = slots.reshape(16 * SLOTS // 4, 4, D)
+        result = base_ref[side]
+        values = jnp.concatenate([lhs[side * 10 + n] for n in range(10)], 1)
+        high, low = halves(values)
+        values = jnp.concatenate([high.astype(f32), low.astype(f32)], 0).astype(bf16)
+        for first_lane, start, count in (
+            (0, side * 512, 512),
+            (512, 1024 + side * 512, 512),
+            (1024, 2048 + side * 256, 256),
+        ):
+            part = dot(values[:, first_lane : first_lane + count], weight_ref[start : start + count, :])
+            result = result + (part[:24] + part[24:])
+        high = result.astype(bf16).astype(f32)
+        low = result - high
+        slots = jnp.concatenate([high[: 2 * EXT], low[:4], low[16 : 2 * EXT]], 0).astype(bf16)
+        row = side * 15 * SLOTS // 4
+        out_ref[row : row + SLOTS // 4] = slots.reshape(SLOTS // 4, 4, D)
+    copy.wait()
 
 
 def layer_norm(hidden):
@@ -347,6 +370,7 @@
         three[:, columns] = dot(normed, qkv_ref[:, columns]).astype(bf16)
     first = lax.broadcasted_iota(jnp.int32, (128, 128), 1) < 64
     none = jnp.zeros((128, 128), bf16)
+    ones = jnp.concatenate([jnp.where(first, 1.0, 0.0), jnp.where(first, 0.0, 1.0)], 0).astype(bf16)
     for a in range(2):
         groups = [slice(g * 32 + a * 16, g * 32 + a * 16 + 16) for g in range(8)]
         for pair in range(PAIRS):
@@ -356,15 +380,13 @@
                 for n in range(3)
             ]
             keys = jnp.concatenate([jnp.where(first, keys, none), jnp.where(first, none, keys)], 0)
+            values = values * (1.0 / SHRINK)
             values = jnp.concatenate(
                 [jnp.where(first, values, none), jnp.where(first, none, values)], 0
             )
-            weights = jnp.exp(dot_t(query, keys) * 0.125)
-            left, right = weights[:, :128], weights[:, 128:]
-            left = left * (1.0 / jnp.sum(left, axis=-1, keepdims=True))
-            right = right * (1.0 / jnp.sum(right, axis=-1, keepdims=True))
-            weights = jnp.concatenate([left.astype(bf16), right.astype(bf16)], 1)
-            result = dot(weights, values).astype(bf16)
+            weights = jnp.exp(dot_t(query, keys) * 0.125).astype(bf16)
+            result = dot(weights, jnp.concatenate([values, ones], 1))
+            result = (result[:, :128] * (1.0 / result[:, 128:]) * SHRINK).astype(bf16)
             for g, rows in enumerate(groups):
                 mixed[rows, start : start + 128] = result[g * 16 : g * 16 + 16]
     for tile in range(3):
@@ -455,30 +477,33 @@
     smooth, upper, lower = prepare(fields)
     upper = lax.ppermute(upper, "gy", [(i, (i + 1) % count) for i in range(count)])
     lower = lax.ppermute(lower, "gy", [((i + 1) % count, i) for i in range(count)])
-    total, edge, weight = whole(
+    slots = like((16 * SLOTS // 4, 4, D))
+    inner, base, edge, weight = whole(
         main_kernel,
-        [like((HI_ROWS, D), f32), like((2, 32, KIN // 2), f32), like((KIN, D))],
+        [slots, like((2, 24, D), f32), like((20, 24, 128), f32), like((KIN, D))],
         [
             pltpu.VMEM((NF, ZS, 80, CY), f32),
             pltpu.VMEM((NF, ZS, 80, CY), f32),
             pltpu.VMEM((ALL_ROWS, KIN), bf16),
             pltpu.VMEM((ALL_ROWS, D), f32),
+            pltpu.VMEM((6, HI_ROWS, 128), f32),
+            pltpu.VMEM((ALL_ROWS, D), bf16),
         ],
         2 * 6400 * 256 * 256 + 2 * KIN * 256 * D + 2 * ALL_ROWS * KIN * D,
-        16,
+        18,
     )(smooth, embed_weight)
     slots = whole(
         edge_kernel,
-        like((16 * SLOTS // 4, 4, D)),
+        slots,
         [
             pltpu.VMEM((400, 128), f32),
             pltpu.VMEM((160, 128), f32),
-            pltpu.VMEM((2, 32, KIN // 2), f32),
-            pltpu.VMEM((ALL_ROWS, D), bf16),
+            pltpu.VMEM((20, 24, 128), f32),
+            pltpu.SemaphoreType.DMA(()),
         ],
         2 * 64 * KIN * D,
         8,
-    )(upper, lower, strip_table(), edge, total, weight, message_order())
+    )(upper, lower, strip_table(), edge, base, weight, inner)
     slots = lax.all_to_all(
         slots.reshape(NXL, SLOTS // 4, 4, D), "gx", split_axis=0, concat_axis=0, tiled=True
     ).reshape(NXL * SLOTS // 4, 4, D)

time: 77 us -> 76.5 us (level)
  no operation moved by 1% of the time
where the time goes in v6:
time: 76.5 us; the launch traced here: 76.3 us
  blocking collectives  49.5 us (65%)
  Pallas kernels  20.2 us (26%)
  starting transfers between devices  6.31 us (8%)
    all_to_all x1, blocking collectives, shards(): lax.all_to_all(tokens, ('gx', 'gy'), split_axis=0, concat_axis=0, tiled=T...  18.1 us
    all_to_all x1, blocking collectives, shards(): lax.all_to_all(slots.reshape(NXL, SLOTS // 4, 4, D), 'gx', split_axis=0,...  17.9 us
    pallas_call x5, Pallas kernels, call(): pl.pallas_call(kernel, out_shape=out_shape, in_specs=[space] * len(operan...  17.5 us
    all_to_all x1, blocking collectives, shards(): lax.all_to_all(tokens.reshape(8, 32, D), 'gy', split_axis=0, concat_axis=...  13.6 us
    ppermute x1, starting transfers between devices, shards(): lax.ppermute(upper, 'gy', [(i, (i + 1) % count) for i in range(count)])  4.03 us
    pallas_call x1, Pallas kernels, prepare(): pl.pallas_call(prep_kernel, in_specs=[pl.BlockSpec(memory_space=pltpu.HBM...  2.76 us
    ppermute x1, starting transfers between devices, shards(): lax.ppermute(lower, 'gy', [((i + 1) % count, i) for i in range(count)])  2.28 us
  transfers between devices with their start and end apart: 2, of which 0 were waited for; matrix products, arithmetic and copies ran while one was open for 0% of the time, Pallas kernels for 7%

profile of v6, /device:TPU:0, one launch (start us, length us, event | category | flops | bytes accessed | tf_op | source)
XLA Modules:
  0.0 76.3 jit_solution(4727022202316758733)
XLA Ops:
  0.0 2.8 %shard_map.109 = (f32[5,16,96,128]{3,2,1,0:T(8,128)S(1)}, f32[40,4,128]{2,1,0:T(4,128)S(1)}, f32[40,4,128]{2,1,0:T(4,128)S(1)}) custom-call(f32[5,24,64,128]{3,2,1,0:T(8,128)} %fields_ref.1), custom_call_target="tpu_custom_call" | custom-call | tf_op jit(solution)/shard_map/pallas_call | solution.py:458
  2.8 4.0 %collective-permute-start = (f32[40,4,128]{2,1,0:T(4,128)S(1)}, f32[40,4,128]{2,1,0:T(4,128)S(1)}, u32[]{:S(2)}, u32[]{:S(2)}) collective-permute-start(f32[40,4,128]{2,1,0:T(4,128)S(1)} %get-tuple-element.12), channel_id=1, source_target_pairs={{0,1},{1,2},{2,3},{3,4},{4,5},{5,6},{6,7},{7,0},{8,9},{9,10},{10,1... | collective-permute-start | bytes 245768 | tf_op jit(solution)/shard_map/ppermute | solution.py:478
  6.8 2.3 %collective-permute-start.1 = (f32[40,4,128]{2,1,0:T(4,128)S(1)}, f32[40,4,128]{2,1,0:T(4,128)S(1)}, u32[]{:S(2)}, u32[]{:S(2)}) collective-permute-start(f32[40,4,128]{2,1,0:T(4,128)S(1)} %get-tuple-element.13), channel_id=1, source_target_pairs={{1,0},{2,1},{3,2},{4,3},{5,4},{6,5},{7,6},{0,7},{9,8},{10,9},{11,1... | collective-permute-start | bytes 245768 | tf_op jit(solution)/shard_map/ppermute | solution.py:479
  9.1 5.6 %shard_map.110 = (bf16[112,4,768]{2,1,0:T(4,128)(2,1)S(1)}, f32[2,24,768]{2,1,0:T(8,128)S(1)}, f32[20,24,128]{2,1,0:T(8,128)S(1)}, bf16[2560,768]{1,0:T(8,128)(2,1)S(1)}) custom-call(f32[5,16,96,128]{3,2,1,0:T(8,128)S(1)} %get-tuple-element.14.smooth_ref, bf16[2560,768]{1,0:T(8,128)(2,1)S(1)} %copy-done.7), custom_call_target="tpu_custom_call" | custom-call | flops 3607101440 | bytes 7864320 | tf_op jit(solution)/shard_map/pallas_call | solution.py:439
  14.7 0.0 copy-start
  14.7 0.0 copy-start.1
  14.7 0.0 copy-start.3
  14.7 0.0 copy-start.6
  14.8 0.0 collective-permute-done.upper_ref
  14.8 0.0 collective-permute-done.1.lower_ref
  14.8 0.0 slice-start
  14.8 1.9 %shard_map.111 = bf16[112,4,768]{2,1,0:T(4,128)(2,1)S(1)} custom-call(f32[40,4,128]{2,1,0:T(4,128)S(1)} %collective-permute-done.upper_ref, f32[40,4,128]{2,1,0:T(4,128)S(1)} %collective-permute-done.1.lower_ref, bf16[1152,128]{1,0:T(8,128)(2,1)S(1)} %copy-done.2, f32[20,24,128]{2,1,0:T(8,128)S(1)} %get-tuple-element.15.edge_ref, ...), custom_call_target="tpu_custom_call" | custom-call | flops 251658240 | bytes 5472256 | tf_op jit(solution)/shard_map/pallas_call | solution.py:439
  16.7 0.0 slice-start.1
  16.7 0.0 copy-start.4
  16.7 17.9 %all_to_all.15 = bf16[16,7,4,768]{3,2,1,0:T(4,128)(2,1)S(1)} all-to-all(bf16[16,7,4,768]{3,2,1,0:T(4,128)(2,1)S(1)} %bitcast.9), channel_id=1, replica_groups=mesh['gx'=16,'gy'=8] {'gx'}, dimensions={0} | all-to-all | bytes 1376256 | tf_op jit(solution)/shard_map/all_to_all | solution.py:507
  34.6 0.0 copy-done
  34.6 0.0 copy-done.3
  34.6 2.8 %shard_map.112 = bf16[128,2,768]{2,1,0:T(2,128)(2,1)S(1)} custom-call(bf16[112,4,768]{2,1,0:T(4,128)(2,1)S(1)} %bitcast.10, bf16[256,448]{1,0:T(8,128)(2,1)S(1)} %copy-done.3, bf16[768,2304]{1,0:T(8,128)(2,1)S(1)} %copy-done, bf16[768,768]{1,0:T(8,128)(2,1)S(1)} %copy-done.1, bf16[256,256]{1,0:T(8,128)(2,1)S(1)} %copy-done.6), custom_call_target="tpu_custom_call" | custom-call | flops 1207959552 | bytes 5767168 | tf_op jit(solution)/shard_map/pallas_call | solution.py:439
  37.4 18.1 %all_to_all.16.tokens_ref = bf16[128,2,768]{2,1,0:T(2,128)(2,1)S(1)} all-to-all(bf16[128,2,768]{2,1,0:T(2,128)(2,1)S(1)} %shard_map.112), channel_id=1, replica_groups=mesh['gx'=16,'gy'=8] {'gx','gy'}, dimensions={0} | all-to-all | bytes 786432 | tf_op jit(solution)/shard_map/all_to_all | solution.py:518
  55.5 0.0 slice-done.3
  55.5 0.0 copy-start.5
  55.5 6.2 %shard_map.113 = bf16[256,768]{1,0:T(8,128)(2,1)S(1)} custom-call(bf16[128,2,768]{2,1,0:T(2,128)(2,1)S(1)} %all_to_all.16.tokens_ref, bf16[256,256]{1,0:T(8,128)(2,1)S(1)} %copy-done.4, bf16[768,2304]{1,0:T(8,128)(2,1)S(1)} %copy-done, bf16[768,768]{1,0:T(8,128)(2,1)S(1)} %copy-done.1, bf16[768,3072]{1,0:T(8,128)(2,1)S(1)} %bitcast.6, ...), custom_call_target="tpu_custom_call" | custom-call | flops 3623878656 | bytes 14680064 | tf_op jit(solution)/shard_map/pallas_call | solution.py:439
  61.7 13.6 %all_to_all.17 = bf16[8,32,768]{2,1,0:T(8,128)(2,1)S(1)} all-to-all(bf16[8,32,768]{2,1,0:T(8,128)(2,1)S(1)} %bitcast.12), channel_id=1, replica_groups=mesh['gx'=16,'gy'=8] {'gy'}, dimensions={0} | all-to-all | bytes 786432 | tf_op jit(solution)/shard_map/all_to_all | solution.py:528
  75.3 1.0 %shard_map.114 = bf16[256,768]{1,0:T(8,128)(2,1)} custom-call(bf16[256,768]{1,0:T(8,128)(2,1)S(1)} %bitcast.11, bf16[256,256]{1,0:T(8,128)(2,1)S(1)} %copy-done.5), custom_call_target="tpu_custom_call" | custom-call | flops 100663296 | bytes 524288 | tf_op jit(solution)/shard_map/pallas_call | solution.py:439
  (15 shorter events, 0.0 us)
Async XLA Ops:
  0.0 9.1 %copy-start.7 = (bf16[2560,768]{1,0:T(8,128)(2,1)S(1)}, bf16[2560,768]{1,0:T(8,128)(2,1)}, u32[]{:S(2)}) copy-start(bf16[2560,768]{1,0:T(8,128)(2,1)} %weight_ref.1) | copy-start | bytes 11796484
  0.0 55.5 %slice-start.2 = ((s8[4718592]{0:T(1024)(128)(4,1)}), s8[524288]{0:T(1024)(128)(4,1)S(1)}, s32[]{:S(2)}) async-start(s8[4718592]{0:T(1024)(128)(4,1)} %bitcast.7), calls=%async_computation.5 | async-start | bytes 1048576
  2.8 12.0 %collective-permute-start = (f32[40,4,128]{2,1,0:T(4,128)S(1)}, f32[40,4,128]{2,1,0:T(4,128)S(1)}, u32[]{:S(2)}, u32[]{:S(2)}) collective-permute-start(f32[40,4,128]{2,1,0:T(4,128)S(1)} %get-tuple-element.12), channel_id=1, source_target_pairs={{0,1},{1,2},{2,3},{3,4},{4,5},{5,6},{6,7},{7,0},{8,9},{9,10},{10,1... | collective-permute-start | bytes 245768 | tf_op jit(solution)/shard_map/ppermute | solution.py:478
  6.8 8.0 %collective-permute-start.1 = (f32[40,4,128]{2,1,0:T(4,128)S(1)}, f32[40,4,128]{2,1,0:T(4,128)S(1)}, u32[]{:S(2)}, u32[]{:S(2)}) collective-permute-start(f32[40,4,128]{2,1,0:T(4,128)S(1)} %get-tuple-element.13), channel_id=1, source_target_pairs={{1,0},{2,1},{3,2},{4,3},{5,4},{6,5},{7,6},{0,7},{9,8},{10,9},{11,1... | collective-permute-start | bytes 245768 | tf_op jit(solution)/shard_map/ppermute | solution.py:479
  9.1 5.7 %copy-start.2 = (bf16[1152,128]{1,0:T(8,128)(2,1)S(1)}, bf16[1152,128]{1,0:T(8,128)(2,1)}, u32[]{:S(2)}) copy-start(bf16[1152,128]{1,0:T(8,128)(2,1)} %constant.10.clone.table_ref) | copy-start | bytes 884740
  9.1 46.4 %slice-start.3 = ((s8[4718592]{0:T(1024)(128)(4,1)}), s8[4194304]{0:T(1024)(128)(4,1)S(1)}, s32[]{:S(2)}) async-start(s8[4718592]{0:T(1024)(128)(4,1)} %bitcast.7), calls=%async_computation.6 | async-start | bytes 8388608
  14.7 19.9 %copy-start = (bf16[768,2304]{1,0:T(8,128)(2,1)S(1)}, bf16[768,2304]{1,0:T(8,128)(2,1)}, u32[]{:S(2)}) copy-start(bf16[768,2304]{1,0:T(8,128)(2,1)} %qkv_ref.3) | copy-start | bytes 10616836
  14.7 19.8 %copy-start.1 = (bf16[768,768]{1,0:T(8,128)(2,1)S(1)}, bf16[768,768]{1,0:T(8,128)(2,1)}, u32[]{:S(2)}) copy-start(bf16[768,768]{1,0:T(8,128)(2,1)} %outw_ref.3) | copy-start | bytes 3538948
  14.7 19.8 %copy-start.3 = (bf16[256,448]{1,0:T(8,128)(2,1)S(1)}, bf16[256,448]{1,0:T(8,128)(2,1)}, u32[]{:S(2)}) copy-start(bf16[256,448]{1,0:T(8,128)(2,1)} %constant.11.clone.sum_ref) | copy-start | bytes 688132
  14.7 19.8 %copy-start.6 = (bf16[256,256]{1,0:T(8,128)(2,1)S(1)}, bf16[256,256]{1,0:T(8,128)(2,1)}, u32[]{:S(2)}) copy-start(bf16[256,256]{1,0:T(8,128)(2,1)} %constant.12.clone.order_ref) | copy-start | bytes 393220
  14.8 40.7 %slice-start = ((s8[4718592]{0:T(1024)(128)(4,1)}), s8[4194304]{0:T(1024)(128)(4,1)S(1)}, s32[]{:S(2)}) async-start(s8[4718592]{0:T(1024)(128)(4,1)} %bitcast.5), calls=%async_computation.3 | async-start | bytes 8388608
  16.7 38.8 %slice-start.1 = ((s8[4718592]{0:T(1024)(128)(4,1)}), s8[524288]{0:T(1024)(128)(4,1)S(1)}, s32[]{:S(2)}) async-start(s8[4718592]{0:T(1024)(128)(4,1)} %bitcast.5), calls=%async_computation.4 | async-start | bytes 1048576
  16.7 38.8 %copy-start.4 = (bf16[256,256]{1,0:T(8,128)(2,1)S(1)}, bf16[256,256]{1,0:T(8,128)(2,1)}, u32[]{:S(2)}) copy-start(bf16[256,256]{1,0:T(8,128)(2,1)} %constant.13.clone.split_ref) | copy-start | bytes 393220
  55.5 19.8 %copy-start.5 = (bf16[256,256]{1,0:T(8,128)(2,1)S(1)}, bf16[256,256]{1,0:T(8,128)(2,1)}, u32[]{:S(2)}) copy-start(bf16[256,256]{1,0:T(8,128)(2,1)} %constant.14.clone.order_ref) | copy-start | bytes 393220

commit v7 on v6

--- a/solution.py
+++ b/solution.py
@@ -101,7 +101,7 @@
     low = {ext: 2 * EXT + 2 * n for n, ext in enumerate(BOUND)}
 
     def source(row):
-        a, i, c = row // 16 % 2, row // 32 * 2 + row // 8 % 2, row % 8
+        a, i, c = row // 128, row // 8 % 16, row % 8
         found = [i * SLOTS + (c + 1) * 2 + a]
         if c == 0:
             left = (i - 1) % NXL * SLOTS
@@ -115,11 +115,11 @@
 
 
 def interleave():
-    return permutation(TOK, TOK, lambda r: [r // 32 * 32 + r % 2 * 16 + r // 2 % 16])
+    return permutation(TOK, TOK, lambda r: [(r % 2) * 128 + r // 2])
 
 
 def separate():
-    return permutation(TOK, TOK, lambda r: [((r % 16) * 8 + r // 32) * 2 + r // 16 % 2])
+    return permutation(TOK, TOK, lambda r: [((r % 16) * 8 + r // 16 % 8) * 2 + r // 128])
 
 
 def to_home():
@@ -363,41 +363,77 @@
     return (center * lax.rsqrt(spread + 1e-05)).astype(bf16)
 
 
-def attend(hidden, qkv_ref, out_ref, three, mixed):
-    normed = layer_norm(hidden[...])
+def attention(a, hidden, qkv_ref, out_ref, three, mixed):
+    rows = slice(a * 128, a * 128 + 128)
+    normed = layer_norm(hidden[rows])
+    yield
     for tile in range(9):
         columns = slice(tile * 256, tile * 256 + 256)
-        three[:, columns] = dot(normed, qkv_ref[:, columns]).astype(bf16)
+        three[rows, columns] = dot(normed, qkv_ref[:, columns]).astype(bf16)
+        yield
     first = lax.broadcasted_iota(jnp.int32, (128, 128), 1) < 64
     none = jnp.zeros((128, 128), bf16)
     ones = jnp.concatenate([jnp.where(first, 1.0, 0.0), jnp.where(first, 0.0, 1.0)], 0).astype(bf16)
-    for a in range(2):
-        groups = [slice(g * 32 + a * 16, g * 32 + a * 16 + 16) for g in range(8)]
-        for pair in range(PAIRS):
-            start = pair * 128
-            query, keys, values = [
-                jnp.concatenate([three[rows, D * n + start : D * n + start + 128] for rows in groups], 0)
-                for n in range(3)
-            ]
-            keys = jnp.concatenate([jnp.where(first, keys, none), jnp.where(first, none, keys)], 0)
-            values = values * (1.0 / SHRINK)
-            values = jnp.concatenate(
-                [jnp.where(first, values, none), jnp.where(first, none, values)], 0
-            )
-            weights = jnp.exp(dot_t(query, keys) * 0.125).astype(bf16)
-            result = dot(weights, jnp.concatenate([values, ones], 1))
-            result = (result[:, :128] * (1.0 / result[:, 128:]) * SHRINK).astype(bf16)
-            for g, rows in enumerate(groups):
-                mixed[rows, start : start + 128] = result[g * 16 : g * 16 + 16]
+    for pair in range(PAIRS):
+        columns = slice(pair * 128, pair * 128 + 128)
+        query, keys, values = [
+            three[rows, D * n + pair * 128 : D * n + pair * 128 + 128] for n in range(3)
+        ]
+        keys = jnp.concatenate([jnp.where(first, keys, none), jnp.where(first, none, keys)], 0)
+        values = values * (1.0 / SHRINK)
+        values = jnp.concatenate([jnp.where(first, values, none), jnp.where(first, none, values)], 0)
+        weights = jnp.exp(dot_t(query, keys) * 0.125).astype(bf16)
+        result = dot(weights, jnp.concatenate([values, ones], 1))
+        mixed[rows, columns] = (result[:, :128] * (1.0 / result[:, 128:]) * SHRINK).astype(bf16)
+        yield
     for tile in range(3):
         columns = slice(tile * 256, tile * 256 + 256)
-        branch = dot(mixed[...], out_ref[:, columns]).astype(bf16)
-        hidden[:, columns] = hidden[:, columns] + branch.astype(f32)
+        branch = dot(mixed[rows], out_ref[:, columns]).astype(bf16)
+        hidden[rows, columns] = hidden[rows, columns] + branch.astype(f32)
+        yield
+
+
+def feed_forward(a, hidden, up_ref, down_ref, out_ref, upper):
+    rows = slice(a * 128, a * 128 + 128)
+    normed = layer_norm(hidden[rows])
+    yield
+    for tile in range(FF // 256):
+        columns = slice(tile * 256, tile * 256 + 256)
+        values = jax.nn.gelu(dot(normed, up_ref[:, columns]), approximate=True)
+        upper[rows, columns] = values.astype(bf16)
+        yield
+    for tile in range(3):
+        columns = slice(tile * 256, tile * 256 + 256)
+        total = (hidden[rows, columns] + dot(upper[rows], down_ref[:, columns])).astype(bf16)
+        for j in range(8):
+            start = j * 32 + a * 16
+            out_ref[start : start + 16, columns] = total[j * 16 : j * 16 + 16]
+        yield
+
+
+def staggered(chains, lag):
+    lead, trail = chains
+    for _ in range(lag):
+        next(lead, None)
+    while True:
+        done = [next(lead, "end"), next(trail, "end")]
+        if done == ["end", "end"]:
+            break
+
+
+X_LAG = 0
+Y_LAG = 0
 
 
 def x_kernel(slots_ref, sum_ref, qkv_ref, outw_ref, order_ref, out_ref, hidden, three, mixed):
-    hidden[...] = dot(sum_ref[...], slots_ref[...].reshape(NXL * SLOTS, D))
-    attend(hidden, qkv_ref, outw_ref, three, mixed)
+    slots = slots_ref[...].reshape(NXL * SLOTS, D)
+
+    def chain(a):
+        rows = slice(a * 128, a * 128 + 128)
+        hidden[rows] = dot(sum_ref[rows], slots)
+        yield from attention(a, hidden, qkv_ref, outw_ref, three, mixed)
+
+    staggered([chain(0), chain(1)], X_LAG)
     tokens = dot(order_ref[...], hidden[...].astype(bf16)).astype(bf16)
     out_ref[...] = tokens.reshape(128, 2, D)
 
@@ -415,16 +451,15 @@
     mixed,
     upper,
 ):
-    hidden[...] = dot(split_ref[...], tokens_ref[...].reshape(TOK, D))
-    attend(hidden, qkv_ref, outw_ref, three, mixed)
-    normed = layer_norm(hidden[...])
-    for tile in range(FF // 256):
-        columns = slice(tile * 256, tile * 256 + 256)
-        upper[:, columns] = jax.nn.gelu(dot(normed, up_ref[:, columns]), approximate=True).astype(bf16)
-    for tile in range(3):
-        columns = slice(tile * 256, tile * 256 + 256)
-        total = hidden[:, columns] + dot(upper[...], down_ref[:, columns])
-        out_ref[:, columns] = total.astype(bf16)
+    tokens = tokens_ref[...].reshape(TOK, D)
+
+    def chain(a):
+        rows = slice(a * 128, a * 128 + 128)
+        hidden[rows] = dot(split_ref[rows], tokens)
+        yield from attention(a, hidden, qkv_ref, outw_ref, three, mixed)
+        yield from feed_forward(a, hidden, up_ref, down_ref, out_ref, upper)
+
+    staggered([chain(0), chain(1)], Y_LAG)
 
 
 def home_kernel(tokens_ref, order_ref, out_ref):

time: 76.5 us -> 75.4 us (0.986)
  Pallas kernels: 20.2 us -> 19.1 us
    pallas_call x5, Pallas kernels: 17.5 us -> 16.4 us  [call(): pl.pallas_call(kernel, out_shape=out_shape, in_specs=[space] * len(operan...]
where the time goes in v7:
time: 75.4 us; the launch traced here: 75.2 us
  blocking collectives  49.5 us (66%)
  Pallas kernels  19.1 us (25%)
  starting transfers between devices  6.31 us (8%)
    all_to_all x1, blocking collectives, shards(): lax.all_to_all(tokens, ('gx', 'gy'), split_axis=0, concat_axis=0, tiled=T...  18.1 us
    all_to_all x1, blocking collectives, shards(): lax.all_to_all(slots.reshape(NXL, SLOTS // 4, 4, D), 'gx', split_axis=0,...  17.9 us
    pallas_call x5, Pallas kernels, call(): pl.pallas_call(kernel, out_shape=out_shape, in_specs=[space] * len(operan...  16.4 us
    all_to_all x1, blocking collectives, shards(): lax.all_to_all(tokens.reshape(8, 32, D), 'gy', split_axis=0, concat_axis=...  13.6 us
    ppermute x1, starting transfers between devices, shards(): lax.ppermute(upper, 'gy', [(i, (i + 1) % count) for i in range(count)])  4.03 us
    pallas_call x1, Pallas kernels, prepare(): pl.pallas_call(prep_kernel, in_specs=[pl.BlockSpec(memory_space=pltpu.HBM...  2.76 us
    ppermute x1, starting transfers between devices, shards(): lax.ppermute(lower, 'gy', [((i + 1) % count, i) for i in range(count)])  2.28 us
  transfers between devices with their start and end apart: 2, of which 0 were waited for; matrix products, arithmetic and copies ran while one was open for 0% of the time, Pallas kernels for 7%

profile of v7, /device:TPU:0, one launch (start us, length us, event | category | flops | bytes accessed | tf_op | source)
XLA Modules:
  0.0 75.2 jit_solution(7415635378975231804)
XLA Ops:
  0.0 2.8 %shard_map.109 = (f32[5,16,96,128]{3,2,1,0:T(8,128)S(1)}, f32[40,4,128]{2,1,0:T(4,128)S(1)}, f32[40,4,128]{2,1,0:T(4,128)S(1)}) custom-call(f32[5,24,64,128]{3,2,1,0:T(8,128)} %fields_ref.1), custom_call_target="tpu_custom_call" | custom-call | tf_op jit(solution)/shard_map/pallas_call | solution.py:493
  2.8 4.0 %collective-permute-start = (f32[40,4,128]{2,1,0:T(4,128)S(1)}, f32[40,4,128]{2,1,0:T(4,128)S(1)}, u32[]{:S(2)}, u32[]{:S(2)}) collective-permute-start(f32[40,4,128]{2,1,0:T(4,128)S(1)} %get-tuple-element.12), channel_id=1, source_target_pairs={{0,1},{1,2},{2,3},{3,4},{4,5},{5,6},{6,7},{7,0},{8,9},{9,10},{10,1... | collective-permute-start | bytes 245768 | tf_op jit(solution)/shard_map/ppermute | solution.py:513
  6.8 2.3 %collective-permute-start.1 = (f32[40,4,128]{2,1,0:T(4,128)S(1)}, f32[40,4,128]{2,1,0:T(4,128)S(1)}, u32[]{:S(2)}, u32[]{:S(2)}) collective-permute-start(f32[40,4,128]{2,1,0:T(4,128)S(1)} %get-tuple-element.13), channel_id=1, source_target_pairs={{1,0},{2,1},{3,2},{4,3},{5,4},{6,5},{7,6},{0,7},{9,8},{10,9},{11,1... | collective-permute-start | bytes 245768 | tf_op jit(solution)/shard_map/ppermute | solution.py:514
  9.1 5.6 %shard_map.110 = (bf16[112,4,768]{2,1,0:T(4,128)(2,1)S(1)}, f32[2,24,768]{2,1,0:T(8,128)S(1)}, f32[20,24,128]{2,1,0:T(8,128)S(1)}, bf16[2560,768]{1,0:T(8,128)(2,1)S(1)}) custom-call(f32[5,16,96,128]{3,2,1,0:T(8,128)S(1)} %get-tuple-element.14.smooth_ref, bf16[2560,768]{1,0:T(8,128)(2,1)S(1)} %copy-done.7), custom_call_target="tpu_custom_call" | custom-call | flops 3607101440 | bytes 7864320 | tf_op jit(solution)/shard_map/pallas_call | solution.py:474
  14.7 0.0 copy-start
  14.7 0.0 copy-start.1
  14.7 0.0 copy-start.3
  14.7 0.0 copy-start.6
  14.8 0.0 collective-permute-done.upper_ref
  14.8 0.0 collective-permute-done.1.lower_ref
  14.8 0.0 slice-start
  14.8 1.9 %shard_map.111 = bf16[112,4,768]{2,1,0:T(4,128)(2,1)S(1)} custom-call(f32[40,4,128]{2,1,0:T(4,128)S(1)} %collective-permute-done.upper_ref, f32[40,4,128]{2,1,0:T(4,128)S(1)} %collective-permute-done.1.lower_ref, bf16[1152,128]{1,0:T(8,128)(2,1)S(1)} %copy-done.2, f32[20,24,128]{2,1,0:T(8,128)S(1)} %get-tuple-element.15.edge_ref, ...), custom_call_target="tpu_custom_call" | custom-call | flops 251658240 | bytes 5472256 | tf_op jit(solution)/shard_map/pallas_call | solution.py:474
  16.7 0.0 slice-start.1
  16.7 0.0 copy-start.4
  16.7 17.9 %all_to_all.15 = bf16[16,7,4,768]{3,2,1,0:T(4,128)(2,1)S(1)} all-to-all(bf16[16,7,4,768]{3,2,1,0:T(4,128)(2,1)S(1)} %bitcast.9), channel_id=1, replica_groups=mesh['gx'=16,'gy'=8] {'gx'}, dimensions={0} | all-to-all | bytes 1376256 | tf_op jit(solution)/shard_map/all_to_all | solution.py:542
  34.6 0.0 copy-done
  34.6 0.0 copy-done.3
  34.6 2.6 %shard_map.112 = bf16[128,2,768]{2,1,0:T(2,128)(2,1)S(1)} custom-call(bf16[112,4,768]{2,1,0:T(4,128)(2,1)S(1)} %bitcast.10, bf16[256,448]{1,0:T(8,128)(2,1)S(1)} %copy-done.3, bf16[768,2304]{1,0:T(8,128)(2,1)S(1)} %copy-done, bf16[768,768]{1,0:T(8,128)(2,1)S(1)} %copy-done.1, bf16[256,256]{1,0:T(8,128)(2,1)S(1)} %copy-done.6), custom_call_target="tpu_custom_call" | custom-call | flops 1207959552 | bytes 5767168 | tf_op jit(solution)/shard_map/pallas_call | solution.py:474
  37.2 18.1 %all_to_all.16.tokens_ref = bf16[128,2,768]{2,1,0:T(2,128)(2,1)S(1)} all-to-all(bf16[128,2,768]{2,1,0:T(2,128)(2,1)S(1)} %shard_map.112), channel_id=1, replica_groups=mesh['gx'=16,'gy'=8] {'gx','gy'}, dimensions={0} | all-to-all | bytes 786432 | tf_op jit(solution)/shard_map/all_to_all | solution.py:553
  55.3 0.0 slice-done
  55.3 0.0 copy-start.5
  55.3 5.3 %shard_map.113 = bf16[256,768]{1,0:T(8,128)(2,1)S(1)} custom-call(bf16[128,2,768]{2,1,0:T(2,128)(2,1)S(1)} %all_to_all.16.tokens_ref, bf16[256,256]{1,0:T(8,128)(2,1)S(1)} %copy-done.4, bf16[768,2304]{1,0:T(8,128)(2,1)S(1)} %copy-done, bf16[768,768]{1,0:T(8,128)(2,1)S(1)} %copy-done.1, bf16[768,3072]{1,0:T(8,128)(2,1)S(1)} %bitcast.6, ...), custom_call_target="tpu_custom_call" | custom-call | flops 3623878656 | bytes 14680064 | tf_op jit(solution)/shard_map/pallas_call | solution.py:474
  60.6 13.6 %all_to_all.17 = bf16[8,32,768]{2,1,0:T(8,128)(2,1)S(1)} all-to-all(bf16[8,32,768]{2,1,0:T(8,128)(2,1)S(1)} %bitcast.12), channel_id=1, replica_groups=mesh['gx'=16,'gy'=8] {'gy'}, dimensions={0} | all-to-all | bytes 786432 | tf_op jit(solution)/shard_map/all_to_all | solution.py:563
  74.2 1.0 %shard_map.114 = bf16[256,768]{1,0:T(8,128)(2,1)} custom-call(bf16[256,768]{1,0:T(8,128)(2,1)S(1)} %bitcast.11, bf16[256,256]{1,0:T(8,128)(2,1)S(1)} %copy-done.5), custom_call_target="tpu_custom_call" | custom-call | flops 100663296 | bytes 524288 | tf_op jit(solution)/shard_map/pallas_call | solution.py:474
  (15 shorter events, 0.0 us)
Async XLA Ops:
  0.0 9.1 %copy-start.7 = (bf16[2560,768]{1,0:T(8,128)(2,1)S(1)}, bf16[2560,768]{1,0:T(8,128)(2,1)}, u32[]{:S(2)}) copy-start(bf16[2560,768]{1,0:T(8,128)(2,1)} %weight_ref.1) | copy-start | bytes 11796484
  0.0 55.2 %slice-start.2 = ((s8[4718592]{0:T(1024)(128)(4,1)}), s8[524288]{0:T(1024)(128)(4,1)S(1)}, s32[]{:S(2)}) async-start(s8[4718592]{0:T(1024)(128)(4,1)} %bitcast.7), calls=%async_computation.5 | async-start | bytes 1048576
  2.8 12.0 %collective-permute-start = (f32[40,4,128]{2,1,0:T(4,128)S(1)}, f32[40,4,128]{2,1,0:T(4,128)S(1)}, u32[]{:S(2)}, u32[]{:S(2)}) collective-permute-start(f32[40,4,128]{2,1,0:T(4,128)S(1)} %get-tuple-element.12), channel_id=1, source_target_pairs={{0,1},{1,2},{2,3},{3,4},{4,5},{5,6},{6,7},{7,0},{8,9},{9,10},{10,1... | collective-permute-start | bytes 245768 | tf_op jit(solution)/shard_map/ppermute | solution.py:513
  6.8 8.0 %collective-permute-start.1 = (f32[40,4,128]{2,1,0:T(4,128)S(1)}, f32[40,4,128]{2,1,0:T(4,128)S(1)}, u32[]{:S(2)}, u32[]{:S(2)}) collective-permute-start(f32[40,4,128]{2,1,0:T(4,128)S(1)} %get-tuple-element.13), channel_id=1, source_target_pairs={{1,0},{2,1},{3,2},{4,3},{5,4},{6,5},{7,6},{0,7},{9,8},{10,9},{11,1... | collective-permute-start | bytes 245768 | tf_op jit(solution)/shard_map/ppermute | solution.py:514
  9.1 5.7 %copy-start.2 = (bf16[1152,128]{1,0:T(8,128)(2,1)S(1)}, bf16[1152,128]{1,0:T(8,128)(2,1)}, u32[]{:S(2)}) copy-start(bf16[1152,128]{1,0:T(8,128)(2,1)} %constant.10.clone.table_ref) | copy-start | bytes 884740
  9.1 46.2 %slice-start.3 = ((s8[4718592]{0:T(1024)(128)(4,1)}), s8[4194304]{0:T(1024)(128)(4,1)S(1)}, s32[]{:S(2)}) async-start(s8[4718592]{0:T(1024)(128)(4,1)} %bitcast.7), calls=%async_computation.6 | async-start | bytes 8388608
  14.7 19.9 %copy-start = (bf16[768,2304]{1,0:T(8,128)(2,1)S(1)}, bf16[768,2304]{1,0:T(8,128)(2,1)}, u32[]{:S(2)}) copy-start(bf16[768,2304]{1,0:T(8,128)(2,1)} %qkv_ref.3) | copy-start | bytes 10616836
  14.7 19.8 %copy-start.1 = (bf16[768,768]{1,0:T(8,128)(2,1)S(1)}, bf16[768,768]{1,0:T(8,128)(2,1)}, u32[]{:S(2)}) copy-start(bf16[768,768]{1,0:T(8,128)(2,1)} %outw_ref.3) | copy-start | bytes 3538948
  14.7 19.8 %copy-start.3 = (bf16[256,448]{1,0:T(8,128)(2,1)S(1)}, bf16[256,448]{1,0:T(8,128)(2,1)}, u32[]{:S(2)}) copy-start(bf16[256,448]{1,0:T(8,128)(2,1)} %constant.11.clone.sum_ref) | copy-start | bytes 688132
  14.7 19.8 %copy-start.6 = (bf16[256,256]{1,0:T(8,128)(2,1)S(1)}, bf16[256,256]{1,0:T(8,128)(2,1)}, u32[]{:S(2)}) copy-start(bf16[256,256]{1,0:T(8,128)(2,1)} %constant.12.clone.order_ref) | copy-start | bytes 393220
  14.8 40.5 %slice-start = ((s8[4718592]{0:T(1024)(128)(4,1)}), s8[4194304]{0:T(1024)(128)(4,1)S(1)}, s32[]{:S(2)}) async-start(s8[4718592]{0:T(1024)(128)(4,1)} %bitcast.5), calls=%async_computation.3 | async-start | bytes 8388608
  16.7 38.6 %slice-start.1 = ((s8[4718592]{0:T(1024)(128)(4,1)}), s8[524288]{0:T(1024)(128)(4,1)S(1)}, s32[]{:S(2)}) async-start(s8[4718592]{0:T(1024)(128)(4,1)} %bitcast.5), calls=%async_computation.4 | async-start | bytes 1048576
  16.7 38.6 %copy-start.4 = (bf16[256,256]{1,0:T(8,128)(2,1)S(1)}, bf16[256,256]{1,0:T(8,128)(2,1)}, u32[]{:S(2)}) copy-start(bf16[256,256]{1,0:T(8,128)(2,1)} %constant.13.clone.split_ref) | copy-start | bytes 393220
  55.3 18.9 %copy-start.5 = (bf16[256,256]{1,0:T(8,128)(2,1)S(1)}, bf16[256,256]{1,0:T(8,128)(2,1)}, u32[]{:S(2)}) copy-start(bf16[256,256]{1,0:T(8,128)(2,1)} %constant.14.clone.order_ref) | copy-start | bytes 393220

commit v8 on v7

--- a/solution.py
+++ b/solution.py
@@ -179,6 +179,10 @@
         strip(32 + c, smooth_ref[NF - 1, :, PADX + c * 8 : PADX + c * 8 + 8, :])
 
 
+CHUNKS = (0, 2, 1)
+STRIDE = 2
+
+
 def main_kernel(
     smooth_ref,
     weight_ref,
@@ -199,19 +203,20 @@
     edge_ref[...] = jnp.zeros_like(edge_ref)
 
     def filtered(f):
-        for z in range(ZS):
-            total = float(TAPS[R]) * smooth_ref[f, z, PADX - 8 : PADX + 72, :]
-            for k in range(1, R + 1):
-                total = total + float(TAPS[R + k]) * (
-                    smooth_ref[f, z, PADX - 8 - k : PADX + 72 - k, :]
-                    + smooth_ref[f, z, PADX - 8 + k : PADX + 72 + k, :]
-                )
-            across[f, z] = total
         for part in range(4):
             planes = slice(part * 4, part * 4 + 4)
+            for z in range(part * 4, part * 4 + 4):
+                total = float(TAPS[R]) * smooth_ref[f, z, PADX - 8 : PADX + 72, :]
+                for k in range(1, R + 1):
+                    total = total + float(TAPS[R + k]) * (
+                        smooth_ref[f, z, PADX - 8 - k : PADX + 72 - k, :]
+                        + smooth_ref[f, z, PADX - 8 + k : PADX + 72 + k, :]
+                    )
+                across[f, z] = total
             high, low = halves(across[f, planes].reshape(320, CY))
             pair = dot(jnp.concatenate([high, low], 1), band)
             along[f, planes] = (pair[:, :CY] + pair[:, CY:]).reshape(4, 80, CY)
+            yield
 
     def reordered(f):
         for tile in (2 * f, 2 * f + 1):
@@ -222,6 +227,7 @@
                 else:
                     start = 2048 + y * 64 + (tile - 8) * 32
                 order_ref[start : start + 32, :] = turned[y * 32 : y * 32 + 32]
+            yield
 
     def put(ext, a, start, side, place, values):
         high = values.astype(bf16)
@@ -235,10 +241,11 @@
             row = ext * 2 + a
             edge_ref[side * 10 + place, row : row + 1, :] = rest[side * 15 : side * 15 + 1]
 
-    for chunk, members in enumerate(((0, 1), (2, 3), (4,))):
+    def produce(chunk):
+        members = range(chunk * 2, min(chunk * 2 + 2, NF))
         for f in members:
-            filtered(f)
-            reordered(f)
+            yield from filtered(f)
+            yield from reordered(f)
         for ext in range(EXT):
             rows = slice(ext * 8, ext * 8 + 8)
             if len(members) == 2:
@@ -257,11 +264,26 @@
                     start, place = 2048 + m * 128, 8 + m % 2
                     put(ext, 0, start, m // 2, place, jnp.where(first, even, pltpu.roll(odd, 64, 1)))
                     put(ext, 1, start, m // 2, place, jnp.where(first, pltpu.roll(even, 64, 1), odd))
+            yield
+
+    def consume(chunk, fresh):
         deep = slice(chunk * 1024, min(chunk * 1024 + 1024, KIN))
         for tile in range(3):
             columns = slice(tile * 256, tile * 256 + 256)
-            part = dot(lhs[:, deep], order_ref[deep, columns])
-            both[:, columns] = part if chunk == 0 else both[:, columns] + part
+            for rows in (slice(0, ALL_ROWS // 2), slice(ALL_ROWS // 2, ALL_ROWS)):
+                part = dot(lhs[rows, deep], order_ref[deep, columns])
+                both[rows, columns] = part if fresh else both[rows, columns] + part
+                yield
+
+    for _ in produce(CHUNKS[0]):
+        pass
+    for n, chunk in enumerate(CHUNKS):
+        ahead = produce(CHUNKS[n + 1]) if n + 1 < len(CHUNKS) else iter(())
+        for _ in consume(chunk, n == 0):
+            for _ in range(STRIDE):
+                next(ahead, None)
+        for _ in ahead:
+            pass
     for tile in range(6):
         columns = slice(tile * 128, tile * 128 + 128)
         for start, low in ((0, HI_ROWS), (256, HI_ROWS + 64)):

time: 75.4 us -> 75.2 us (level)
  no operation moved by 1% of the time
where the time goes in v8:
time: 75.2 us; the launch traced here: 75 us
  blocking collectives  49.5 us (66%)
  Pallas kernels  18.9 us (25%)
  starting transfers between devices  6.31 us (8%)
    all_to_all x1, blocking collectives, shards(): lax.all_to_all(tokens, ('gx', 'gy'), split_axis=0, concat_axis=0, tiled=T...  18.1 us
    all_to_all x1, blocking collectives, shards(): lax.all_to_all(slots.reshape(NXL, SLOTS // 4, 4, D), 'gx', split_axis=0,...  17.9 us
    pallas_call x5, Pallas kernels, call(): pl.pallas_call(kernel, out_shape=out_shape, in_specs=[space] * len(operan...  16.2 us
    all_to_all x1, blocking collectives, shards(): lax.all_to_all(tokens.reshape(8, 32, D), 'gy', split_axis=0, concat_axis=...  13.6 us
    ppermute x1, starting transfers between devices, shards(): lax.ppermute(upper, 'gy', [(i, (i + 1) % count) for i in range(count)])  4.03 us
    pallas_call x1, Pallas kernels, prepare(): pl.pallas_call(prep_kernel, in_specs=[pl.BlockSpec(memory_space=pltpu.HBM...  2.76 us
    ppermute x1, starting transfers between devices, shards(): lax.ppermute(lower, 'gy', [((i + 1) % count, i) for i in range(count)])  2.28 us
  transfers between devices with their start and end apart: 2, of which 0 were waited for; matrix products, arithmetic and copies ran while one was open for 0% of the time, Pallas kernels for 7%

profile of v8, /device:TPU:0, one launch (start us, length us, event | category | flops | bytes accessed | tf_op | source)
XLA Modules:
  0.0 75.0 jit_solution(2540766662933839547)
XLA Ops:
  0.0 2.8 %shard_map.109 = (f32[5,16,96,128]{3,2,1,0:T(8,128)S(1)}, f32[40,4,128]{2,1,0:T(4,128)S(1)}, f32[40,4,128]{2,1,0:T(4,128)S(1)}) custom-call(f32[5,24,64,128]{3,2,1,0:T(8,128)} %fields_ref.1), custom_call_target="tpu_custom_call" | custom-call | tf_op jit(solution)/shard_map/pallas_call | solution.py:515
  2.8 4.0 %collective-permute-start = (f32[40,4,128]{2,1,0:T(4,128)S(1)}, f32[40,4,128]{2,1,0:T(4,128)S(1)}, u32[]{:S(2)}, u32[]{:S(2)}) collective-permute-start(f32[40,4,128]{2,1,0:T(4,128)S(1)} %get-tuple-element.12), channel_id=1, source_target_pairs={{0,1},{1,2},{2,3},{3,4},{4,5},{5,6},{6,7},{7,0},{8,9},{9,10},{10,1... | collective-permute-start | bytes 245768 | tf_op jit(solution)/shard_map/ppermute | solution.py:535
  6.8 2.3 %collective-permute-start.1 = (f32[40,4,128]{2,1,0:T(4,128)S(1)}, f32[40,4,128]{2,1,0:T(4,128)S(1)}, u32[]{:S(2)}, u32[]{:S(2)}) collective-permute-start(f32[40,4,128]{2,1,0:T(4,128)S(1)} %get-tuple-element.13), channel_id=1, source_target_pairs={{1,0},{2,1},{3,2},{4,3},{5,4},{6,5},{7,6},{0,7},{9,8},{10,9},{11,1... | collective-permute-start | bytes 245768 | tf_op jit(solution)/shard_map/ppermute | solution.py:536
  9.1 5.4 %shard_map.110 = (bf16[112,4,768]{2,1,0:T(4,128)(2,1)S(1)}, f32[2,24,768]{2,1,0:T(8,128)S(1)}, f32[20,24,128]{2,1,0:T(8,128)S(1)}, bf16[2560,768]{1,0:T(8,128)(2,1)S(1)}) custom-call(f32[5,16,96,128]{3,2,1,0:T(8,128)S(1)} %get-tuple-element.14.smooth_ref, bf16[2560,768]{1,0:T(8,128)(2,1)S(1)} %copy-done.7), custom_call_target="tpu_custom_call" | custom-call | flops 3607101440 | bytes 7864320 | tf_op jit(solution)/shard_map/pallas_call | solution.py:496
  14.5 0.0 copy-start
  14.5 0.0 copy-start.1
  14.5 0.0 copy-start.3
  14.5 0.0 copy-start.6
  14.5 0.0 collective-permute-done.upper_ref
  14.6 0.0 collective-permute-done.1.lower_ref
  14.6 0.0 copy-done.2
  14.6 0.0 slice-start
  14.6 1.9 %shard_map.111 = bf16[112,4,768]{2,1,0:T(4,128)(2,1)S(1)} custom-call(f32[40,4,128]{2,1,0:T(4,128)S(1)} %collective-permute-done.upper_ref, f32[40,4,128]{2,1,0:T(4,128)S(1)} %collective-permute-done.1.lower_ref, bf16[1152,128]{1,0:T(8,128)(2,1)S(1)} %copy-done.2, f32[20,24,128]{2,1,0:T(8,128)S(1)} %get-tuple-element.15.edge_ref, ...), custom_call_target="tpu_custom_call" | custom-call | flops 251658240 | bytes 5472256 | tf_op jit(solution)/shard_map/pallas_call | solution.py:496
  16.5 0.0 slice-start.1
  16.5 0.0 copy-start.4
  16.5 17.9 %all_to_all.15 = bf16[16,7,4,768]{3,2,1,0:T(4,128)(2,1)S(1)} all-to-all(bf16[16,7,4,768]{3,2,1,0:T(4,128)(2,1)S(1)} %bitcast.9), channel_id=1, replica_groups=mesh['gx'=16,'gy'=8] {'gx'}, dimensions={0} | all-to-all | bytes 1376256 | tf_op jit(solution)/shard_map/all_to_all | solution.py:564
  34.4 0.0 copy-done
  34.4 2.6 %shard_map.112 = bf16[128,2,768]{2,1,0:T(2,128)(2,1)S(1)} custom-call(bf16[112,4,768]{2,1,0:T(4,128)(2,1)S(1)} %bitcast.10, bf16[256,448]{1,0:T(8,128)(2,1)S(1)} %copy-done.3, bf16[768,2304]{1,0:T(8,128)(2,1)S(1)} %copy-done, bf16[768,768]{1,0:T(8,128)(2,1)S(1)} %copy-done.1, bf16[256,256]{1,0:T(8,128)(2,1)S(1)} %copy-done.6), custom_call_target="tpu_custom_call" | custom-call | flops 1207959552 | bytes 5767168 | tf_op jit(solution)/shard_map/pallas_call | solution.py:496
  37.0 18.1 %all_to_all.16.tokens_ref = bf16[128,2,768]{2,1,0:T(2,128)(2,1)S(1)} all-to-all(bf16[128,2,768]{2,1,0:T(2,128)(2,1)S(1)} %shard_map.112), channel_id=1, replica_groups=mesh['gx'=16,'gy'=8] {'gx','gy'}, dimensions={0} | all-to-all | bytes 786432 | tf_op jit(solution)/shard_map/all_to_all | solution.py:575
  55.0 0.0 slice-done.3
  55.1 0.0 copy-start.5
  55.1 5.3 %shard_map.113 = bf16[256,768]{1,0:T(8,128)(2,1)S(1)} custom-call(bf16[128,2,768]{2,1,0:T(2,128)(2,1)S(1)} %all_to_all.16.tokens_ref, bf16[256,256]{1,0:T(8,128)(2,1)S(1)} %copy-done.4, bf16[768,2304]{1,0:T(8,128)(2,1)S(1)} %copy-done, bf16[768,768]{1,0:T(8,128)(2,1)S(1)} %copy-done.1, bf16[768,3072]{1,0:T(8,128)(2,1)S(1)} %bitcast.6, ...), custom_call_target="tpu_custom_call" | custom-call | flops 3623878656 | bytes 14680064 | tf_op jit(solution)/shard_map/pallas_call | solution.py:496
  60.4 13.6 %all_to_all.17 = bf16[8,32,768]{2,1,0:T(8,128)(2,1)S(1)} all-to-all(bf16[8,32,768]{2,1,0:T(8,128)(2,1)S(1)} %bitcast.12), channel_id=1, replica_groups=mesh['gx'=16,'gy'=8] {'gy'}, dimensions={0} | all-to-all | bytes 786432 | tf_op jit(solution)/shard_map/all_to_all | solution.py:585
  74.0 1.0 %shard_map.114 = bf16[256,768]{1,0:T(8,128)(2,1)} custom-call(bf16[256,768]{1,0:T(8,128)(2,1)S(1)} %bitcast.11, bf16[256,256]{1,0:T(8,128)(2,1)S(1)} %copy-done.5), custom_call_target="tpu_custom_call" | custom-call | flops 100663296 | bytes 524288 | tf_op jit(solution)/shard_map/pallas_call | solution.py:496
  (15 shorter events, 0.0 us)
Async XLA Ops:
  0.0 9.1 %copy-start.7 = (bf16[2560,768]{1,0:T(8,128)(2,1)S(1)}, bf16[2560,768]{1,0:T(8,128)(2,1)}, u32[]{:S(2)}) copy-start(bf16[2560,768]{1,0:T(8,128)(2,1)} %weight_ref.1) | copy-start | bytes 11796484
  0.0 55.0 %slice-start.2 = ((s8[4718592]{0:T(1024)(128)(4,1)}), s8[524288]{0:T(1024)(128)(4,1)S(1)}, s32[]{:S(2)}) async-start(s8[4718592]{0:T(1024)(128)(4,1)} %bitcast.7), calls=%async_computation.5 | async-start | bytes 1048576
  2.8 11.8 %collective-permute-start = (f32[40,4,128]{2,1,0:T(4,128)S(1)}, f32[40,4,128]{2,1,0:T(4,128)S(1)}, u32[]{:S(2)}, u32[]{:S(2)}) collective-permute-start(f32[40,4,128]{2,1,0:T(4,128)S(1)} %get-tuple-element.12), channel_id=1, source_target_pairs={{0,1},{1,2},{2,3},{3,4},{4,5},{5,6},{6,7},{7,0},{8,9},{9,10},{10,1... | collective-permute-start | bytes 245768 | tf_op jit(solution)/shard_map/ppermute | solution.py:535
  6.8 7.8 %collective-permute-start.1 = (f32[40,4,128]{2,1,0:T(4,128)S(1)}, f32[40,4,128]{2,1,0:T(4,128)S(1)}, u32[]{:S(2)}, u32[]{:S(2)}) collective-permute-start(f32[40,4,128]{2,1,0:T(4,128)S(1)} %get-tuple-element.13), channel_id=1, source_target_pairs={{1,0},{2,1},{3,2},{4,3},{5,4},{6,5},{7,6},{0,7},{9,8},{10,9},{11,1... | collective-permute-start | bytes 245768 | tf_op jit(solution)/shard_map/ppermute | solution.py:536
  9.1 5.5 %copy-start.2 = (bf16[1152,128]{1,0:T(8,128)(2,1)S(1)}, bf16[1152,128]{1,0:T(8,128)(2,1)}, u32[]{:S(2)}) copy-start(bf16[1152,128]{1,0:T(8,128)(2,1)} %constant.10.clone.table_ref) | copy-start | bytes 884740
  9.1 46.0 %slice-start.3 = ((s8[4718592]{0:T(1024)(128)(4,1)}), s8[4194304]{0:T(1024)(128)(4,1)S(1)}, s32[]{:S(2)}) async-start(s8[4718592]{0:T(1024)(128)(4,1)} %bitcast.7), calls=%async_computation.6 | async-start | bytes 8388608
  14.5 19.9 %copy-start = (bf16[768,2304]{1,0:T(8,128)(2,1)S(1)}, bf16[768,2304]{1,0:T(8,128)(2,1)}, u32[]{:S(2)}) copy-start(bf16[768,2304]{1,0:T(8,128)(2,1)} %qkv_ref.3) | copy-start | bytes 10616836
  14.5 19.8 %copy-start.1 = (bf16[768,768]{1,0:T(8,128)(2,1)S(1)}, bf16[768,768]{1,0:T(8,128)(2,1)}, u32[]{:S(2)}) copy-start(bf16[768,768]{1,0:T(8,128)(2,1)} %outw_ref.3) | copy-start | bytes 3538948
  14.5 19.8 %copy-start.3 = (bf16[256,448]{1,0:T(8,128)(2,1)S(1)}, bf16[256,448]{1,0:T(8,128)(2,1)}, u32[]{:S(2)}) copy-start(bf16[256,448]{1,0:T(8,128)(2,1)} %constant.11.clone.sum_ref) | copy-start | bytes 688132
  14.5 19.8 %copy-start.6 = (bf16[256,256]{1,0:T(8,128)(2,1)S(1)}, bf16[256,256]{1,0:T(8,128)(2,1)}, u32[]{:S(2)}) copy-start(bf16[256,256]{1,0:T(8,128)(2,1)} %constant.12.clone.order_ref) | copy-start | bytes 393220
  14.6 40.5 %slice-start = ((s8[4718592]{0:T(1024)(128)(4,1)}), s8[4194304]{0:T(1024)(128)(4,1)S(1)}, s32[]{:S(2)}) async-start(s8[4718592]{0:T(1024)(128)(4,1)} %bitcast.5), calls=%async_computation.3 | async-start | bytes 8388608
  16.5 38.6 %slice-start.1 = ((s8[4718592]{0:T(1024)(128)(4,1)}), s8[524288]{0:T(1024)(128)(4,1)S(1)}, s32[]{:S(2)}) async-start(s8[4718592]{0:T(1024)(128)(4,1)} %bitcast.5), calls=%async_computation.4 | async-start | bytes 1048576
  16.5 38.6 %copy-start.4 = (bf16[256,256]{1,0:T(8,128)(2,1)S(1)}, bf16[256,256]{1,0:T(8,128)(2,1)}, u32[]{:S(2)}) copy-start(bf16[256,256]{1,0:T(8,128)(2,1)} %constant.13.clone.split_ref) | copy-start | bytes 393220
  55.1 18.9 %copy-start.5 = (bf16[256,256]{1,0:T(8,128)(2,1)S(1)}, bf16[256,256]{1,0:T(8,128)(2,1)}, u32[]{:S(2)}) copy-start(bf16[256,256]{1,0:T(8,128)(2,1)} %constant.14.clone.order_ref) | copy-start | bytes 393220

commit v9 on v8

--- a/solution.py
+++ b/solution.py
@@ -190,7 +190,6 @@
     base_ref,
     edge_ref,
     order_ref,
-    across,
     along,
     lhs,
     both,
@@ -203,19 +202,20 @@
     edge_ref[...] = jnp.zeros_like(edge_ref)
 
     def filtered(f):
-        for part in range(4):
-            planes = slice(part * 4, part * 4 + 4)
-            for z in range(part * 4, part * 4 + 4):
+        for part in range(8):
+            planes = slice(part * 2, part * 2 + 2)
+            found = []
+            for z in range(part * 2, part * 2 + 2):
                 total = float(TAPS[R]) * smooth_ref[f, z, PADX - 8 : PADX + 72, :]
                 for k in range(1, R + 1):
                     total = total + float(TAPS[R + k]) * (
                         smooth_ref[f, z, PADX - 8 - k : PADX + 72 - k, :]
                         + smooth_ref[f, z, PADX - 8 + k : PADX + 72 + k, :]
                     )
-                across[f, z] = total
-            high, low = halves(across[f, planes].reshape(320, CY))
+                found.append(total)
+            high, low = halves(jnp.concatenate(found, 0))
             pair = dot(jnp.concatenate([high, low], 1), band)
-            along[f, planes] = (pair[:, :CY] + pair[:, CY:]).reshape(4, 80, CY)
+            along[f, planes] = (pair[:, :CY] + pair[:, CY:]).reshape(2, 80, CY)
             yield
 
     def reordered(f):
@@ -540,7 +540,6 @@
         [slots, like((2, 24, D), f32), like((20, 24, 128), f32), like((KIN, D))],
         [
             pltpu.VMEM((NF, ZS, 80, CY), f32),
-            pltpu.VMEM((NF, ZS, 80, CY), f32),
             pltpu.VMEM((ALL_ROWS, KIN), bf16),
             pltpu.VMEM((ALL_ROWS, D), f32),
             pltpu.VMEM((6, HI_ROWS, 128), f32),

time: 75.2 us -> 75.1 us (level)
  no operation moved by 1% of the time
where the time goes in v9:
time: 75.1 us; the launch traced here: 74.9 us
  blocking collectives  49.5 us (66%)
  Pallas kernels  18.8 us (25%)
  starting transfers between devices  6.31 us (8%)
    all_to_all x1, blocking collectives, shards(): lax.all_to_all(tokens, ('gx', 'gy'), split_axis=0, concat_axis=0, tiled=T...  18.1 us
    all_to_all x1, blocking collectives, shards(): lax.all_to_all(slots.reshape(NXL, SLOTS // 4, 4, D), 'gx', split_axis=0,...  17.9 us
    pallas_call x5, Pallas kernels, call(): pl.pallas_call(kernel, out_shape=out_shape, in_specs=[space] * len(operan...  16 us
    all_to_all x1, blocking collectives, shards(): lax.all_to_all(tokens.reshape(8, 32, D), 'gy', split_axis=0, concat_axis=...  13.6 us
    ppermute x1, starting transfers between devices, shards(): lax.ppermute(upper, 'gy', [(i, (i + 1) % count) for i in range(count)])  4.03 us
    pallas_call x1, Pallas kernels, prepare(): pl.pallas_call(prep_kernel, in_specs=[pl.BlockSpec(memory_space=pltpu.HBM...  2.76 us
    ppermute x1, starting transfers between devices, shards(): lax.ppermute(lower, 'gy', [((i + 1) % count, i) for i in range(count)])  2.28 us
  transfers between devices with their start and end apart: 2, of which 0 were waited for; matrix products, arithmetic and copies ran while one was open for 0% of the time, Pallas kernels for 7%

profile of v9, /device:TPU:0, one launch (start us, length us, event | category | flops | bytes accessed | tf_op | source)
XLA Modules:
  0.0 74.9 jit_solution(7055199825233460245)
XLA Ops:
  0.0 2.8 %shard_map.109 = (f32[5,16,96,128]{3,2,1,0:T(8,128)S(1)}, f32[40,4,128]{2,1,0:T(4,128)S(1)}, f32[40,4,128]{2,1,0:T(4,128)S(1)}) custom-call(f32[5,24,64,128]{3,2,1,0:T(8,128)} %fields_ref.1), custom_call_target="tpu_custom_call" | custom-call | tf_op jit(solution)/shard_map/pallas_call | solution.py:515
  2.8 4.0 %collective-permute-start = (f32[40,4,128]{2,1,0:T(4,128)S(1)}, f32[40,4,128]{2,1,0:T(4,128)S(1)}, u32[]{:S(2)}, u32[]{:S(2)}) collective-permute-start(f32[40,4,128]{2,1,0:T(4,128)S(1)} %get-tuple-element.12), channel_id=1, source_target_pairs={{0,1},{1,2},{2,3},{3,4},{4,5},{5,6},{6,7},{7,0},{8,9},{9,10},{10,1... | collective-permute-start | bytes 245768 | tf_op jit(solution)/shard_map/ppermute | solution.py:535
  6.8 2.3 %collective-permute-start.1 = (f32[40,4,128]{2,1,0:T(4,128)S(1)}, f32[40,4,128]{2,1,0:T(4,128)S(1)}, u32[]{:S(2)}, u32[]{:S(2)}) collective-permute-start(f32[40,4,128]{2,1,0:T(4,128)S(1)} %get-tuple-element.13), channel_id=1, source_target_pairs={{1,0},{2,1},{3,2},{4,3},{5,4},{6,5},{7,6},{0,7},{9,8},{10,9},{11,1... | collective-permute-start | bytes 245768 | tf_op jit(solution)/shard_map/ppermute | solution.py:536
  9.1 0.0 copy-done.7
  9.1 5.3 %shard_map.110 = (bf16[112,4,768]{2,1,0:T(4,128)(2,1)S(1)}, f32[2,24,768]{2,1,0:T(8,128)S(1)}, f32[20,24,128]{2,1,0:T(8,128)S(1)}, bf16[2560,768]{1,0:T(8,128)(2,1)S(1)}) custom-call(f32[5,16,96,128]{3,2,1,0:T(8,128)S(1)} %get-tuple-element.14.smooth_ref, bf16[2560,768]{1,0:T(8,128)(2,1)S(1)} %copy-done.7), custom_call_target="tpu_custom_call" | custom-call | flops 3607101440 | bytes 7864320 | tf_op jit(solution)/shard_map/pallas_call | solution.py:496
  14.4 0.0 copy-start
  14.4 0.0 copy-start.1
  14.4 0.0 copy-start.3
  14.4 0.0 copy-start.6
  14.4 0.0 collective-permute-done.upper_ref
  14.4 0.0 collective-permute-done.1.lower_ref
  14.4 0.0 copy-done.2
  14.5 0.0 slice-start
  14.5 1.9 %shard_map.111 = bf16[112,4,768]{2,1,0:T(4,128)(2,1)S(1)} custom-call(f32[40,4,128]{2,1,0:T(4,128)S(1)} %collective-permute-done.upper_ref, f32[40,4,128]{2,1,0:T(4,128)S(1)} %collective-permute-done.1.lower_ref, bf16[1152,128]{1,0:T(8,128)(2,1)S(1)} %copy-done.2, f32[20,24,128]{2,1,0:T(8,128)S(1)} %get-tuple-element.15.edge_ref, ...), custom_call_target="tpu_custom_call" | custom-call | flops 251658240 | bytes 5472256 | tf_op jit(solution)/shard_map/pallas_call | solution.py:496
  16.3 0.0 slice-start.1
  16.3 0.0 copy-start.4
  16.4 17.9 %all_to_all.15 = bf16[16,7,4,768]{3,2,1,0:T(4,128)(2,1)S(1)} all-to-all(bf16[16,7,4,768]{3,2,1,0:T(4,128)(2,1)S(1)} %bitcast.9), channel_id=1, replica_groups=mesh['gx'=16,'gy'=8] {'gx'}, dimensions={0} | all-to-all | bytes 1376256 | tf_op jit(solution)/shard_map/all_to_all | solution.py:563
  34.2 2.6 %shard_map.112 = bf16[128,2,768]{2,1,0:T(2,128)(2,1)S(1)} custom-call(bf16[112,4,768]{2,1,0:T(4,128)(2,1)S(1)} %bitcast.10, bf16[256,448]{1,0:T(8,128)(2,1)S(1)} %copy-done.3, bf16[768,2304]{1,0:T(8,128)(2,1)S(1)} %copy-done, bf16[768,768]{1,0:T(8,128)(2,1)S(1)} %copy-done.1, bf16[256,256]{1,0:T(8,128)(2,1)S(1)} %copy-done.6), custom_call_target="tpu_custom_call" | custom-call | flops 1207959552 | bytes 5767168 | tf_op jit(solution)/shard_map/pallas_call | solution.py:496
  36.8 18.1 %all_to_all.16.tokens_ref = bf16[128,2,768]{2,1,0:T(2,128)(2,1)S(1)} all-to-all(bf16[128,2,768]{2,1,0:T(2,128)(2,1)S(1)} %shard_map.112), channel_id=1, replica_groups=mesh['gx'=16,'gy'=8] {'gx','gy'}, dimensions={0} | all-to-all | bytes 786432 | tf_op jit(solution)/shard_map/all_to_all | solution.py:574
  54.9 0.0 slice-done.2
  55.0 0.0 copy-start.5
  55.0 5.3 %shard_map.113 = bf16[256,768]{1,0:T(8,128)(2,1)S(1)} custom-call(bf16[128,2,768]{2,1,0:T(2,128)(2,1)S(1)} %all_to_all.16.tokens_ref, bf16[256,256]{1,0:T(8,128)(2,1)S(1)} %copy-done.4, bf16[768,2304]{1,0:T(8,128)(2,1)S(1)} %copy-done, bf16[768,768]{1,0:T(8,128)(2,1)S(1)} %copy-done.1, bf16[768,3072]{1,0:T(8,128)(2,1)S(1)} %bitcast.6, ...), custom_call_target="tpu_custom_call" | custom-call | flops 3623878656 | bytes 14680064 | tf_op jit(solution)/shard_map/pallas_call | solution.py:496
  60.3 13.6 %all_to_all.17 = bf16[8,32,768]{2,1,0:T(8,128)(2,1)S(1)} all-to-all(bf16[8,32,768]{2,1,0:T(8,128)(2,1)S(1)} %bitcast.12), channel_id=1, replica_groups=mesh['gx'=16,'gy'=8] {'gy'}, dimensions={0} | all-to-all | bytes 786432 | tf_op jit(solution)/shard_map/all_to_all | solution.py:584
  73.9 1.0 %shard_map.114 = bf16[256,768]{1,0:T(8,128)(2,1)} custom-call(bf16[256,768]{1,0:T(8,128)(2,1)S(1)} %bitcast.11, bf16[256,256]{1,0:T(8,128)(2,1)S(1)} %copy-done.5), custom_call_target="tpu_custom_call" | custom-call | flops 100663296 | bytes 524288 | tf_op jit(solution)/shard_map/pallas_call | solution.py:496
  (15 shorter events, 0.0 us)
Async XLA Ops:
  0.0 9.1 %copy-start.7 = (bf16[2560,768]{1,0:T(8,128)(2,1)S(1)}, bf16[2560,768]{1,0:T(8,128)(2,1)}, u32[]{:S(2)}) copy-start(bf16[2560,768]{1,0:T(8,128)(2,1)} %weight_ref.1) | copy-start | bytes 11796484
  0.0 54.9 %slice-start.2 = ((s8[4718592]{0:T(1024)(128)(4,1)}), s8[524288]{0:T(1024)(128)(4,1)S(1)}, s32[]{:S(2)}) async-start(s8[4718592]{0:T(1024)(128)(4,1)} %bitcast.7), calls=%async_computation.5 | async-start | bytes 1048576
  2.8 11.6 %collective-permute-start = (f32[40,4,128]{2,1,0:T(4,128)S(1)}, f32[40,4,128]{2,1,0:T(4,128)S(1)}, u32[]{:S(2)}, u32[]{:S(2)}) collective-permute-start(f32[40,4,128]{2,1,0:T(4,128)S(1)} %get-tuple-element.12), channel_id=1, source_target_pairs={{0,1},{1,2},{2,3},{3,4},{4,5},{5,6},{6,7},{7,0},{8,9},{9,10},{10,1... | collective-permute-start | bytes 245768 | tf_op jit(solution)/shard_map/ppermute | solution.py:535
  6.8 7.6 %collective-permute-start.1 = (f32[40,4,128]{2,1,0:T(4,128)S(1)}, f32[40,4,128]{2,1,0:T(4,128)S(1)}, u32[]{:S(2)}, u32[]{:S(2)}) collective-permute-start(f32[40,4,128]{2,1,0:T(4,128)S(1)} %get-tuple-element.13), channel_id=1, source_target_pairs={{1,0},{2,1},{3,2},{4,3},{5,4},{6,5},{7,6},{0,7},{9,8},{10,9},{11,1... | collective-permute-start | bytes 245768 | tf_op jit(solution)/shard_map/ppermute | solution.py:536
  9.1 5.4 %copy-start.2 = (bf16[1152,128]{1,0:T(8,128)(2,1)S(1)}, bf16[1152,128]{1,0:T(8,128)(2,1)}, u32[]{:S(2)}) copy-start(bf16[1152,128]{1,0:T(8,128)(2,1)} %constant.10.clone.table_ref) | copy-start | bytes 884740
  9.1 45.8 %slice-start.3 = ((s8[4718592]{0:T(1024)(128)(4,1)}), s8[4194304]{0:T(1024)(128)(4,1)S(1)}, s32[]{:S(2)}) async-start(s8[4718592]{0:T(1024)(128)(4,1)} %bitcast.7), calls=%async_computation.6 | async-start | bytes 8388608
  14.4 19.9 %copy-start = (bf16[768,2304]{1,0:T(8,128)(2,1)S(1)}, bf16[768,2304]{1,0:T(8,128)(2,1)}, u32[]{:S(2)}) copy-start(bf16[768,2304]{1,0:T(8,128)(2,1)} %qkv_ref.3) | copy-start | bytes 10616836
  14.4 19.8 %copy-start.1 = (bf16[768,768]{1,0:T(8,128)(2,1)S(1)}, bf16[768,768]{1,0:T(8,128)(2,1)}, u32[]{:S(2)}) copy-start(bf16[768,768]{1,0:T(8,128)(2,1)} %outw_ref.3) | copy-start | bytes 3538948
  14.4 19.8 %copy-start.3 = (bf16[256,448]{1,0:T(8,128)(2,1)S(1)}, bf16[256,448]{1,0:T(8,128)(2,1)}, u32[]{:S(2)}) copy-start(bf16[256,448]{1,0:T(8,128)(2,1)} %constant.11.clone.sum_ref) | copy-start | bytes 688132
  14.4 19.8 %copy-start.6 = (bf16[256,256]{1,0:T(8,128)(2,1)S(1)}, bf16[256,256]{1,0:T(8,128)(2,1)}, u32[]{:S(2)}) copy-start(bf16[256,256]{1,0:T(8,128)(2,1)} %constant.12.clone.order_ref) | copy-start | bytes 393220
  14.5 40.5 %slice-start = ((s8[4718592]{0:T(1024)(128)(4,1)}), s8[4194304]{0:T(1024)(128)(4,1)S(1)}, s32[]{:S(2)}) async-start(s8[4718592]{0:T(1024)(128)(4,1)} %bitcast.5), calls=%async_computation.3 | async-start | bytes 8388608
  16.3 38.6 %slice-start.1 = ((s8[4718592]{0:T(1024)(128)(4,1)}), s8[524288]{0:T(1024)(128)(4,1)S(1)}, s32[]{:S(2)}) async-start(s8[4718592]{0:T(1024)(128)(4,1)} %bitcast.5), calls=%async_computation.4 | async-start | bytes 1048576
  16.3 38.6 %copy-start.4 = (bf16[256,256]{1,0:T(8,128)(2,1)S(1)}, bf16[256,256]{1,0:T(8,128)(2,1)}, u32[]{:S(2)}) copy-start(bf16[256,256]{1,0:T(8,128)(2,1)} %constant.13.clone.split_ref) | copy-start | bytes 393220
  55.0 18.9 %copy-start.5 = (bf16[256,256]{1,0:T(8,128)(2,1)S(1)}, bf16[256,256]{1,0:T(8,128)(2,1)}, u32[]{:S(2)}) copy-start(bf16[256,256]{1,0:T(8,128)(2,1)} %constant.14.clone.order_ref) | copy-start | bytes 393220

commit v10 on v9

--- a/solution.py
+++ b/solution.py
@@ -73,7 +73,8 @@
                 source = x + k + 8
                 table[source // 8 * 128 + group * 8 + source % 8, group * 8 + x] = TAPS[R + k]
     high, low = split_np(table)
-    return np.concatenate([high, high, low], 0)
+    right = np.concatenate([low, np.zeros_like(low)], 0)
+    return np.concatenate([np.concatenate([high, high], 0), right], 1)
 
 
 def weight_order():
@@ -341,7 +342,8 @@
             )
         )
     high, low = halves(jnp.concatenate(blocks, 0))
-    parts[...] = dot(jnp.concatenate([high, low, high], 1), table_ref[...])
+    pair = dot(jnp.concatenate([high, low], 1), table_ref[...])
+    parts[...] = pair[:, :128] + pair[:, 128:]
     last = parts[320:]
     first = lax.broadcasted_iota(jnp.int32, (80, 128), 1) < 64
     rolled = pltpu.roll(last, 64, 1)

time: 75.1 us -> 74.8 us (level)
  no operation moved by 1% of the time
where the time goes in v10:
time: 74.8 us; the launch traced here: 74.6 us
  blocking collectives  49.5 us (66%)
  Pallas kernels  18.5 us (25%)
  starting transfers between devices  6.31 us (8%)
    all_to_all x1, blocking collectives, shards(): lax.all_to_all(tokens, ('gx', 'gy'), split_axis=0, concat_axis=0, tiled=T...  18.1 us
    all_to_all x1, blocking collectives, shards(): lax.all_to_all(slots.reshape(NXL, SLOTS // 4, 4, D), 'gx', split_axis=0,...  17.9 us
    pallas_call x5, Pallas kernels, call(): pl.pallas_call(kernel, out_shape=out_shape, in_specs=[space] * len(operan...  15.7 us
    all_to_all x1, blocking collectives, shards(): lax.all_to_all(tokens.reshape(8, 32, D), 'gy', split_axis=0, concat_axis=...  13.6 us
    ppermute x1, starting transfers between devices, shards(): lax.ppermute(upper, 'gy', [(i, (i + 1) % count) for i in range(count)])  4.03 us
    pallas_call x1, Pallas kernels, prepare(): pl.pallas_call(prep_kernel, in_specs=[pl.BlockSpec(memory_space=pltpu.HBM...  2.76 us
    ppermute x1, starting transfers between devices, shards(): lax.ppermute(lower, 'gy', [((i + 1) % count, i) for i in range(count)])  2.28 us
  transfers between devices with their start and end apart: 2, of which 0 were waited for; matrix products, arithmetic and copies ran while one was open for 0% of the time, Pallas kernels for 7%

profile of v10, /device:TPU:0, one launch (start us, length us, event | category | flops | bytes accessed | tf_op | source)
XLA Modules:
  0.0 74.6 jit_solution(1554325696084075269)
XLA Ops:
  0.0 2.8 %shard_map.109 = (f32[5,16,96,128]{3,2,1,0:T(8,128)S(1)}, f32[40,4,128]{2,1,0:T(4,128)S(1)}, f32[40,4,128]{2,1,0:T(4,128)S(1)}) custom-call(f32[5,24,64,128]{3,2,1,0:T(8,128)} %fields_ref.1), custom_call_target="tpu_custom_call" | custom-call | tf_op jit(solution)/shard_map/pallas_call | solution.py:517
  2.8 4.0 %collective-permute-start = (f32[40,4,128]{2,1,0:T(4,128)S(1)}, f32[40,4,128]{2,1,0:T(4,128)S(1)}, u32[]{:S(2)}, u32[]{:S(2)}) collective-permute-start(f32[40,4,128]{2,1,0:T(4,128)S(1)} %get-tuple-element.12), channel_id=1, source_target_pairs={{0,1},{1,2},{2,3},{3,4},{4,5},{5,6},{6,7},{7,0},{8,9},{9,10},{10,1... | collective-permute-start | bytes 245768 | tf_op jit(solution)/shard_map/ppermute | solution.py:537
  6.8 2.3 %collective-permute-start.1 = (f32[40,4,128]{2,1,0:T(4,128)S(1)}, f32[40,4,128]{2,1,0:T(4,128)S(1)}, u32[]{:S(2)}, u32[]{:S(2)}) collective-permute-start(f32[40,4,128]{2,1,0:T(4,128)S(1)} %get-tuple-element.13), channel_id=1, source_target_pairs={{1,0},{2,1},{3,2},{4,3},{5,4},{6,5},{7,6},{0,7},{9,8},{10,9},{11,1... | collective-permute-start | bytes 245768 | tf_op jit(solution)/shard_map/ppermute | solution.py:538
  9.1 5.3 %shard_map.110 = (bf16[112,4,768]{2,1,0:T(4,128)(2,1)S(1)}, f32[2,24,768]{2,1,0:T(8,128)S(1)}, f32[20,24,128]{2,1,0:T(8,128)S(1)}, bf16[2560,768]{1,0:T(8,128)(2,1)S(1)}) custom-call(f32[5,16,96,128]{3,2,1,0:T(8,128)S(1)} %get-tuple-element.14.smooth_ref, bf16[2560,768]{1,0:T(8,128)(2,1)S(1)} %copy-done.7), custom_call_target="tpu_custom_call" | custom-call | flops 3607101440 | bytes 7864320 | tf_op jit(solution)/shard_map/pallas_call | solution.py:498
  14.4 0.0 copy-start
  14.4 0.0 copy-start.1
  14.4 0.0 copy-start.3
  14.4 0.0 copy-start.6
  14.4 0.0 collective-permute-done.upper_ref
  14.4 0.0 collective-permute-done.1.lower_ref
  14.5 0.0 slice-start
  14.5 1.6 %shard_map.111 = bf16[112,4,768]{2,1,0:T(4,128)(2,1)S(1)} custom-call(f32[40,4,128]{2,1,0:T(4,128)S(1)} %collective-permute-done.upper_ref, f32[40,4,128]{2,1,0:T(4,128)S(1)} %collective-permute-done.1.lower_ref, bf16[768,256]{1,0:T(8,128)(2,1)S(1)} %copy-done.2, f32[20,24,128]{2,1,0:T(8,128)S(1)} %get-tuple-element.15.edge_ref, ...), custom_call_target="tpu_custom_call" | custom-call | flops 251658240 | bytes 5570560 | tf_op jit(solution)/shard_map/pallas_call | solution.py:498
  16.0 0.0 slice-start.1
  16.1 0.0 copy-start.4
  16.1 17.9 %all_to_all.15 = bf16[16,7,4,768]{3,2,1,0:T(4,128)(2,1)S(1)} all-to-all(bf16[16,7,4,768]{3,2,1,0:T(4,128)(2,1)S(1)} %bitcast.9), channel_id=1, replica_groups=mesh['gx'=16,'gy'=8] {'gx'}, dimensions={0} | all-to-all | bytes 1376256 | tf_op jit(solution)/shard_map/all_to_all | solution.py:565
  34.0 0.0 copy-done.6
  34.0 2.6 %shard_map.112 = bf16[128,2,768]{2,1,0:T(2,128)(2,1)S(1)} custom-call(bf16[112,4,768]{2,1,0:T(4,128)(2,1)S(1)} %bitcast.10, bf16[256,448]{1,0:T(8,128)(2,1)S(1)} %copy-done.3, bf16[768,2304]{1,0:T(8,128)(2,1)S(1)} %copy-done, bf16[768,768]{1,0:T(8,128)(2,1)S(1)} %copy-done.1, bf16[256,256]{1,0:T(8,128)(2,1)S(1)} %copy-done.6), custom_call_target="tpu_custom_call" | custom-call | flops 1207959552 | bytes 5767168 | tf_op jit(solution)/shard_map/pallas_call | solution.py:498
  36.6 18.1 %all_to_all.16.tokens_ref = bf16[128,2,768]{2,1,0:T(2,128)(2,1)S(1)} all-to-all(bf16[128,2,768]{2,1,0:T(2,128)(2,1)S(1)} %shard_map.112), channel_id=1, replica_groups=mesh['gx'=16,'gy'=8] {'gx','gy'}, dimensions={0} | all-to-all | bytes 786432 | tf_op jit(solution)/shard_map/all_to_all | solution.py:576
  54.6 0.0 slice-done.2
  54.6 0.0 slice-done
  54.7 0.0 copy-start.5
  54.7 5.3 %shard_map.113 = bf16[256,768]{1,0:T(8,128)(2,1)S(1)} custom-call(bf16[128,2,768]{2,1,0:T(2,128)(2,1)S(1)} %all_to_all.16.tokens_ref, bf16[256,256]{1,0:T(8,128)(2,1)S(1)} %copy-done.4, bf16[768,2304]{1,0:T(8,128)(2,1)S(1)} %copy-done, bf16[768,768]{1,0:T(8,128)(2,1)S(1)} %copy-done.1, bf16[768,3072]{1,0:T(8,128)(2,1)S(1)} %bitcast.6, ...), custom_call_target="tpu_custom_call" | custom-call | flops 3623878656 | bytes 14680064 | tf_op jit(solution)/shard_map/pallas_call | solution.py:498
  60.0 13.6 %all_to_all.17 = bf16[8,32,768]{2,1,0:T(8,128)(2,1)S(1)} all-to-all(bf16[8,32,768]{2,1,0:T(8,128)(2,1)S(1)} %bitcast.12), channel_id=1, replica_groups=mesh['gx'=16,'gy'=8] {'gy'}, dimensions={0} | all-to-all | bytes 786432 | tf_op jit(solution)/shard_map/all_to_all | solution.py:586
  73.6 1.0 %shard_map.114 = bf16[256,768]{1,0:T(8,128)(2,1)} custom-call(bf16[256,768]{1,0:T(8,128)(2,1)S(1)} %bitcast.11, bf16[256,256]{1,0:T(8,128)(2,1)S(1)} %copy-done.5), custom_call_target="tpu_custom_call" | custom-call | flops 100663296 | bytes 524288 | tf_op jit(solution)/shard_map/pallas_call | solution.py:498
  (15 shorter events, 0.0 us)
Async XLA Ops:
  0.0 9.1 %copy-start.7 = (bf16[2560,768]{1,0:T(8,128)(2,1)S(1)}, bf16[2560,768]{1,0:T(8,128)(2,1)}, u32[]{:S(2)}) copy-start(bf16[2560,768]{1,0:T(8,128)(2,1)} %weight_ref.1) | copy-start | bytes 11796484
  0.0 54.6 %slice-start.2 = ((s8[4718592]{0:T(1024)(128)(4,1)}), s8[524288]{0:T(1024)(128)(4,1)S(1)}, s32[]{:S(2)}) async-start(s8[4718592]{0:T(1024)(128)(4,1)} %bitcast.7), calls=%async_computation.5 | async-start | bytes 1048576
  2.8 11.6 %collective-permute-start = (f32[40,4,128]{2,1,0:T(4,128)S(1)}, f32[40,4,128]{2,1,0:T(4,128)S(1)}, u32[]{:S(2)}, u32[]{:S(2)}) collective-permute-start(f32[40,4,128]{2,1,0:T(4,128)S(1)} %get-tuple-element.12), channel_id=1, source_target_pairs={{0,1},{1,2},{2,3},{3,4},{4,5},{5,6},{6,7},{7,0},{8,9},{9,10},{10,1... | collective-permute-start | bytes 245768 | tf_op jit(solution)/shard_map/ppermute | solution.py:537
  6.8 7.6 %collective-permute-start.1 = (f32[40,4,128]{2,1,0:T(4,128)S(1)}, f32[40,4,128]{2,1,0:T(4,128)S(1)}, u32[]{:S(2)}, u32[]{:S(2)}) collective-permute-start(f32[40,4,128]{2,1,0:T(4,128)S(1)} %get-tuple-element.13), channel_id=1, source_target_pairs={{1,0},{2,1},{3,2},{4,3},{5,4},{6,5},{7,6},{0,7},{9,8},{10,9},{11,1... | collective-permute-start | bytes 245768 | tf_op jit(solution)/shard_map/ppermute | solution.py:538
  9.1 5.4 %copy-start.2 = (bf16[768,256]{1,0:T(8,128)(2,1)S(1)}, bf16[768,256]{1,0:T(8,128)(2,1)}, u32[]{:S(2)}) copy-start(bf16[768,256]{1,0:T(8,128)(2,1)} %constant.10.clone.table_ref) | copy-start | bytes 1179652
  9.1 45.5 %slice-start.3 = ((s8[4718592]{0:T(1024)(128)(4,1)}), s8[4194304]{0:T(1024)(128)(4,1)S(1)}, s32[]{:S(2)}) async-start(s8[4718592]{0:T(1024)(128)(4,1)} %bitcast.7), calls=%async_computation.6 | async-start | bytes 8388608
  14.4 19.6 %copy-start = (bf16[768,2304]{1,0:T(8,128)(2,1)S(1)}, bf16[768,2304]{1,0:T(8,128)(2,1)}, u32[]{:S(2)}) copy-start(bf16[768,2304]{1,0:T(8,128)(2,1)} %qkv_ref.3) | copy-start | bytes 10616836
  14.4 19.6 %copy-start.1 = (bf16[768,768]{1,0:T(8,128)(2,1)S(1)}, bf16[768,768]{1,0:T(8,128)(2,1)}, u32[]{:S(2)}) copy-start(bf16[768,768]{1,0:T(8,128)(2,1)} %outw_ref.3) | copy-start | bytes 3538948
  14.4 19.6 %copy-start.3 = (bf16[256,448]{1,0:T(8,128)(2,1)S(1)}, bf16[256,448]{1,0:T(8,128)(2,1)}, u32[]{:S(2)}) copy-start(bf16[256,448]{1,0:T(8,128)(2,1)} %constant.11.clone.sum_ref) | copy-start | bytes 688132
  14.4 19.5 %copy-start.6 = (bf16[256,256]{1,0:T(8,128)(2,1)S(1)}, bf16[256,256]{1,0:T(8,128)(2,1)}, u32[]{:S(2)}) copy-start(bf16[256,256]{1,0:T(8,128)(2,1)} %constant.12.clone.order_ref) | copy-start | bytes 393220
  14.5 40.2 %slice-start = ((s8[4718592]{0:T(1024)(128)(4,1)}), s8[4194304]{0:T(1024)(128)(4,1)S(1)}, s32[]{:S(2)}) async-start(s8[4718592]{0:T(1024)(128)(4,1)} %bitcast.5), calls=%async_computation.3 | async-start | bytes 8388608
  16.0 38.6 %slice-start.1 = ((s8[4718592]{0:T(1024)(128)(4,1)}), s8[524288]{0:T(1024)(128)(4,1)S(1)}, s32[]{:S(2)}) async-start(s8[4718592]{0:T(1024)(128)(4,1)} %bitcast.5), calls=%async_computation.4 | async-start | bytes 1048576
  16.1 38.6 %copy-start.4 = (bf16[256,256]{1,0:T(8,128)(2,1)S(1)}, bf16[256,256]{1,0:T(8,128)(2,1)}, u32[]{:S(2)}) copy-start(bf16[256,256]{1,0:T(8,128)(2,1)} %constant.13.clone.split_ref) | copy-start | bytes 393220
  54.7 18.9 %copy-start.5 = (bf16[256,256]{1,0:T(8,128)(2,1)S(1)}, bf16[256,256]{1,0:T(8,128)(2,1)}, u32[]{:S(2)}) copy-start(bf16[256,256]{1,0:T(8,128)(2,1)} %constant.14.clone.order_ref) | copy-start | bytes 393220

commit v11 on v10

--- a/solution.py
+++ b/solution.py
@@ -349,7 +349,7 @@
     rolled = pltpu.roll(last, 64, 1)
     mixed[0:80] = jnp.where(first, last, pltpu.roll(rolled, 79, 0))
     mixed[80:160] = jnp.where(first, rolled, pltpu.roll(last, 79, 0))
-    lhs[...] = edge_ref[...]
+    lhs[:, 0:24] = edge_ref[...]
     for side in range(2):
         for a in range(2):
             rows = pl.ds(a, EXT, stride=2)
@@ -363,7 +363,7 @@
                 lhs[side * 10 + 8 + q, rows] += found
     for side in range(2):
         result = base_ref[side]
-        values = jnp.concatenate([lhs[side * 10 + n] for n in range(10)], 1)
+        values = jnp.concatenate([lhs[side * 10 + n, 0:24] for n in range(10)], 1)
         high, low = halves(values)
         values = jnp.concatenate([high.astype(f32), low.astype(f32)], 0).astype(bf16)
         for first_lane, start, count in (
@@ -544,7 +544,7 @@
             pltpu.VMEM((NF, ZS, 80, CY), f32),
             pltpu.VMEM((ALL_ROWS, KIN), bf16),
             pltpu.VMEM((ALL_ROWS, D), f32),
-            pltpu.VMEM((6, HI_ROWS, 128), f32),
+            pltpu.VMEM((6, HI_ROWS + 80, 128), f32),
             pltpu.VMEM((ALL_ROWS, D), bf16),
         ],
         2 * 6400 * 256 * 256 + 2 * KIN * 256 * D + 2 * ALL_ROWS * KIN * D,
@@ -555,8 +555,8 @@
         slots,
         [
             pltpu.VMEM((400, 128), f32),
-            pltpu.VMEM((160, 128), f32),
-            pltpu.VMEM((20, 24, 128), f32),
+            pltpu.VMEM((224, 128), f32),
+            pltpu.VMEM((20, 40, 128), f32),
             pltpu.SemaphoreType.DMA(()),
         ],
         2 * 64 * KIN * D,

time: 74.8 us -> 74.8 us (level)
  no operation moved by 1% of the time
where the time goes in v11:
time: 74.8 us; the launch traced here: 74.6 us
  blocking collectives  49.5 us (66%)
  Pallas kernels  18.5 us (25%)
  starting transfers between devices  6.31 us (8%)
    all_to_all x1, blocking collectives, shards(): lax.all_to_all(tokens, ('gx', 'gy'), split_axis=0, concat_axis=0, tiled=T...  18.1 us
    all_to_all x1, blocking collectives, shards(): lax.all_to_all(slots.reshape(NXL, SLOTS // 4, 4, D), 'gx', split_axis=0,...  17.9 us
    pallas_call x5, Pallas kernels, call(): pl.pallas_call(kernel, out_shape=out_shape, in_specs=[space] * len(operan...  15.7 us
    all_to_all x1, blocking collectives, shards(): lax.all_to_all(tokens.reshape(8, 32, D), 'gy', split_axis=0, concat_axis=...  13.6 us
    ppermute x1, starting transfers between devices, shards(): lax.ppermute(upper, 'gy', [(i, (i + 1) % count) for i in range(count)])  4.03 us
    pallas_call x1, Pallas kernels, prepare(): pl.pallas_call(prep_kernel, in_specs=[pl.BlockSpec(memory_space=pltpu.HBM...  2.76 us
    ppermute x1, starting transfers between devices, shards(): lax.ppermute(lower, 'gy', [((i + 1) % count, i) for i in range(count)])  2.28 us
  transfers between devices with their start and end apart: 2, of which 0 were waited for; matrix products, arithmetic and copies ran while one was open for 0% of the time, Pallas kernels for 7%

profile of v11, /device:TPU:0, one launch (start us, length us, event | category | flops | bytes accessed | tf_op | source)
XLA Modules:
  0.0 74.6 jit_solution(8450233202278739617)
XLA Ops:
  0.0 2.8 %shard_map.109 = (f32[5,16,96,128]{3,2,1,0:T(8,128)S(1)}, f32[40,4,128]{2,1,0:T(4,128)S(1)}, f32[40,4,128]{2,1,0:T(4,128)S(1)}) custom-call(f32[5,24,64,128]{3,2,1,0:T(8,128)} %fields_ref.1), custom_call_target="tpu_custom_call" | custom-call | tf_op jit(solution)/shard_map/pallas_call | solution.py:517
  2.8 4.0 %collective-permute-start = (f32[40,4,128]{2,1,0:T(4,128)S(1)}, f32[40,4,128]{2,1,0:T(4,128)S(1)}, u32[]{:S(2)}, u32[]{:S(2)}) collective-permute-start(f32[40,4,128]{2,1,0:T(4,128)S(1)} %get-tuple-element.12), channel_id=1, source_target_pairs={{0,1},{1,2},{2,3},{3,4},{4,5},{5,6},{6,7},{7,0},{8,9},{9,10},{10,1... | collective-permute-start | bytes 245768 | tf_op jit(solution)/shard_map/ppermute | solution.py:537
  6.8 2.3 %collective-permute-start.1 = (f32[40,4,128]{2,1,0:T(4,128)S(1)}, f32[40,4,128]{2,1,0:T(4,128)S(1)}, u32[]{:S(2)}, u32[]{:S(2)}) collective-permute-start(f32[40,4,128]{2,1,0:T(4,128)S(1)} %get-tuple-element.13), channel_id=1, source_target_pairs={{1,0},{2,1},{3,2},{4,3},{5,4},{6,5},{7,6},{0,7},{9,8},{10,9},{11,1... | collective-permute-start | bytes 245768 | tf_op jit(solution)/shard_map/ppermute | solution.py:538
  9.1 5.3 %shard_map.110 = (bf16[112,4,768]{2,1,0:T(4,128)(2,1)S(1)}, f32[2,24,768]{2,1,0:T(8,128)S(1)}, f32[20,24,128]{2,1,0:T(8,128)S(1)}, bf16[2560,768]{1,0:T(8,128)(2,1)S(1)}) custom-call(f32[5,16,96,128]{3,2,1,0:T(8,128)S(1)} %get-tuple-element.14.smooth_ref, bf16[2560,768]{1,0:T(8,128)(2,1)S(1)} %copy-done.7), custom_call_target="tpu_custom_call" | custom-call | flops 3607101440 | bytes 7864320 | tf_op jit(solution)/shard_map/pallas_call | solution.py:498
  14.4 0.0 copy-start
  14.4 0.0 copy-start.1
  14.4 0.0 copy-start.3
  14.4 0.0 copy-start.6
  14.4 0.0 collective-permute-done.upper_ref
  14.4 0.0 collective-permute-done.1.lower_ref
  14.4 0.0 slice-start
  14.5 1.6 %shard_map.111 = bf16[112,4,768]{2,1,0:T(4,128)(2,1)S(1)} custom-call(f32[40,4,128]{2,1,0:T(4,128)S(1)} %collective-permute-done.upper_ref, f32[40,4,128]{2,1,0:T(4,128)S(1)} %collective-permute-done.1.lower_ref, bf16[768,256]{1,0:T(8,128)(2,1)S(1)} %copy-done.2, f32[20,24,128]{2,1,0:T(8,128)S(1)} %get-tuple-element.15.edge_ref, ...), custom_call_target="tpu_custom_call" | custom-call | flops 251658240 | bytes 5570560 | tf_op jit(solution)/shard_map/pallas_call | solution.py:498
  16.0 0.0 slice-start.1
  16.1 0.0 copy-start.4
  16.1 17.9 %all_to_all.15 = bf16[16,7,4,768]{3,2,1,0:T(4,128)(2,1)S(1)} all-to-all(bf16[16,7,4,768]{3,2,1,0:T(4,128)(2,1)S(1)} %bitcast.9), channel_id=1, replica_groups=mesh['gx'=16,'gy'=8] {'gx'}, dimensions={0} | all-to-all | bytes 1376256 | tf_op jit(solution)/shard_map/all_to_all | solution.py:565
  33.9 0.0 copy-done.3
  34.0 0.0 copy-done.6
  34.0 2.6 %shard_map.112 = bf16[128,2,768]{2,1,0:T(2,128)(2,1)S(1)} custom-call(bf16[112,4,768]{2,1,0:T(4,128)(2,1)S(1)} %bitcast.10, bf16[256,448]{1,0:T(8,128)(2,1)S(1)} %copy-done.3, bf16[768,2304]{1,0:T(8,128)(2,1)S(1)} %copy-done, bf16[768,768]{1,0:T(8,128)(2,1)S(1)} %copy-done.1, bf16[256,256]{1,0:T(8,128)(2,1)S(1)} %copy-done.6), custom_call_target="tpu_custom_call" | custom-call | flops 1207959552 | bytes 5767168 | tf_op jit(solution)/shard_map/pallas_call | solution.py:498
  36.6 18.1 %all_to_all.16.tokens_ref = bf16[128,2,768]{2,1,0:T(2,128)(2,1)S(1)} all-to-all(bf16[128,2,768]{2,1,0:T(2,128)(2,1)S(1)} %shard_map.112), channel_id=1, replica_groups=mesh['gx'=16,'gy'=8] {'gx','gy'}, dimensions={0} | all-to-all | bytes 786432 | tf_op jit(solution)/shard_map/all_to_all | solution.py:576
  54.6 0.0 slice-done.3
  54.7 0.0 copy-start.5
  54.7 5.3 %shard_map.113 = bf16[256,768]{1,0:T(8,128)(2,1)S(1)} custom-call(bf16[128,2,768]{2,1,0:T(2,128)(2,1)S(1)} %all_to_all.16.tokens_ref, bf16[256,256]{1,0:T(8,128)(2,1)S(1)} %copy-done.4, bf16[768,2304]{1,0:T(8,128)(2,1)S(1)} %copy-done, bf16[768,768]{1,0:T(8,128)(2,1)S(1)} %copy-done.1, bf16[768,3072]{1,0:T(8,128)(2,1)S(1)} %bitcast.6, ...), custom_call_target="tpu_custom_call" | custom-call | flops 3623878656 | bytes 14680064 | tf_op jit(solution)/shard_map/pallas_call | solution.py:498
  60.0 13.6 %all_to_all.17 = bf16[8,32,768]{2,1,0:T(8,128)(2,1)S(1)} all-to-all(bf16[8,32,768]{2,1,0:T(8,128)(2,1)S(1)} %bitcast.12), channel_id=1, replica_groups=mesh['gx'=16,'gy'=8] {'gy'}, dimensions={0} | all-to-all | bytes 786432 | tf_op jit(solution)/shard_map/all_to_all | solution.py:586
  73.6 1.0 %shard_map.114 = bf16[256,768]{1,0:T(8,128)(2,1)} custom-call(bf16[256,768]{1,0:T(8,128)(2,1)S(1)} %bitcast.11, bf16[256,256]{1,0:T(8,128)(2,1)S(1)} %copy-done.5), custom_call_target="tpu_custom_call" | custom-call | flops 100663296 | bytes 524288 | tf_op jit(solution)/shard_map/pallas_call | solution.py:498
  (15 shorter events, 0.0 us)
Async XLA Ops:
  0.0 9.1 %copy-start.7 = (bf16[2560,768]{1,0:T(8,128)(2,1)S(1)}, bf16[2560,768]{1,0:T(8,128)(2,1)}, u32[]{:S(2)}) copy-start(bf16[2560,768]{1,0:T(8,128)(2,1)} %weight_ref.1) | copy-start | bytes 11796484
  0.0 54.6 %slice-start.2 = ((s8[4718592]{0:T(1024)(128)(4,1)}), s8[524288]{0:T(1024)(128)(4,1)S(1)}, s32[]{:S(2)}) async-start(s8[4718592]{0:T(1024)(128)(4,1)} %bitcast.7), calls=%async_computation.5 | async-start | bytes 1048576
  2.8 11.6 %collective-permute-start = (f32[40,4,128]{2,1,0:T(4,128)S(1)}, f32[40,4,128]{2,1,0:T(4,128)S(1)}, u32[]{:S(2)}, u32[]{:S(2)}) collective-permute-start(f32[40,4,128]{2,1,0:T(4,128)S(1)} %get-tuple-element.12), channel_id=1, source_target_pairs={{0,1},{1,2},{2,3},{3,4},{4,5},{5,6},{6,7},{7,0},{8,9},{9,10},{10,1... | collective-permute-start | bytes 245768 | tf_op jit(solution)/shard_map/ppermute | solution.py:537
  6.8 7.6 %collective-permute-start.1 = (f32[40,4,128]{2,1,0:T(4,128)S(1)}, f32[40,4,128]{2,1,0:T(4,128)S(1)}, u32[]{:S(2)}, u32[]{:S(2)}) collective-permute-start(f32[40,4,128]{2,1,0:T(4,128)S(1)} %get-tuple-element.13), channel_id=1, source_target_pairs={{1,0},{2,1},{3,2},{4,3},{5,4},{6,5},{7,6},{0,7},{9,8},{10,9},{11,1... | collective-permute-start | bytes 245768 | tf_op jit(solution)/shard_map/ppermute | solution.py:538
  9.1 5.4 %copy-start.2 = (bf16[768,256]{1,0:T(8,128)(2,1)S(1)}, bf16[768,256]{1,0:T(8,128)(2,1)}, u32[]{:S(2)}) copy-start(bf16[768,256]{1,0:T(8,128)(2,1)} %constant.10.clone.table_ref) | copy-start | bytes 1179652
  9.1 45.5 %slice-start.3 = ((s8[4718592]{0:T(1024)(128)(4,1)}), s8[4194304]{0:T(1024)(128)(4,1)S(1)}, s32[]{:S(2)}) async-start(s8[4718592]{0:T(1024)(128)(4,1)} %bitcast.7), calls=%async_computation.6 | async-start | bytes 8388608
  14.4 19.6 %copy-start = (bf16[768,2304]{1,0:T(8,128)(2,1)S(1)}, bf16[768,2304]{1,0:T(8,128)(2,1)}, u32[]{:S(2)}) copy-start(bf16[768,2304]{1,0:T(8,128)(2,1)} %qkv_ref.3) | copy-start | bytes 10616836
  14.4 19.6 %copy-start.1 = (bf16[768,768]{1,0:T(8,128)(2,1)S(1)}, bf16[768,768]{1,0:T(8,128)(2,1)}, u32[]{:S(2)}) copy-start(bf16[768,768]{1,0:T(8,128)(2,1)} %outw_ref.3) | copy-start | bytes 3538948
  14.4 19.6 %copy-start.3 = (bf16[256,448]{1,0:T(8,128)(2,1)S(1)}, bf16[256,448]{1,0:T(8,128)(2,1)}, u32[]{:S(2)}) copy-start(bf16[256,448]{1,0:T(8,128)(2,1)} %constant.11.clone.sum_ref) | copy-start | bytes 688132
  14.4 19.5 %copy-start.6 = (bf16[256,256]{1,0:T(8,128)(2,1)S(1)}, bf16[256,256]{1,0:T(8,128)(2,1)}, u32[]{:S(2)}) copy-start(bf16[256,256]{1,0:T(8,128)(2,1)} %constant.12.clone.order_ref) | copy-start | bytes 393220
  14.4 40.2 %slice-start = ((s8[4718592]{0:T(1024)(128)(4,1)}), s8[4194304]{0:T(1024)(128)(4,1)S(1)}, s32[]{:S(2)}) async-start(s8[4718592]{0:T(1024)(128)(4,1)} %bitcast.5), calls=%async_computation.3 | async-start | bytes 8388608
  16.0 38.6 %slice-start.1 = ((s8[4718592]{0:T(1024)(128)(4,1)}), s8[524288]{0:T(1024)(128)(4,1)S(1)}, s32[]{:S(2)}) async-start(s8[4718592]{0:T(1024)(128)(4,1)} %bitcast.5), calls=%async_computation.4 | async-start | bytes 1048576
  16.1 38.6 %copy-start.4 = (bf16[256,256]{1,0:T(8,128)(2,1)S(1)}, bf16[256,256]{1,0:T(8,128)(2,1)}, u32[]{:S(2)}) copy-start(bf16[256,256]{1,0:T(8,128)(2,1)} %constant.13.clone.split_ref) | copy-start | bytes 393220
  54.7 18.9 %copy-start.5 = (bf16[256,256]{1,0:T(8,128)(2,1)S(1)}, bf16[256,256]{1,0:T(8,128)(2,1)}, u32[]{:S(2)}) copy-start(bf16[256,256]{1,0:T(8,128)(2,1)} %constant.14.clone.order_ref) | copy-start | bytes 393220
